TPU v7x, 32 devices: a whole 2x2x4 slice. The times are simulated.
32 devices in a mesh: dp: 8 (over z, y), seq: 2 (over x), tensor: 2 (over core).
Axes of the slice: x: 2, y: 2, z: 4, core: 2. Of those that a mesh axis runs over, the one named last changes fastest.
Arguments:
- latents: bfloat16 [2, 8, 32, 32, 2240], P(None, 'dp', 'seq'), may hold values from -6 to 6
- text: bfloat16 [2, 8, 300, 2240], P(None, 'dp'), may hold values from -6 to 6
- timesteps: int32 [2, 8], P(None, 'dp'), may hold values from 0 to 999
- text_lengths: int32 [2, 8], P(None, 'dp'), may hold values from 1 to 300, as said below
- cotangent: bfloat16 [2, 8, 32, 32, 2240], P(None, 'dp', 'seq'), may hold values from -6 to 6
- table: float32 [6, 2240], replicated
- self_qkv: bfloat16 [3, 2240, 2240], P(None, ('dp', 'seq'), 'tensor')
- self_out: bfloat16 [2240, 2240], P('tensor', ('dp', 'seq')), may hold values from -0.75 to 0.75
- cross_q: bfloat16 [2240, 2240], P(('dp', 'seq'), 'tensor')
- cross_kv: bfloat16 [2, 2240, 2240], P(None, ('dp', 'seq'), 'tensor'), may hold values from -0.125 to 0.125
- cross_out: bfloat16 [2240, 2240], P('tensor', ('dp', 'seq')), may hold values from -0.5 to 0.5
- up_w: bfloat16 [2, 2240, 5600], P(None, ('dp', 'seq'), 'tensor')
- up_b: float32 [2, 5600], P(None, 'tensor'), may hold values from -3 to 3
- conv_w: float32 [9, 2, 5600], P(None, None, 'tensor'), may hold values from -2 to 2
- conv_b: float32 [2, 5600], P(None, 'tensor'), may hold values from -3 to 3
- down_w: bfloat16 [5600, 2240], P('tensor', ('dp', 'seq')), may hold values from -0.21875 to 0.21875
Outputs:
- output: bfloat16 [2, 8, 32, 32, 2240], P(None, 'dp', 'seq')
- latents_grad: float32 [2, 8, 32, 32, 2240], P(None, 'dp', 'seq')
- table_grad: float32 [6, 2240], replicated
- self_qkv_grad: float32 [3, 2240, 2240], P(None, ('dp', 'seq'), 'tensor')
- self_out_grad: float32 [2240, 2240], P('tensor', ('dp', 'seq'))
- cross_q_grad: float32 [2240, 2240], P(('dp', 'seq'), 'tensor')
- cross_kv_grad: float32 [2, 2240, 2240], P(None, ('dp', 'seq'), 'tensor')
- cross_out_grad: float32 [2240, 2240], P('tensor', ('dp', 'seq'))
- up_w_grad: float32 [2, 2240, 5600], P(None, ('dp', 'seq'), 'tensor')
- up_b_grad: float32 [2, 5600], P(None, 'tensor')
- conv_w_grad: float32 [9, 2, 5600], P(None, None, 'tensor')
- conv_b_grad: float32 [2, 5600], P(None, 'tensor')
- down_w_grad: float32 [5600, 2240], P('tensor', ('dp', 'seq'))
- cross_q_clipped: float32 [2240, 2240], P(('dp', 'seq'), 'tensor')
- cross_k_clipped: float32 [2240, 2240], P(('dp', 'seq'), 'tensor')
Inputs may be any that keep to these rules, and one draw needn't show every extreme that they name: `text_lengths`: for each latent position, at least one of the 2 micro-batches has length 300.
All inputs are finite; a program needn't handle non-finite values.
Results may differ from a plain program's by a relative error of at most 0.03.
Values may be sent and summed in bfloat16 or wider, within the bound.
A program may use at most 536 MiB of HBM per device.

v0:
```python
import functools
import math

import jax
import jax.numpy as jnp
from jax import lax
from jax.experimental import pallas as pl
from jax.experimental.pallas import tpu as pltpu
from jax.sharding import PartitionSpec as P

DP, SEQ, TP = "dp", "seq", "tensor"
HEAD_DIM = 32
LANES = 128
NORM_EPS = 1e-06
ATTN_EPS = 1e-06
CLIP_TAU = 3.5
MASKED_FILL = -1e30
F32, BF16 = jnp.float32, jnp.bfloat16
VMEM_LIMIT = 48 * 1024 * 1024


def up_to(value, step):
    return -(-value // step) * step


def dot(left, right, left_dim, right_dim):
    return lax.dot_general(
        left, right, (((left_dim,), (right_dim,)), ((), ())), preferred_element_type=F32
    )


def split(values):
    high = values.astype(BF16)
    return high, (values - high.astype(F32)).astype(BF16)


def ring_of(axis):
    size = lax.axis_size(axis)
    if axis == DP and size % 2 == 0:
        return list(range(0, size, 2)) + list(range(size - 1, 0, -2))
    return list(range(size))


def ring_place(axis):
    size, index = lax.axis_size(axis), lax.axis_index(axis)
    if axis == DP and size % 2 == 0:
        return jnp.where(index % 2 == 0, index // 2, size - 1 - index // 2)
    return index


def ring_member(axis, place):
    size = lax.axis_size(axis)
    if axis == DP and size % 2 == 0:
        return jnp.where(place < size // 2, 2 * place, 2 * (size - 1 - place) + 1)
    return place


def shift(values, axis, step):
    cycle = ring_of(axis)
    size = len(cycle)
    return lax.ppermute(values, axis, [(cycle[i], cycle[(i + step) % size]) for i in range(size)])


def ring_gather(own, axis, flip):
    size = lax.axis_size(axis)
    pieces = [own] + [None] * (size - 1)
    ahead = size // 2 if not flip else size - 1 - size // 2
    for a in range(1, ahead + 1):
        pieces[a] = shift(pieces[a - 1], axis, 1)
    for a in range(size - 1, ahead, -1):
        pieces[a] = shift(pieces[(a + 1) % size], axis, -1)
    return pieces


def ring_scatter(blocks, axis, flip):
    size = lax.axis_size(axis)
    ahead = size // 2 if not flip else size - 1 - size // 2
    total = blocks[0]().astype(F32)
    if ahead > 0:
        running = blocks[ahead]().astype(BF16)
        for a in range(ahead - 1, 0, -1):
            running = (shift(running, axis, -1).astype(F32) + blocks[a]()).astype(BF16)
        total = total + shift(running, axis, -1).astype(F32)
    if ahead < size - 1:
        running = blocks[ahead + 1]().astype(BF16)
        for a in range(ahead + 2, size):
            running = (shift(running, axis, 1).astype(F32) + blocks[a]()).astype(BF16)
        total = total + shift(running, axis, 1).astype(F32)
    return total


def gather_rows(shard, long_first, flip):
    if long_first:
        near = jnp.concatenate(ring_gather(shard, DP, flip), axis=0)
        return jnp.concatenate(ring_gather(near, SEQ, False), axis=0)
    pair = jnp.stack(ring_gather(shard, SEQ, False))
    pieces = ring_gather(pair, DP, flip)
    return jnp.concatenate([piece[b] for b in range(pair.shape[0]) for piece in pieces], axis=0)


def scatter_rows(parts, long_first, flip):
    dp_size = lax.axis_size(DP)
    parts = [part.reshape(dp_size, part.shape[0] // dp_size, part.shape[1]) for part in parts]
    if long_first:
        near = ring_scatter([lambda b=b: parts[b].astype(F32) for b in range(len(parts))], SEQ, False)
        return ring_scatter([lambda a=a: near[a] for a in range(dp_size)], DP, flip)
    far = [
        ring_scatter([lambda a=a, part=part: part[a].astype(F32) for a in range(dp_size)], DP, flip)
        for part in parts
    ]
    return ring_scatter([lambda b=b: far[b] for b in range(len(far))], SEQ, False)


def butterfly(values, axes, combine):
    for axis in axes:
        size = lax.axis_size(axis)
        bit = 1
        while bit < size:
            values = combine(values, lax.ppermute(values, axis, [(i, i ^ bit) for i in range(size)]))
            bit *= 2
    return values


def other_core(values):
    return lax.ppermute(values, TP, [(0, 1), (1, 0)])


def head_block():
    row = lax.broadcasted_iota(jnp.int32, (LANES, LANES), 0) // HEAD_DIM
    col = lax.broadcasted_iota(jnp.int32, (LANES, LANES), 1) // HEAD_DIM
    return row == col


def fold(state, total):
    state = jnp.where(head_block(), state, 0.0)
    rows = sum(state[i * HEAD_DIM : (i + 1) * HEAD_DIM] for i in range(LANES // HEAD_DIM))
    return jnp.concatenate([rows, total, jnp.zeros((7, LANES), F32)], axis=0)


def unfold(folded):
    state = jnp.concatenate([folded[:HEAD_DIM]] * (LANES // HEAD_DIM), axis=0)
    return jnp.where(head_block(), state, 0.0), folded[HEAD_DIM : HEAD_DIM + 1]


def softplus(values):
    return jnp.maximum(values, 0.0) + jnp.log1p(jnp.exp(-jnp.abs(values)))


def head_sum(values):
    ones = jnp.where(head_block(), 1.0, 0.0).astype(BF16)
    high, low = split(values)
    return dot(high, ones, 1, 0) + dot(low, ones, 1, 0)


def state_kernel(key_ref, value_ref, state_ref):
    key = softplus(key_ref[...]).astype(BF16)
    value = value_ref[...].astype(BF16)
    total = jnp.sum(key.astype(F32), axis=0, keepdims=True)
    state_ref[0, 0] = fold(dot(key, value, 0, 0), total)


def ratio_parts(query_ref, state_ref):
    query = softplus(query_ref[...]).astype(BF16)
    state, total = unfold(state_ref[0, 0])
    high, low = split(state)
    numerator = dot(query, high, 1, 0) + dot(query, low, 1, 0)
    denominator = head_sum(query.astype(F32) * total) + ATTN_EPS
    return query, high, low, total, numerator, denominator


def mix_kernel(query_ref, state_ref, mixed_ref):
    query, high, low, total, numerator, denominator = ratio_parts(query_ref, state_ref)
    mixed_ref[...] = (numerator / denominator).astype(BF16)


def mix_back_kernel(query_ref, state_ref, grad_ref, query_grad_ref, state_grad_ref):
    query, high, low, total, numerator, denominator = ratio_parts(query_ref, state_ref)
    mixed_grad = grad_ref[...]
    numer_grad = mixed_grad / denominator
    denom_grad = -head_sum(mixed_grad * numerator) / (denominator * denominator)
    up, down = split(numer_grad)
    state_grad = dot(query, up, 0, 0) + dot(query, down, 0, 0)
    total_grad = jnp.sum(query.astype(F32) * denom_grad, axis=0, keepdims=True)
    state_grad_ref[0, 0] = fold(state_grad, total_grad)
    side = dot(up, high, 1, 1) + dot(up, low, 1, 1) + dot(down, high, 1, 1) + denom_grad * total
    query_grad_ref[...] = (side * jax.nn.sigmoid(query_ref[...])).astype(BF16)


def state_back_kernel(key_ref, value_ref, state_ref, out_ref):
    state, total = unfold(state_ref[0, 0])
    high, low = split(state)

    @pl.when(pl.program_id(0) == 0)
    def _():
        value = value_ref[...].astype(BF16)
        side = dot(value, high, 1, 1) + dot(value, low, 1, 1) + total
        out_ref[...] = (side * jax.nn.sigmoid(key_ref[...])).astype(BF16)

    @pl.when(pl.program_id(0) == 1)
    def _():
        key = softplus(key_ref[...]).astype(BF16)
        out_ref[...] = (dot(key, high, 1, 0) + dot(key, low, 1, 0)).astype(BF16)


def head_of(values, head):
    lane = lax.broadcasted_iota(jnp.int32, values.shape, 1) // HEAD_DIM
    return jnp.where(lane == head, values, jnp.zeros_like(values))


def weigh(key_head, query, visible):
    scores = dot(key_head, query, 1, 1) * HEAD_DIM ** (-0.5)
    masked = jnp.where(visible, scores, MASKED_FILL)
    top = jnp.max(masked, axis=0, keepdims=True)
    exponent = jnp.exp(masked - top)
    return exponent * (1.0 / jnp.sum(exponent, axis=0, keepdims=True)), top


def cross_kernel(length_ref, query_ref, key_ref, value_ref, out_ref, peak_ref):
    query, key, value = query_ref[...], key_ref[...], value_ref[...]
    tokens, slots = query.shape[0], key.shape[0]
    visible = lax.broadcasted_iota(jnp.int32, (slots, tokens), 0) < length_ref[pl.program_id(0)]
    total = jnp.zeros((LANES, tokens), F32)
    peak_ref[0, 0] = jnp.zeros((8, LANES), F32)
    for head in range(LANES // HEAD_DIM):
        probability, top = weigh(head_of(key, head), query, visible)
        total = total + dot(head_of(value, head), probability.astype(BF16), 0, 0)
        peak_ref[0, 0, head : head + 1] = jnp.broadcast_to(jnp.max(top, axis=1, keepdims=True), (1, LANES))
    out_ref[...] = total.T.astype(BF16)


def cross_back_kernel(length_ref, query_ref, key_ref, value_ref, grad_ref, query_grad_ref, key_grad_ref, value_grad_ref):
    query, key, value, grad = query_ref[...], key_ref[...], value_ref[...], grad_ref[...]
    tokens, slots = query.shape[0], key.shape[0]
    visible = lax.broadcasted_iota(jnp.int32, (slots, tokens), 0) < length_ref[pl.program_id(0)]
    query_grad = jnp.zeros((LANES, tokens), F32)
    key_grad = jnp.zeros((slots, LANES), F32)
    value_grad = jnp.zeros((slots, LANES), F32)
    for head in range(LANES // HEAD_DIM):
        key_head = head_of(key, head)
        probability, top = weigh(key_head, query, visible)
        prob_grad = dot(head_of(value, head), grad, 1, 1)
        value_grad = value_grad + head_of(dot(probability.astype(BF16), grad, 1, 0), head)
        mean = jnp.sum(probability * prob_grad, axis=0, keepdims=True)
        score_grad = (probability * (prob_grad - mean)).astype(BF16)
        key_grad = key_grad + head_of(dot(score_grad, query, 1, 0), head)
        query_grad = query_grad + dot(key_head, score_grad, 0, 0)
    scale = HEAD_DIM ** (-0.5)
    query_grad_ref[...] = (query_grad * scale).T.astype(BF16)
    key_grad_ref[...] = (key_grad * scale).astype(BF16)
    value_grad_ref[...] = value_grad.astype(BF16)


def silu(values):
    return values * jax.nn.sigmoid(values)


def silu_slope(values):
    sigma = jax.nn.sigmoid(values)
    return sigma * (1.0 + values * (1.0 - sigma))


def columns_of(values, cols):
    place = lax.broadcasted_iota(jnp.int32, values.shape, 0) % cols
    count = values.shape[0]
    left = jnp.where(place == 0, 0.0, pltpu.roll(values, 1, 0))
    right = jnp.where(place == cols - 1, 0.0, pltpu.roll(values, count - 1, 0))
    return left, values, right


def strips_of(tokens, cols):
    size = 4 * cols if tokens % (4 * cols) == 0 else cols
    return [(at, size) for at in range(0, tokens, size)]


def stage_columns(scratch, top, middle, bottom, cols):
    tokens = middle.shape[0]
    full = jnp.concatenate([top.astype(F32), middle, bottom.astype(F32)], axis=0)
    for place, part in enumerate(columns_of(full, cols)):
        scratch[place] = part


def taps(scratch, weight, at, size, cols, mirror):
    result = None
    for row_tap in range(3):
        for col_tap in range(3):
            row_at = 2 - row_tap if mirror else row_tap
            col_at = 2 - col_tap if mirror else col_tap
            tap = 3 * row_tap + col_tap
            term = scratch[col_at, at + row_at * cols : at + row_at * cols + size] * weight[tap : tap + 1]
            result = term if result is None else result + term
    return result


def conv_kernel(cols, z0, z1, top0, top1, bottom0, bottom1, w_ref, b_ref, out_ref, s0, s1):
    tokens = z0.shape[0]
    for z, top, bottom, scratch in ((z0, top0, bottom0, s0), (z1, top1, bottom1, s1)):
        stage_columns(scratch, top[0], silu(z[...]).astype(BF16).astype(F32), bottom[0], cols)
    for at, size in strips_of(tokens, cols):
        first = taps(s0, w_ref[0], at, size, cols, False) + b_ref[0, 0:1]
        second = taps(s1, w_ref[1], at, size, cols, False) + b_ref[1, 0:1]
        out_ref[at : at + size] = (first * silu(second)).astype(BF16)


def conv_back_kernel(cols, z0, z1, top0, top1, bottom0, bottom1, grad_ref, w_ref, b_ref, out0, out1, small_ref, s0, s1):
    tokens = z0.shape[0]
    for z, top, bottom, scratch in ((z0, top0, bottom0, s0), (z1, top1, bottom1, s1)):
        stage_columns(scratch, top[0], silu(z[...]).astype(BF16).astype(F32), bottom[0], cols)
    sums = [jnp.zeros((8, LANES), F32) for _ in range(20)]
    for at, size in strips_of(tokens, cols):
        first = taps(s0, w_ref[0], at, size, cols, False) + b_ref[0, 0:1]
        second = taps(s1, w_ref[1], at, size, cols, False) + b_ref[1, 0:1]
        grad = grad_ref[at : at + size]
        sigma = jax.nn.sigmoid(second)
        slope = sigma * (1.0 + second * (1.0 - sigma))
        for j, (part, scratch, out) in enumerate(
            ((grad * second * sigma, s0, out0), (grad * first * slope, s1, out1))
        ):
            out[at : at + size] = part.astype(BF16)
            for row_tap in range(3):
                for col_tap in range(3):
                    start = at + row_tap * cols
                    product = part * scratch[col_tap, start : start + size]
                    place = 9 * j + 3 * row_tap + col_tap
                    sums[place] = sums[place] + jnp.sum(product.reshape(size // 8, 8, LANES), axis=0)
            sums[18 + j] = sums[18 + j] + jnp.sum(part.reshape(size // 8, 8, LANES), axis=0)
    for place in range(20):
        small_ref[0, place : place + 1] = jnp.sum(sums[place], axis=0, keepdims=True)
    small_ref[0, 20:24] = jnp.zeros((4, LANES), F32)


def act_back_kernel(cols, z_ref, grad_ref, top, bottom, w_ref, out_ref, bias_ref, scratch):
    tokens = z_ref.shape[0]
    stage_columns(scratch, top[0], grad_ref[...].astype(F32), bottom[0], cols)
    total = jnp.zeros((8, LANES), F32)
    for at, size in strips_of(tokens, cols):
        part = taps(scratch, w_ref[0], at, size, cols, True) * silu_slope(z_ref[at : at + size])
        out_ref[at : at + size] = part.astype(BF16)
        total = total + jnp.sum(part.reshape(size // 8, 8, LANES), axis=0)
    bias_ref[0] = jnp.broadcast_to(jnp.sum(total, axis=0, keepdims=True), (8, LANES))


def call(kernel, grid, in_specs, out_specs, out_shape, flops, moved, scratch=(), **extra):
    return pl.pallas_call(
        kernel,
        grid=grid,
        in_specs=in_specs,
        out_specs=out_specs,
        out_shape=out_shape,
        scratch_shapes=list(scratch),
        compiler_params=pltpu.CompilerParams(vmem_limit_bytes=VMEM_LIMIT),
        cost_estimate=pl.CostEstimate(flops=int(flops), bytes_accessed=int(moved), transcendentals=0),
        **extra,
    )


def struct(shape, dtype):
    return jax.ShapeDtypeStruct(shape, dtype)


class Kernels:
    def __init__(self, micro, tokens, cols, width, hidden, slots):
        self.micro, self.tokens, self.cols = micro, tokens, cols
        self.width, self.hidden, self.slots = width, hidden, slots
        self.groups, self.units = width // LANES, hidden // LANES

    def tile(self, offset=0):
        return pl.BlockSpec((self.tokens, LANES), lambda m, g: (m, g + offset))

    def folded(self):
        return pl.BlockSpec((1, 1, HEAD_DIM + 8, LANES), lambda m, g: (m, g, 0, 0))

    def folded_shape(self):
        return struct((self.micro, self.groups, HEAD_DIM + 8, LANES), F32)

    def states(self, keys_values):
        size = self.micro * self.tokens * self.width
        return call(
            state_kernel, (self.micro, self.groups), [self.tile(), self.tile(self.groups)],
            self.folded(), self.folded_shape(), size * 600, size * 8,
        )(keys_values, keys_values)

    def mix(self, queries, states):
        size = self.micro * self.tokens * self.width
        return call(
            mix_kernel, (self.micro, self.groups), [self.tile(), self.folded()],
            self.tile(), struct(queries.shape, BF16), size * 1500, size * 6,
        )(queries, states)

    def mix_back(self, queries, states, mixed_grad):
        size = self.micro * self.tokens * self.width
        return call(
            mix_back_kernel, (self.micro, self.groups), [self.tile(), self.folded(), self.tile()],
            [self.tile(), self.folded()], [struct(queries.shape, BF16), self.folded_shape()],
            size * 4000, size * 10,
        )(queries, states, mixed_grad)

    def states_back(self, keys_values, state_grad):
        groups = self.groups
        size = self.micro * self.tokens * self.width
        tile = lambda offset: pl.BlockSpec((self.tokens, LANES), lambda j, m, g: (m, g + offset))
        return call(
            state_back_kernel, (2, self.micro, groups),
            [tile(0), tile(groups), pl.BlockSpec((1, 1, HEAD_DIM + 8, LANES), lambda j, m, g: (m, g, 0, 0))],
            pl.BlockSpec((self.tokens, LANES), lambda j, m, g: (m, g + j * groups)),
            struct(keys_values.shape, BF16), size * 1500, size * 20,
        )(keys_values, keys_values, state_grad)

    def text_tile(self, offset):
        return pl.BlockSpec((self.slots, LANES), lambda m, g: (m, g + offset))

    def cross(self, lengths, queries, text):
        size = self.micro * self.tokens * self.width
        smem = pl.BlockSpec(memory_space=pltpu.SMEM)
        peak = pl.BlockSpec((1, 1, 8, LANES), lambda m, g: (m, g, 0, 0))
        return call(
            cross_kernel, (self.micro, self.groups),
            [smem, self.tile(), self.text_tile(0), self.text_tile(self.groups)],
            [self.tile(), peak],
            [struct(queries.shape, BF16), struct((self.micro, self.groups, 8, LANES), F32)],
            size * 20000, size * 6,
        )(lengths, queries, text, text)

    def cross_back(self, lengths, queries, text, attended_grad):
        size = self.micro * self.tokens * self.width
        smem = pl.BlockSpec(memory_space=pltpu.SMEM)
        return call(
            cross_back_kernel, (self.micro, self.groups),
            [smem, self.tile(), self.text_tile(0), self.text_tile(self.groups), self.tile()],
            [self.tile(), self.text_tile(0), self.text_tile(0)],
            [struct(queries.shape, BF16), struct((text.shape[0], self.width), BF16), struct((text.shape[0], self.width), BF16)],
            size * 50000, size * 6,
        )(lengths, queries, text, text, attended_grad)

    def edge(self, offset=0):
        return pl.BlockSpec((1, self.cols, LANES), lambda m, g: (m, 0, g + offset))

    def scratch(self):
        return pltpu.VMEM((3, self.tokens + 2 * self.cols, LANES), F32)

    def conv_specs(self):
        units = self.units
        return (
            [self.tile(), self.tile(units), self.edge(), self.edge(units), self.edge(), self.edge(units)],
            [
                pl.BlockSpec((2, 9, LANES), lambda m, g: (0, 0, g)),
                pl.BlockSpec((2, 1, LANES), lambda m, g: (0, 0, g)),
            ],
        )

    def conv(self, pre, top, bottom, conv_w, conv_b):
        size = self.micro * self.tokens * self.hidden
        data, weights = self.conv_specs()
        return call(
            functools.partial(conv_kernel, self.cols), (self.micro, self.units), data + weights,
            self.tile(), struct((pre.shape[0], self.hidden), BF16), size * 20000, size * 10,
            [self.scratch(), self.scratch()],
        )(pre, pre, top, top, bottom, bottom, conv_w, conv_b)

    def conv_back(self, pre, top, bottom, grad, conv_w, conv_b):
        size = self.micro * self.tokens * self.hidden
        data, weights = self.conv_specs()
        one = struct((pre.shape[0], self.hidden), BF16)
        return call(
            functools.partial(conv_back_kernel, self.cols), (self.micro, self.units),
            data + [self.tile()] + weights,
            [self.tile(), self.tile(), pl.BlockSpec((1, 24, LANES), lambda m, g: (m, 0, g))],
            [one, one, struct((self.micro, 24, self.hidden), F32)], size * 40000, size * 16,
            [self.scratch(), self.scratch()],
        )(pre, pre, top, top, bottom, bottom, grad, conv_w, conv_b)

    def act_back(self, pre, grad, top, bottom, conv_w):
        size = self.micro * self.tokens * self.hidden
        units = self.units
        return call(
            functools.partial(act_back_kernel, self.cols), (self.micro, 2 * units),
            [
                self.tile(), self.tile(), self.edge(), self.edge(),
                pl.BlockSpec((1, 9, LANES), lambda m, g: (g // units, 0, g % units)),
            ],
            [self.tile(), pl.BlockSpec((1, 8, LANES), lambda m, g: (m, 0, g))],
            [struct(pre.shape, BF16), struct((self.micro, 8, pre.shape[1]), F32)], size * 20000, size * 16,
            [self.scratch()],
        )(pre, grad, top, bottom, conv_w)


def pad_to(values, *sizes):
    return jnp.pad(values, [(0, size - now) for size, now in zip(sizes, values.shape)])


def side_by_side(parts, width):
    return jnp.concatenate([pad_to(part, part.shape[0], width) for part in parts], axis=1)


def halos(rows, cols):
    size = lax.axis_size(SEQ)
    up = [(i, i + 1) for i in range(size - 1)]
    down = [(j, i) for i, j in up]
    return (
        lax.ppermute(rows[:, -cols:], SEQ, up),
        lax.ppermute(rows[:, :cols], SEQ, down),
    )


def shards(latents, text, timesteps, text_lengths, cotangent, table, self_qkv, self_out, cross_q, cross_kv,
           cross_out, up_w, up_b, conv_w, conv_b, down_w):
    micro, _, row_count, cols, features = latents.shape
    tokens = row_count * cols
    own_rows, heads_width = cross_q.shape
    hidden_width = up_b.shape[1]
    text_len = text.shape[2]
    width, hidden, slots = up_to(heads_width, LANES), up_to(hidden_width, LANES), up_to(text_len, 16)
    rows = up_to(own_rows, 16)
    dp_size, seq_size = lax.axis_size(DP), lax.axis_size(SEQ)
    near = dp_size * rows
    wide = seq_size * near
    core = lax.axis_index(TP)
    kernels = Kernels(micro, tokens, cols, width, hidden, slots)

    packed = (
        (pad_to(self_qkv[0], rows, width), False),
        (pad_to(side_by_side([self_qkv[1], self_qkv[2]], width), rows, 2 * width), True),
        (pad_to(self_out.T, rows, width), False),
        (pad_to(cross_q, rows, width), False),
        (pad_to(side_by_side([cross_kv[0], cross_kv[1]], width), rows, 2 * width), True),
        (pad_to(cross_out.T, rows, width), False),
        (pad_to(side_by_side([up_w[0], up_w[1]], hidden), rows, 2 * hidden), True),
        (pad_to(down_w.T, rows, hidden), False),
    )
    flips = (False, True, True, False, False, True, False, True)
    full = []
    for place, ((shard, long_first), flip) in enumerate(zip(packed, flips)):
        full.append(gather_rows(shard, long_first, flip))
    w_q, w_kv, w_so, w_cq, w_ckv, w_co, w_up, w_down = full

    slot = jnp.arange(wide)
    block, row = slot // rows, slot % rows
    back_seq, back_dp = block // dp_size, block % dp_size
    from_seq = (lax.axis_index(SEQ) - back_seq) % seq_size
    from_dp = ring_member(DP, (ring_place(DP) - back_dp) % dp_size)
    valid = row < own_rows
    channel = jnp.where(valid, (from_dp * seq_size + from_seq) * own_rows + row, -1)
    pick = (jnp.arange(features)[:, None] == channel[None, :]).astype(BF16)

    def relative(values):
        return jnp.where(core == 0, values, jnp.flip(values, axis=0))

    lengths = relative(text_lengths[:, 0])
    caption = jnp.pad(relative(text[:, 0]), ((0, 0), (0, slots - text_len), (0, 0))).reshape(micro * slots, features)
    caption = dot(caption, pick, 1, 0).astype(BF16)
    resid_in = dot(lax.dynamic_index_in_dim(latents, core, 0, False).reshape(tokens, features), pick, 1, 0)
    grad_out = dot(lax.dynamic_index_in_dim(cotangent, core, 0, False).reshape(tokens, features), pick, 1, 0)

    frequency = jnp.exp(-math.log(10000.0) * channel.astype(F32) / features)
    time = lax.dynamic_index_in_dim(timesteps[:, 0], core, 0, False).astype(F32)
    waves = 0.5 * jnp.sin(time * frequency[None, :] + jnp.arange(6, dtype=F32)[:, None])
    mod_table = jnp.dot(table, pick.astype(F32), precision=lax.Precision.HIGHEST)
    modulation = jnp.where(valid[None, :], mod_table + waves, 0.0)
    shift_a, scale_a, gate_a, shift_f, scale_f, gate_f = [modulation[i] for i in range(6)]

    def normalise(values):
        center = jnp.where(valid[None, :], values - jnp.sum(values, axis=1, keepdims=True) / features, 0.0)
        spread = jnp.sum(center * center, axis=1, keepdims=True) / features
        inverse = lax.rsqrt(spread + NORM_EPS)
        return center * inverse, inverse

    def normalise_back(values, grad, stretch):
        unit, inverse = normalise(values)
        shift_grad = jnp.sum(grad, axis=0)
        scale_grad = jnp.sum(grad * unit, axis=0)
        scaled = grad * (1.0 + stretch)
        mean = jnp.sum(scaled, axis=1, keepdims=True) / features
        along = jnp.sum(scaled * unit, axis=1, keepdims=True) / features
        return jnp.where(valid[None, :], inverse * (scaled - mean - unit * along), 0.0), shift_grad, scale_grad

    def both(own):
        return jnp.concatenate([own, other_core(own)], axis=0)

    def core_total(parts):
        def product(at):
            return sum(dot(left[at : at + tokens], right, 1, dim) for left, right, dim in parts)

        return other_core(product(tokens).astype(BF16)).astype(F32) + product(0)

    ffn_grad = both((gate_f * grad_out).astype(BF16))

    unit_a, _ = normalise(resid_in)
    normed = both((unit_a * (1.0 + scale_a) + shift_a).astype(BF16))
    queries = dot(normed, w_q, 1, 0)
    keys_values = dot(normed, w_kv, 1, 0)
    states = butterfly(kernels.states(keys_values), (SEQ,), jnp.add)
    mixed = kernels.mix(queries, states)
    self_term = core_total([(mixed, w_so, 1)])
    resid_a = resid_in + gate_a * self_term
    cross_input = both(resid_a.astype(BF16))
    cross_query = dot(cross_input, w_cq, 1, 0).astype(BF16)
    text_proj = dot(caption, w_ckv, 1, 0).astype(BF16)
    attended, peaks = kernels.cross(lengths, cross_query, text_proj)
    resid_b = resid_a + core_total([(attended, w_co, 1)])
    unit_f, _ = normalise(resid_b)
    normed_ffn = both((unit_f * (1.0 + scale_f) + shift_f).astype(BF16))
    bias = side_by_side([up_b[0:1], up_b[1:2]], hidden)
    pre = dot(normed_ffn, w_up, 1, 0) + bias
    edges = jnp.concatenate(
        [pre.reshape(micro, tokens, 2 * hidden)[:, :cols], pre.reshape(micro, tokens, 2 * hidden)[:, -cols:]], axis=1
    )
    top, bottom = halos(silu(edges).astype(BF16), cols)
    filters = pad_to(conv_w.transpose(1, 0, 2), 2, 9, hidden)
    filter_bias = pad_to(conv_b, 2, hidden)[:, None]
    gated = kernels.conv(pre, top, bottom, filters, filter_bias)
    ffn_out = core_total([(gated, w_down, 1)])
    resid_c = resid_b + gate_f * ffn_out
    gate_f_grad = jnp.sum(grad_out * ffn_out, axis=0)

    def weight_grad(activation, grad, long_first, flip):
        parts = [
            dot(activation[:, b * near : (b + 1) * near], grad, 0, 0).astype(BF16) for b in range(seq_size)
        ]
        return scatter_rows(parts, long_first, flip)

    down_grad = weight_grad(ffn_grad, gated, False, True)
    gated_grad = dot(ffn_grad, w_down, 1, 0)
    conv_grad0, conv_grad1, small = kernels.conv_back(pre, top, bottom, gated_grad, filters, filter_bias)
    conv_grad = jnp.concatenate([conv_grad0, conv_grad1], axis=1)
    top_grad, bottom_grad = halos(conv_grad.reshape(micro, tokens, 2 * hidden), cols)
    up_low, bias_grad = kernels.act_back(pre, conv_grad, top_grad, bottom_grad, filters)
    small = butterfly(
        jnp.concatenate([jnp.sum(small, axis=0)[:20], jnp.sum(bias_grad, axis=0)[:1].reshape(2, hidden)], axis=0),
        (SEQ, DP), jnp.add,
    )
    up_grad = weight_grad(normed_ffn, up_low, True, False)
    normed_ffn_grad = core_total([(up_low, w_up, 1)])
    resid_b_part, shift_f_grad, scale_f_grad = normalise_back(resid_b, normed_ffn_grad, scale_f)
    resid_b_grad = grad_out + resid_b_part
    cross_grad = both(resid_b_grad.astype(BF16))
    attended_grad = dot(cross_grad, w_co, 1, 0).astype(BF16)
    cross_out_grad = weight_grad(cross_grad, attended, False, True)
    query_grad, key_grad, value_grad = kernels.cross_back(lengths, cross_query, text_proj, attended_grad)
    cross_kv_grad = weight_grad(caption, jnp.concatenate([key_grad, value_grad], axis=1), True, False)
    resid_a_grad = resid_b_grad + core_total([(query_grad, w_cq, 1)])
    cross_q_grad = weight_grad(cross_input, query_grad, False, False)
    gate_a_grad = jnp.sum(resid_a_grad * self_term, axis=0)
    self_grad = both((gate_a * resid_a_grad).astype(BF16))
    mixed_grad = dot(self_grad, w_so, 1, 0)
    self_out_grad = weight_grad(self_grad, mixed, False, True)
    q_low, state_grad = kernels.mix_back(queries, states, mixed_grad)
    state_grad = butterfly(state_grad, (SEQ,), jnp.add)
    kv_low = kernels.states_back(keys_values, state_grad)
    q_grad = weight_grad(normed, q_low, False, False)
    kv_grad = weight_grad(normed, kv_low, True, True)
    normed_grad = core_total([(q_low, w_q, 1), (kv_low, w_kv, 1)])
    resid_part, shift_a_grad, scale_a_grad = normalise_back(resid_in, normed_grad, scale_a)
    latent_grad = resid_a_grad + resid_part

    def whole(own):
        other = other_core(own)
        pair = jnp.where(core == 0, jnp.stack([own, other]), jnp.stack([other, own]))
        return pair.reshape(micro, 1, row_count, cols, features)

    high, low = split(latent_grad)
    output = whole(dot(resid_c.astype(BF16), pick, 1, 1).astype(BF16))
    latents_grad = whole(dot(high, pick, 1, 1) + dot(low, pick, 1, 1))
    mod_grad = jnp.stack([shift_a_grad, scale_a_grad, gate_a_grad, shift_f_grad, scale_f_grad, gate_f_grad])
    mod_grad = lax.dot_general(
        mod_grad, pick.astype(F32), (((1,), (1,)), ((), ())), precision=lax.Precision.HIGHEST
    )
    table_grad = butterfly(mod_grad, (TP, SEQ, DP), jnp.add)

    head_count = heads_width // HEAD_DIM
    head_peaks = jnp.max(peaks[:, :, : LANES // HEAD_DIM, 0], axis=0).reshape(-1)[:head_count]
    head_peaks = butterfly(head_peaks, (SEQ, DP), jnp.maximum)
    factor = jnp.repeat(jnp.sqrt(CLIP_TAU / jnp.maximum(head_peaks, CLIP_TAU)), HEAD_DIM)

    def cut(grad, count, each, size):
        grad = grad[:own_rows].reshape(own_rows, count, each)[:, :, :size]
        return grad.transpose(1, 0, 2)

    def heads(grad):
        return grad[:own_rows, :heads_width]

    taps_grad = small[:18].reshape(2, 9, hidden)[:, :, :hidden_width].transpose(1, 0, 2)
    return (
        output,
        latents_grad,
        table_grad,
        jnp.concatenate([heads(q_grad)[None], cut(kv_grad, 2, width, heads_width)], axis=0),
        heads(self_out_grad).T,
        heads(cross_q_grad),
        cut(cross_kv_grad, 2, width, heads_width),
        heads(cross_out_grad).T,
        cut(up_grad, 2, hidden, hidden_width),
        small[20:22, :hidden_width],
        taps_grad,
        small[18:20, :hidden_width],
        down_grad[:own_rows, :hidden_width].T,
        cross_q.astype(F32) * factor[None, :],
        cross_kv[0].astype(F32) * factor[None, :],
    )


def solution(mesh):
    tokens = P(None, DP, SEQ, None, None)
    stacked, by_column, by_row = P(None, (DP, SEQ), TP), P(TP, (DP, SEQ)), P((DP, SEQ), TP)
    return jax.shard_map(
        shards,
        mesh=mesh,
        in_specs=(
            tokens, P(None, DP, None, None), P(None, DP), P(None, DP), tokens, P(), stacked, by_column, by_row,
            stacked, by_column, stacked, P(None, TP), P(None, None, TP), P(None, TP), by_column,
        ),
        out_specs=(
            tokens, tokens, P(), stacked, by_column, by_row, stacked, by_column, stacked, P(None, TP),
            P(None, None, TP), P(None, TP), by_column, by_row, by_row,
        ),
        check_vma=False,
    )
```

profile of v0, /device:TPU:0, one launch (start us, length us, event | category | flops | bytes accessed | tf_op | source)
XLA Modules:
  0.0 3044.7 jit_solution(15647403839385248410)
XLA Ops:
  93.0 41.1 %collective-permute-done.45 = bf16[2,144,1152]{2,1,0:T(8,128)(2,1)S(1)} collective-permute-done((bf16[2,144,1152]{2,1,0:T(8,128)(2,1)S(1)}, bf16[2,144,1152]{2,1,0:T(8,128)(2,1)S(1)}, u32[]{:S(2)}, u32[]{:S(2)}) %collective-permute-start.45) | collective-permute-done | bytes 663584 | tf_op jit(solution)/shard_map/ppermute | solution.py:61
  211.7 42.5 %collective-permute-done.46 = bf16[2,144,1152]{2,1,0:T(8,128)(2,1)S(1)} collective-permute-done((bf16[2,144,1152]{2,1,0:T(8,128)(2,1)S(1)}, bf16[2,144,1152]{2,1,0:T(8,128)(2,1)S(1)}, u32[]{:S(2)}, u32[]{:S(2)}) %collective-permute-start.46) | collective-permute-done | bytes 663584 | tf_op jit(solution)/shard_map/ppermute | solution.py:61
  387.5 65.4 %collective-permute-done.15 = bf16[144,2304]{1,0:T(8,128)(2,1)S(1)} collective-permute-done((bf16[144,2304]{1,0:T(8,128)(2,1)S(1)}, bf16[144,2304]{1,0:T(8,128)(2,1)S(1)}, u32[]{:S(2)}, u32[]{:S(2)}) %collective-permute-start.15) | collective-permute-done | bytes 663584 | tf_op jit(solution)/shard_map/ppermute | solution.py:61
  536.8 84.4 %collective-permute-done.51 = bf16[2,144,1152]{2,1,0:T(8,128)(2,1)S(1)} collective-permute-done((bf16[2,144,1152]{2,1,0:T(8,128)(2,1)S(1)}, bf16[2,144,1152]{2,1,0:T(8,128)(2,1)S(1)}, u32[]{:S(2)}, u32[]{:S(2)}) %collective-permute-start.51) | collective-permute-done | bytes 663584 | tf_op jit(solution)/shard_map/ppermute | solution.py:61
  645.2 56.9 %collective-permute-done.25 = bf16[2,144,1152]{2,1,0:T(8,128)(2,1)S(1)} collective-permute-done((bf16[2,144,1152]{2,1,0:T(8,128)(2,1)S(1)}, bf16[2,144,1152]{2,1,0:T(8,128)(2,1)S(1)}, u32[]{:S(2)}, u32[]{:S(2)}) %collective-permute-start.25) | collective-permute-done | bytes 663584 | tf_op jit(solution)/shard_map/ppermute | solution.py:61
  722.9 31.7 %collective-permute-done.55 = bf16[144,5632]{1,0:T(8,128)(2,1)S(1)} collective-permute-done((bf16[144,5632]{1,0:T(8,128)(2,1)S(1)}, bf16[144,5632]{1,0:T(8,128)(2,1)S(1)}, u32[]{:S(2)}, u32[]{:S(2)}) %collective-permute-start.55) | collective-permute-done | bytes 1622048 | tf_op jit(solution)/shard_map/ppermute | solution.py:61
  793.3 30.8 %collective-permute-done.56 = bf16[144,5632]{1,0:T(8,128)(2,1)S(1)} collective-permute-done((bf16[144,5632]{1,0:T(8,128)(2,1)S(1)}, bf16[144,5632]{1,0:T(8,128)(2,1)S(1)}, u32[]{:S(2)}, u32[]{:S(2)}) %collective-permute-start.56) | collective-permute-done | bytes 1622048 | tf_op jit(solution)/shard_map/ppermute | solution.py:61
  828.5 30.3 collective-permute-done.67
  861.9 30.4 collective-permute-done.57
  901.4 27.4 collective-permute-done.71
  931.7 44.8 %collective-permute-done.16 = bf16[1152,2304]{1,0:T(8,128)(2,1)S(1)} collective-permute-done((bf16[1152,2304]{1,0:T(8,128)(2,1)}, bf16[1152,2304]{1,0:T(8,128)(2,1)S(1)}, u32[]{:S(2)}, u32[]{:S(2)}) %collective-permute-start.16) | collective-permute-done | bytes 5308448 | tf_op jit(solution)/shard_map/ppermute | solution.py:61
  1010.3 362.4 %collective-permute-done.17 = f32[2,9,40,128]{3,2,1,0:T(8,128)S(1)} collective-permute-done((f32[2,9,40,128]{3,2,1,0:T(8,128)S(1)}, f32[2,9,40,128]{3,2,1,0:T(8,128)S(1)}, u32[]{:S(2)}, u32[]{:S(2)}) %collective-permute-start.17) | collective-permute-done | bytes 368672 | tf_op jit(solution)/shard_map/ppermute | solution.py:119
  1432.6 34.9 %shard_map.273 = (bf16[1024,1152]{1,0:T(8,128)(2,1)S(1)}, f32[2,9,8,128]{3,2,1,0:T(8,128)S(1)}) custom-call(s32[2]{0:T(128)S(1)} %broadcast_select_fusion.length_ref, bf16[1024,1152]{1,0:T(8,128)(2,1)S(1)} %fusion.33.query_ref, bf16[608,2304]{1,0:T(8,128)(2,1)} %convolution_convert_fusion.16.key_ref.value_ref, ...), custom_call_target="tpu_custom_call" | custom-call | flops 23592960000 | bytes 7077888 | tf_op jit(solution)/shard_map/pallas_call | solution.py:415
  1528.2 38.0 %convolution_add_fusion.z0.z1.z_ref = f32[1024,5632]{1,0:T(8,128)} fusion(bf16[2304,5632]{1,0:T(8,128)(2,1)} %constant_dynamic-update-slice_fusion.50, f32[5632]{0:T(1024)S(1)} %copy-done.77, bf16[512,2304]{1,0:T(8,128)(2,1)S(1)} %collective-permute-done.53, bf16[512,2304]{1,0:T(8,128)(2,1)S(1)} %add_convert_fusion.1), kind=kOutput, calls=%fused_computation.12 | convolution fusion | flops 26590314496 | bytes 53762048 | tf_op jit(solution)/shard_map/dot_general | solution.py:27
  1592.3 50.7 %shard_map.275 = (bf16[1024,2816]{1,0:T(8,128)(2,1)}, bf16[1024,2816]{1,0:T(8,128)(2,1)}, f32[2,24,2816]{2,1,0:T(8,128)S(1)}) custom-call(f32[1024,5632]{1,0:T(8,128)} %convolution_add_fusion.z0.z1.z_ref, f32[1024,5632]{1,0:T(8,128)} %convolution_add_fusion.z0.z1.z_ref, bf16[2,32,5632]{2,1,0:T(8,128)(2,1)S(1)} %collective-permute-done.62.top0.top1, ...), custom_call_target="tpu_custom_call" | custom-call | flops 115343360000 | bytes 46137344 | tf_op jit(solution)/shard_map/pallas_call | solution.py:463
  1653.7 38.4 %shard_map.274 = bf16[1024,2816]{1,0:T(8,128)(2,1)} custom-call(f32[1024,5632]{1,0:T(8,128)} %convolution_add_fusion.z0.z1.z_ref, f32[1024,5632]{1,0:T(8,128)} %convolution_add_fusion.z0.z1.z_ref, bf16[2,32,5632]{2,1,0:T(8,128)(2,1)S(1)} %collective-permute-done.62.top0.top1, bf16[2,32,5632]{2,1,0:T(8,128)(2,1)S(1)} %collective-permute-done.62.top0.top1, ...), custom_call_target="tpu_custom_call" | custom-call | flops 57671680000 | bytes 28835840 | tf_op jit(solution)/shard_map/pallas_call | solution.py:453
  1733.4 61.9 %shard_map.276 = (bf16[1024,5632]{1,0:T(8,128)(2,1)}, f32[2,8,5632]{2,1,0:T(8,128)S(1)}) custom-call(f32[1024,5632]{1,0:T(8,128)} %convolution_add_fusion.z0.z1.z_ref, bf16[1024,5632]{1,0:T(8,128)(2,1)} %copy-done.23, bf16[2,32,5632]{2,1,0:T(8,128)(2,1)S(1)} %collective-permute-done.75.top, bf16[2,32,5632]{2,1,0:T(8,128)(2,1)S(1)} %collective-permute-done.76.bottom, ...), custom_call_target="tpu_custom_call" | custom-call | flops 57671680000 | bytes 46137344 | tf_op jit(solution)/shard_map/pallas_call | solution.py:474
  2023.2 52.5 %shard_map.277 = (bf16[1024,1152]{1,0:T(8,128)(2,1)S(1)}, bf16[608,1152]{1,0:T(8,128)(2,1)S(1)}, bf16[608,1152]{1,0:T(8,128)(2,1)S(1)}) custom-call(s32[2]{0:T(128)S(1)} %copy-done.7, bf16[1024,1152]{1,0:T(8,128)(2,1)} %copy-done.12, bf16[608,2304]{1,0:T(8,128)(2,1)} %convolution_convert_fusion.16.key_ref.value_ref, ...), custom_call_target="tpu_custom_call" | custom-call | flops 58982400000 | bytes 7077888 | tf_op jit(solution)/shard_map/pallas_call | solution.py:426
  2237.0 44.8 %collective-permute-done.141 = bf16[144,1152]{1,0:T(8,128)(2,1)S(1)} collective-permute-done((bf16[144,1152]{1,0:T(8,128)(2,1)S(1)}, bf16[144,1152]{1,0:T(8,128)(2,1)S(1)}, u32[]{:S(2)}, u32[]{:S(2)}) %collective-permute-start.141) | collective-permute-done | bytes 331808 | tf_op jit(solution)/shard_map/ppermute | solution.py:61
  2372.9 39.4 %collective-permute-done.81 = f32[2,9,40,128]{3,2,1,0:T(8,128)S(1)} collective-permute-done((f32[2,9,40,128]{3,2,1,0:T(8,128)S(1)}, f32[2,9,40,128]{3,2,1,0:T(8,128)S(1)}, u32[]{:S(2)}, u32[]{:S(2)}) %collective-permute-start.81) | collective-permute-done | bytes 368672 | tf_op jit(solution)/shard_map/ppermute | solution.py:119
  2414.0 25.6 shard_map.279
  2641.4 111.3 %collective-permute-done.85 = f32[6,2240]{1,0:T(8,128)S(1)} collective-permute-done((f32[6,2240]{1,0:T(8,128)S(1)}, f32[6,2240]{1,0:T(8,128)S(1)}, u32[]{:S(2)}, u32[]{:S(2)}) %collective-permute-start.85) | collective-permute-done | bytes 53792 | tf_op jit(solution)/shard_map/ppermute | solution.py:119
  2846.9 29.0 collective-permute-done.105
  2902.5 33.0 %collective-permute-done.109 = bf16[144,2304]{1,0:T(8,128)(2,1)} collective-permute-done((bf16[144,2304]{1,0:T(8,128)(2,1)}, bf16[144,2304]{1,0:T(8,128)(2,1)}, u32[]{:S(2)}, u32[]{:S(2)}) %collective-permute-start.109) | collective-permute-done | bytes 663584 | tf_op jit(solution)/shard_map/ppermute | solution.py:61
  (992 shorter events, 1633.6 us)
Async XLA Ops:
  10.5 154.5 %collective-permute-start.12 = (bf16[144,2304]{1,0:T(8,128)(2,1)}, bf16[144,2304]{1,0:T(8,128)(2,1)}, u32[]{:S(2)}, u32[]{:S(2)}) collective-permute-start(bf16[144,2304]{1,0:T(8,128)(2,1)} %get-tuple-element.222), channel_id=1, source_target_pairs={{0,4},{8,0},{16,8},{24,16},{28,24},{20,28},{12,20},{4,12},{1,5},{9... | collective-permute-start | bytes 1990664 | tf_op jit(solution)/shard_map/ppermute | solution.py:61
  68.9 312.4 %collective-permute-start.40 = (bf16[144,2304]{1,0:T(8,128)(2,1)}, bf16[144,2304]{1,0:T(8,128)(2,1)S(1)}, u32[]{:S(2)}, u32[]{:S(2)}) collective-permute-start(bf16[144,2304]{1,0:T(8,128)(2,1)} %get-tuple-element.256), channel_id=1, source_target_pairs={{0,4},{8,0},{16,8},{24,16},{28,24},{20,28},{12,20},{4,12},{1,5},{9... | collective-permute-start | bytes 1990664 | tf_op jit(solution)/shard_map/ppermute | solution.py:61
  74.2 133.9 %collective-permute-start.54 = (bf16[144,5632]{1,0:T(8,128)(2,1)}, bf16[144,5632]{1,0:T(8,128)(2,1)S(1)}, u32[]{:S(2)}, u32[]{:S(2)}) collective-permute-start(bf16[144,5632]{1,0:T(8,128)(2,1)} %get-tuple-element.178), channel_id=1, source_target_pairs={{0,8},{8,16},{16,24},{24,28},{28,20},{20,12},{12,4},{4,0},{1,9},{9... | collective-permute-start | bytes 4866056 | tf_op jit(solution)/shard_map/ppermute | solution.py:61
  176.8 179.4 %collective-permute-start.13 = (bf16[144,2304]{1,0:T(8,128)(2,1)}, bf16[144,2304]{1,0:T(8,128)(2,1)S(1)}, u32[]{:S(2)}, u32[]{:S(2)}) collective-permute-start(bf16[144,2304]{1,0:T(8,128)(2,1)} %collective-permute-done.12), channel_id=1, source_target_pairs={{0,4},{8,0},{16,8},{24,16},{28,24},{20,28},{12,20},{4,12},{1,5},{9... | collective-permute-start | bytes 1990664 | tf_op jit(solution)/shard_map/ppermute | solution.py:61
  191.0 195.1 %collective-permute-start.65 = (bf16[2,144,2816]{2,1,0:T(8,128)(2,1)S(1)}, bf16[2,144,2816]{2,1,0:T(8,128)(2,1)S(1)}, u32[]{:S(2)}, u32[]{:S(2)}) collective-permute-start(bf16[2,144,2816]{2,1,0:T(8,128)(2,1)S(1)} %pad_maximum_fusion.19), channel_id=1, source_target_pairs={{0,8},{8,16},{16,24},{24,28},{28,20},{20,12},{12,4},{4,0},{1,9},{9... | collective-permute-start | bytes 4866056 | tf_op jit(solution)/shard_map/ppermute | solution.py:61
  475.8 236.9 %collective-permute-start.58 = (bf16[144,5632]{1,0:T(8,128)(2,1)}, bf16[144,5632]{1,0:T(8,128)(2,1)S(1)}, u32[]{:S(2)}, u32[]{:S(2)}) collective-permute-start(bf16[144,5632]{1,0:T(8,128)(2,1)} %get-tuple-element.178), channel_id=1, source_target_pairs={{0,4},{8,0},{16,8},{24,16},{28,24},{20,28},{12,20},{4,12},{1,5},{9... | collective-permute-start | bytes 4866056 | tf_op jit(solution)/shard_map/ppermute | solution.py:61
  490.1 145.7 %collective-permute-start.7 = (bf16[2,144,1152]{2,1,0:T(8,128)(2,1)S(1)}, bf16[2,144,1152]{2,1,0:T(8,128)(2,1)S(1)}, u32[]{:S(2)}, u32[]{:S(2)}) collective-permute-start(bf16[2,144,1152]{2,1,0:T(8,128)(2,1)S(1)} %collective-permute-done.6), channel_id=1, source_target_pairs={{0,4},{8,0},{16,8},{24,16},{28,24},{20,28},{12,20},{4,12},{1,5},{9... | collective-permute-start | bytes 1990664 | tf_op jit(solution)/shard_map/ppermute | solution.py:61
  504.3 131.6 %collective-permute-start.35 = (bf16[2,144,1152]{2,1,0:T(8,128)(2,1)S(1)}, bf16[2,144,1152]{2,1,0:T(8,128)(2,1)S(1)}, u32[]{:S(2)}, u32[]{:S(2)}) collective-permute-start(bf16[2,144,1152]{2,1,0:T(8,128)(2,1)S(1)} %collective-permute-done.34), channel_id=1, source_target_pairs={{0,4},{8,0},{16,8},{24,16},{28,24},{20,28},{12,20},{4,12},{1,5},{9... | collective-permute-start | bytes 1990664 | tf_op jit(solution)/shard_map/ppermute | solution.py:61
  722.5 771.2 %collective-permute-start.74 = (bf16[512,2304]{1,0:T(8,128)(2,1)}, bf16[512,2304]{1,0:T(8,128)(2,1)}, u32[]{:S(2)}, u32[]{:S(2)}) collective-permute-start(bf16[512,2304]{1,0:T(8,128)(2,1)} %get-tuple-element.249), channel_id=1, source_target_pairs={{0,1},{1,0},{2,3},{3,2},{4,5},{5,4},{6,7},{7,6},{8,9},{9,8},{10,11... | collective-permute-start | bytes 7077896 | tf_op jit(solution)/shard_map/ppermute | solution.py:125
  767.8 127.0 %collective-permute-start.60 = (bf16[144,5632]{1,0:T(8,128)(2,1)S(1)}, bf16[144,5632]{1,0:T(8,128)(2,1)S(1)}, u32[]{:S(2)}, u32[]{:S(2)}) collective-permute-start(bf16[144,5632]{1,0:T(8,128)(2,1)S(1)} %collective-permute-done.59), channel_id=1, source_target_pairs={{0,4},{8,0},{16,8},{24,16},{28,24},{20,28},{12,20},{4,12},{1,5},{9... | collective-permute-start | bytes 4866056 | tf_op jit(solution)/shard_map/ppermute | solution.py:61
  860.6 545.7 %collective-permute-start.43 = (bf16[1152,2304]{1,0:T(8,128)(2,1)}, bf16[1152,2304]{1,0:T(8,128)(2,1)S(1)}, u32[]{:S(2)}, u32[]{:S(2)}) collective-permute-start(bf16[1152,2304]{1,0:T(8,128)(2,1)} %get-tuple-element.189), channel_id=1, source_target_pairs={{0,2},{2,0},{1,3},{3,1},{4,6},{6,4},{5,7},{7,5},{8,10},{10,8},{9,1... | collective-permute-start | bytes 15925256 | tf_op jit(solution)/shard_map/ppermute | solution.py:61
  900.5 616.9 %collective-permute-start.61 = (bf16[1152,5632]{1,0:T(8,128)(2,1)}, bf16[1152,5632]{1,0:T(8,128)(2,1)}, u32[]{:S(2)}, u32[]{:S(2)}) collective-permute-start(bf16[1152,5632]{1,0:T(8,128)(2,1)} %get-tuple-element.162), channel_id=1, source_target_pairs={{0,2},{2,0},{1,3},{3,1},{4,6},{6,4},{5,7},{7,5},{8,10},{10,8},{9,1... | collective-permute-start | bytes 38928392 | tf_op jit(solution)/shard_map/ppermute | solution.py:61
  1007.5 365.3 %collective-permute-start.17 = (f32[2,9,40,128]{3,2,1,0:T(8,128)S(1)}, f32[2,9,40,128]{3,2,1,0:T(8,128)S(1)}, u32[]{:S(2)}, u32[]{:S(2)}) collective-permute-start(f32[2,9,40,128]{3,2,1,0:T(8,128)S(1)} %shard_map.271), channel_id=1, source_target_pairs={{0,2},{2,0},{1,3},{3,1},{4,6},{6,4},{5,7},{7,5},{8,10},{10,8},{9,1... | collective-permute-start | bytes 1105928 | tf_op jit(solution)/shard_map/ppermute | solution.py:119
  1717.2 149.9 %collective-permute-start.184 = (bf16[144,2816]{1,0:T(8,128)(2,1)}, bf16[144,2816]{1,0:T(8,128)(2,1)}, u32[]{:S(2)}, u32[]{:S(2)}) collective-permute-start(bf16[144,2816]{1,0:T(8,128)(2,1)} %get-tuple-element.101), channel_id=1, source_target_pairs={{0,4},{8,0},{16,8},{24,16},{28,24},{20,28},{12,20},{4,12},{1,5},{9... | collective-permute-start | bytes 2433032 | tf_op jit(solution)/shard_map/ppermute | solution.py:61
  1731.4 141.5 %collective-permute-start.177 = (bf16[144,2816]{1,0:T(8,128)(2,1)}, bf16[144,2816]{1,0:T(8,128)(2,1)S(1)}, u32[]{:S(2)}, u32[]{:S(2)}) collective-permute-start(bf16[144,2816]{1,0:T(8,128)(2,1)} %get-tuple-element.92), channel_id=1, source_target_pairs={{0,4},{8,0},{16,8},{24,16},{28,24},{20,28},{12,20},{4,12},{1,5},{9... | collective-permute-start | bytes 2433032 | tf_op jit(solution)/shard_map/ppermute | solution.py:61
  1982.6 794.3 %collective-permute-start.165 = (bf16[8,144,5632]{2,1,0:T(8,128)(2,1)}, bf16[8,144,5632]{2,1,0:T(8,128)(2,1)}, u32[]{:S(2)}, u32[]{:S(2)}) collective-permute-start(bf16[8,144,5632]{2,1,0:T(8,128)(2,1)} %bitcast.571), channel_id=1, source_target_pairs={{0,2},{2,0},{1,3},{3,1},{4,6},{6,4},{5,7},{7,5},{8,10},{10,8},{9,1... | collective-permute-start | bytes 38928392 | tf_op jit(solution)/shard_map/ppermute | solution.py:61
  2283.0 201.0 %collective-permute-start.142 = (bf16[8,144,2304]{2,1,0:T(8,128)(2,1)}, bf16[8,144,2304]{2,1,0:T(8,128)(2,1)}, u32[]{:S(2)}, u32[]{:S(2)}) collective-permute-start(bf16[8,144,2304]{2,1,0:T(8,128)(2,1)} %bitcast.573), channel_id=1, source_target_pairs={{0,2},{2,0},{1,3},{3,1},{4,6},{6,4},{5,7},{7,5},{8,10},{10,8},{9,1... | collective-permute-start | bytes 15925256 | tf_op jit(solution)/shard_map/ppermute | solution.py:61
  2329.8 172.8 %collective-permute-start.100 = (bf16[144,1152]{1,0:T(8,128)(2,1)}, bf16[144,1152]{1,0:T(8,128)(2,1)}, u32[]{:S(2)}, u32[]{:S(2)}) collective-permute-start(bf16[144,1152]{1,0:T(8,128)(2,1)} %get-tuple-element.161), channel_id=1, source_target_pairs={{0,8},{8,16},{16,24},{24,28},{28,20},{20,12},{12,4},{4,0},{1,9},{9... | collective-permute-start | bytes 995336 | tf_op jit(solution)/shard_map/ppermute | solution.py:61
  2369.6 135.0 %collective-permute-start.93 = (bf16[144,1152]{1,0:T(8,128)(2,1)}, bf16[144,1152]{1,0:T(8,128)(2,1)}, u32[]{:S(2)}, u32[]{:S(2)}) collective-permute-start(bf16[144,1152]{1,0:T(8,128)(2,1)} %get-tuple-element.150), channel_id=1, source_target_pairs={{0,8},{8,16},{16,24},{24,28},{28,20},{20,12},{12,4},{4,0},{1,9},{9... | collective-permute-start | bytes 995336 | tf_op jit(solution)/shard_map/ppermute | solution.py:61
  2623.4 129.6 %collective-permute-start.147 = (bf16[144,2304]{1,0:T(8,128)(2,1)S(1)}, bf16[144,2304]{1,0:T(8,128)(2,1)S(1)}, u32[]{:S(2)}, u32[]{:S(2)}) collective-permute-start(bf16[144,2304]{1,0:T(8,128)(2,1)S(1)} %copy-done.54), channel_id=1, source_target_pairs={{0,8},{8,16},{16,24},{24,28},{28,20},{20,12},{12,4},{4,0},{1,9},{9... | collective-permute-start | bytes 1990664 | tf_op jit(solution)/shard_map/ppermute | solution.py:61
  2628.9 124.2 %collective-permute-start.145 = (bf16[144,2304]{1,0:T(8,128)(2,1)S(1)}, bf16[144,2304]{1,0:T(8,128)(2,1)S(1)}, u32[]{:S(2)}, u32[]{:S(2)}) collective-permute-start(bf16[144,2304]{1,0:T(8,128)(2,1)S(1)} %fusion.94), channel_id=1, source_target_pairs={{0,4},{8,0},{16,8},{24,16},{28,24},{20,28},{12,20},{4,12},{1,5},{9... | collective-permute-start | bytes 1990664 | tf_op jit(solution)/shard_map/ppermute | solution.py:61
  2635.8 194.1 %collective-permute-start.104 = (bf16[8,144,2304]{2,1,0:T(8,128)(2,1)}, bf16[8,144,2304]{2,1,0:T(8,128)(2,1)}, u32[]{:S(2)}, u32[]{:S(2)}) collective-permute-start(bf16[8,144,2304]{2,1,0:T(8,128)(2,1)} %bitcast.572), channel_id=1, source_target_pairs={{0,2},{2,0},{1,3},{3,1},{4,6},{6,4},{5,7},{7,5},{8,10},{10,8},{9,1... | collective-permute-start | bytes 15925256 | tf_op jit(solution)/shard_map/ppermute | solution.py:61
  2757.4 129.3 %collective-permute-start.146 = (bf16[144,2304]{1,0:T(8,128)(2,1)}, bf16[144,2304]{1,0:T(8,128)(2,1)}, u32[]{:S(2)}, u32[]{:S(2)}) collective-permute-start(bf16[144,2304]{1,0:T(8,128)(2,1)} %get-tuple-element.80), channel_id=1, source_target_pairs={{0,4},{8,0},{16,8},{24,16},{28,24},{20,28},{12,20},{4,12},{1,5},{9... | collective-permute-start | bytes 1990664 | tf_op jit(solution)/shard_map/ppermute | solution.py:61
  2808.1 144.1 %collective-permute-start.83 = (f32[512,2240]{0,1:T(8,128)}, f32[512,2240]{0,1:T(8,128)}, u32[]{:S(2)}, u32[]{:S(2)}) collective-permute-start(f32[512,2240]{0,1:T(8,128)} %fusion.20), channel_id=1, source_target_pairs={{0,1},{1,0},{2,3},{3,2},{4,5},{5,4},{6,7},{7,6},{8,9},{9,8},{10,11... | collective-permute-start | bytes 13762568 | tf_op jit(solution)/shard_map/ppermute | solution.py:125
  (311 other events, 12456.6 us)
where the time goes:
time: 3070 us; the launch traced here: 3040 us
  waiting for transfers between devices  1690 us (55%)
  matrix products  470 us (15%)
  Pallas kernels  308 us (10%)
  starting transfers between devices  210 us (7%)
  local copies, waits for them, and re-layouts  201 us (7%)
  other arithmetic  163 us (5%)
    ppermute x163, waiting for transfers between devices, shift(): lax.ppermute(values, axis, [(cycle[i], cycle[(i + step) % size]) for i in...  1120 us
    ppermute x15, waiting for transfers between devices, butterfly(): lax.ppermute(values, axis, [(i, i ^ bit) for i in range(size)])  548 us
    dot_general x44, matrix products, dot(): lax.dot_general(left, right, (((left_dim,), (right_dim,)), ((), ())), pre...  455 us
    ppermute x163, starting transfers between devices, shift(): lax.ppermute(values, axis, [(cycle[i], cycle[(i + step) % size]) for i in...  188 us
    unnamed x376, local copies, waits for them, and re-layouts  97.5 us
    pallas_call x1, Pallas kernels, act_back(): call(functools.partial(act_back_kernel, self.cols), (self.micro, 2 * unit...  61.9 us
  transfers between devices with their start and end apart: 196, of which 89 were waited for; matrix products, arithmetic and copies ran while one was open for 26% of the time, Pallas kernels for 8%

commit v1 on v0

--- a/solution.py
+++ b/solution.py
@@ -56,6 +56,8 @@
 
 
 def shift(values, axis, step):
+    if isinstance(step, list):
+        return lax.ppermute(values, axis, step)
     cycle = ring_of(axis)
     size = len(cycle)
     return lax.ppermute(values, axis, [(cycle[i], cycle[(i + step) % size]) for i in range(size)])
@@ -89,26 +91,216 @@
     return total
 
 
-def gather_rows(shard, long_first, flip):
-    if long_first:
-        near = jnp.concatenate(ring_gather(shard, DP, flip), axis=0)
-        return jnp.concatenate(ring_gather(near, SEQ, False), axis=0)
-    pair = jnp.stack(ring_gather(shard, SEQ, False))
-    pieces = ring_gather(pair, DP, flip)
-    return jnp.concatenate([piece[b] for b in range(pair.shape[0]) for piece in pieces], axis=0)
-
-
-def scatter_rows(parts, long_first, flip):
+def slot_order(size):
+    ahead = size // 2
+    order = []
+    for step in range(ahead):
+        order.append(ahead - step)
+        if ahead + 1 + step < size:
+            order.append(ahead + 1 + step)
+    return order + [0]
+
+
+def in_slots(pieces):
+    return [pieces[a] for a in slot_order(len(pieces))]
+
+
+class Wire:
+    def __init__(self):
+        self.running, self.queue, self.last = [], [], ()
+        self.stride, self.since = lax.axis_size(DP) // 2, lax.axis_size(DP)
+
+    def join(self, phases):
+        self.running.append((phases, next(phases)))
+
+    def push(self, phases):
+        self.queue.append(phases)
+
+    def round(self):
+        if self.queue and self.since >= self.stride:
+            self.join(self.queue.pop(0))
+            self.since = 0
+        if not self.running:
+            return
+        self.since += 1
+        sends = [send for _, pending in self.running for send in pending]
+        values = tuple(value for value, _, _ in sends)
+        if self.last:
+            values, _ = lax.optimization_barrier((values, self.last))
+        arrived = tuple(shift(value, axis, step) for value, (_, axis, step) in zip(values, sends))
+        self.last = arrived
+        running, at = [], 0
+        for phases, pending in self.running:
+            mine = arrived[at : at + len(pending)]
+            at += len(pending)
+            try:
+                running.append((phases, phases.send(mine)))
+            except StopIteration:
+                pass
+        self.running = running
+
+    def step(self, value):
+        before = self.last
+        self.round()
+        return lax.optimization_barrier((value, before))[0] if before else value
+
+    def need(self, done):
+        while not done:
+            self.round()
+        return done
+
+    def finish(self):
+        while self.running or self.queue:
+            self.round()
+
+
+def butterfly_phases(values, axes, combine, done):
+    for axis in axes:
+        size = lax.axis_size(axis)
+        bit = 1
+        while bit < size:
+            (arrived,) = yield [(values, axis, [(i, i ^ bit) for i in range(size)])]
+            values = combine(values, arrived)
+            bit *= 2
+    done.append(values)
+
+
+def columns(values, widths):
+    at, parts = 0, []
+    for width in widths:
+        parts.append(values[:, at : at + width])
+        at += width
+    return parts
+
+
+def gather_phases(first, second, done):
+    size = lax.axis_size(DP)
+    ahead = size // 2
+    widths_a, widths_b = [w.shape[1] for w in first], [w.shape[1] for w in second]
+    shard_a, shard_b = jnp.concatenate(first, axis=1), jnp.concatenate(second, axis=1)
+    n_a, n_b = shard_a.shape[1], shard_b.shape[1]
+    rows = shard_a.shape[0]
+    (far_b,) = yield [(shard_b, SEQ, 1)]
+    pieces = [jnp.concatenate([shard_a, shard_b, far_b], axis=1)] + [None] * (size - 1)
+    far = [None] * size
+    fresh = [0]
+    for hop in range(1, ahead + 2):
+        sends, places = [], []
+        if hop <= ahead:
+            sends.append((pieces[hop - 1], DP, 1))
+            places.append(hop)
+        if size - hop > ahead:
+            sends.append((pieces[(size - hop + 1) % size], DP, -1))
+            places.append(size - hop)
+        across = [pieces[a][:, :n_a] for a in fresh]
+        sends.append((jnp.concatenate(across, axis=0) if len(across) > 1 else across[0], SEQ, 1))
+        arrived = yield sends
+        for i, a in enumerate(fresh):
+            far[a] = arrived[-1][i * rows : (i + 1) * rows]
+        for a, piece in zip(places, arrived):
+            pieces[a] = piece
+        fresh = places
+    full = []
+    at = 0
+    for width in widths_a:
+        blocks = [p[:, at : at + width] for p in in_slots(pieces)] + [p[:, at : at + width] for p in in_slots(far)]
+        full.append(jnp.concatenate(blocks, axis=0))
+        at += width
+    for width in widths_b:
+        blocks = [p[:, at : at + width] for p in in_slots(pieces)]
+        blocks += [p[:, at + n_b : at + n_b + width] for p in in_slots(pieces)]
+        full.append(jnp.concatenate(blocks, axis=0))
+        at += width
+    done.extend(full)
+
+
+def gather_slow(shard):
+    near = jnp.concatenate(in_slots(ring_gather(shard, DP, False)), axis=0)
+    return jnp.concatenate(ring_gather(near, SEQ, False), axis=0)
+
+
+def gather(wire, first, second):
+    done = []
+    if lax.axis_size(SEQ) == 2:
+        wire.push(gather_phases(first, second, done))
+    else:
+        done.extend(gather_slow(shard) for shard in first + second)
+    return done
+
+
+def scatter_slow(parts):
     dp_size = lax.axis_size(DP)
+    order = slot_order(dp_size)
     parts = [part.reshape(dp_size, part.shape[0] // dp_size, part.shape[1]) for part in parts]
-    if long_first:
-        near = ring_scatter([lambda b=b: parts[b].astype(F32) for b in range(len(parts))], SEQ, False)
-        return ring_scatter([lambda a=a: near[a] for a in range(dp_size)], DP, flip)
-    far = [
-        ring_scatter([lambda a=a, part=part: part[a].astype(F32) for a in range(dp_size)], DP, flip)
-        for part in parts
-    ]
-    return ring_scatter([lambda b=b: far[b] for b in range(len(far))], SEQ, False)
+    near = ring_scatter([lambda b=b: parts[b].astype(F32) for b in range(len(parts))], SEQ, False)
+    return ring_scatter([lambda a=a: near[order.index(a)] for a in range(dp_size)], DP, False)
+
+
+def scatter_phases(first, second, done):
+    size = lax.axis_size(DP)
+    ahead = size // 2
+    order = slot_order(size)
+    rows = first[0][0].shape[0] // size
+    widths = [parts[0].shape[1] for parts in first + second]
+    n_a = sum(parts[0].shape[1] for parts in first)
+    n_b = sum(parts[0].shape[1] for parts in second)
+
+    def block(array, start, count=1):
+        return array[start * rows : (start + count) * rows]
+
+    def across(start, count):
+        blocks = [block(parts[1], start, count) for parts in first]
+        return (jnp.concatenate(blocks, axis=1) if len(blocks) > 1 else blocks[0], SEQ, 1)
+
+    def value(a, far):
+        slot = order.index(a)
+        near = [block(parts[0], slot) for parts in first]
+        near = jnp.concatenate(near, axis=1) if len(near) > 1 else near[0]
+        terms = [near.astype(F32) + far[a].astype(F32)]
+        for b in range(2):
+            terms += [block(parts[b], slot).astype(F32) for parts in second]
+        return jnp.concatenate(terms, axis=1)
+
+    def take(far, arrived, start):
+        for i in range(arrived.shape[0] // rows):
+            far[order[start + i]] = arrived[i * rows : (i + 1) * rows]
+
+    far = {}
+    (arrived,) = yield [across(0, 2)]
+    take(far, arrived, 0)
+    back = forth = None
+    for step in range(ahead):
+        sends = []
+        here = value(ahead - step, far)
+        back = here if back is None else back.astype(F32) + here
+        sends.append((back.astype(BF16), DP, -1))
+        place = ahead + 1 + step
+        if place < size:
+            here = value(place, far)
+            forth = here if forth is None else forth.astype(F32) + here
+            sends.append((forth.astype(BF16), DP, 1))
+        start = 2 * step + 2
+        if start < size:
+            sends.append(across(start, min(2, size - start)))
+        arrived = yield sends
+        back = arrived[0]
+        if place < size:
+            forth = arrived[1]
+        if start < size:
+            take(far, arrived[-1], start)
+    total = value(0, far) + back.astype(F32) + forth.astype(F32)
+    (other,) = yield [(total[:, n_a + n_b :].astype(BF16), SEQ, 1)]
+    mine = total[:, n_a : n_a + n_b] + other.astype(F32)
+    done.extend(columns(total[:, :n_a], widths[: len(first)]) + columns(mine, widths[len(first) :]))
+
+
+def scatter(wire, first, second):
+    done = []
+    if lax.axis_size(SEQ) == 2:
+        wire.push(scatter_phases(first, second, done))
+    else:
+        done.extend(scatter_slow(parts) for parts in first + second)
+    return done
 
 
 def butterfly(values, axes, combine):
@@ -508,33 +700,36 @@
     own_rows, heads_width = cross_q.shape
     hidden_width = up_b.shape[1]
     text_len = text.shape[2]
-    width, hidden, slots = up_to(heads_width, LANES), up_to(hidden_width, LANES), up_to(text_len, 16)
+    width, hidden, slots = up_to(heads_width, LANES), up_to(hidden_width, 2 * LANES), up_to(text_len, 16)
     rows = up_to(own_rows, 16)
     dp_size, seq_size = lax.axis_size(DP), lax.axis_size(SEQ)
     near = dp_size * rows
     wide = seq_size * near
     core = lax.axis_index(TP)
-    kernels = Kernels(micro, tokens, cols, width, hidden, slots)
-
-    packed = (
-        (pad_to(self_qkv[0], rows, width), False),
-        (pad_to(side_by_side([self_qkv[1], self_qkv[2]], width), rows, 2 * width), True),
-        (pad_to(self_out.T, rows, width), False),
-        (pad_to(cross_q, rows, width), False),
-        (pad_to(side_by_side([cross_kv[0], cross_kv[1]], width), rows, 2 * width), True),
-        (pad_to(cross_out.T, rows, width), False),
-        (pad_to(side_by_side([up_w[0], up_w[1]], hidden), rows, 2 * hidden), True),
-        (pad_to(down_w.T, rows, hidden), False),
-    )
-    flips = (False, True, True, False, False, True, False, True)
-    full = []
-    for place, ((shard, long_first), flip) in enumerate(zip(packed, flips)):
-        full.append(gather_rows(shard, long_first, flip))
-    w_q, w_kv, w_so, w_cq, w_ckv, w_co, w_up, w_down = full
+    kernels = Kernels(micro, tokens, cols, width, hidden // 2, slots)
+
+    half = hidden // 2
+
+    def units(values, at):
+        return pad_to(values[:, at * half : (at + 1) * half], values.shape[0], half)
+
+    def heads_rows(*parts):
+        return pad_to(side_by_side(parts, width), rows, len(parts) * width)
+
+    def ffn_rows(at):
+        up = jnp.concatenate([units(up_w[0], at), units(up_w[1], at)], axis=1)
+        return [pad_to(up, rows, 2 * half)], [pad_to(units(down_w.T, at), rows, half)]
+
+    wire = Wire()
+    qkv_rows = gather(wire, [heads_rows(self_qkv[1], self_qkv[2])], [heads_rows(self_qkv[0])])
+    token_rows = gather(wire, [heads_rows(cross_q)], [heads_rows(self_out.T)])
+    text_rows = gather(wire, [heads_rows(cross_kv[0], cross_kv[1])], [heads_rows(cross_out.T)])
+    unit_rows = [gather(wire, *ffn_rows(at)) for at in range(2)]
 
     slot = jnp.arange(wide)
     block, row = slot // rows, slot % rows
-    back_seq, back_dp = block // dp_size, block % dp_size
+    back_seq = block // dp_size
+    back_dp = sum(jnp.where(block % dp_size == k, a, 0) for k, a in enumerate(slot_order(dp_size)))
     from_seq = (lax.axis_index(SEQ) - back_seq) % seq_size
     from_dp = ring_member(DP, (ring_place(DP) - back_dp) % dp_size)
     valid = row < own_rows
@@ -581,72 +776,88 @@
 
         return other_core(product(tokens).astype(BF16)).astype(F32) + product(0)
 
-    ffn_grad = both((gate_f * grad_out).astype(BF16))
+    ffn_out_grad = both((gate_f * grad_out).astype(BF16))
+
+    def weight_grad(activation, grad):
+        return [dot(activation[:, b * near : (b + 1) * near], grad, 0, 0).astype(BF16) for b in range(seq_size)]
 
     unit_a, _ = normalise(resid_in)
     normed = both((unit_a * (1.0 + scale_a) + shift_a).astype(BF16))
-    queries = dot(normed, w_q, 1, 0)
+    w_kv, w_q = wire.need(qkv_rows)
     keys_values = dot(normed, w_kv, 1, 0)
     states = butterfly(kernels.states(keys_values), (SEQ,), jnp.add)
-    mixed = kernels.mix(queries, states)
+    queries = dot(wire.step(normed), w_q, 1, 0)
+    mixed = kernels.mix(queries, wire.step(states))
+    w_cq, w_so = wire.need(token_rows)
     self_term = core_total([(mixed, w_so, 1)])
     resid_a = resid_in + gate_a * self_term
     cross_input = both(resid_a.astype(BF16))
     cross_query = dot(cross_input, w_cq, 1, 0).astype(BF16)
+    w_ckv, w_co = wire.need(text_rows)
     text_proj = dot(caption, w_ckv, 1, 0).astype(BF16)
-    attended, peaks = kernels.cross(lengths, cross_query, text_proj)
-    resid_b = resid_a + core_total([(attended, w_co, 1)])
+    attended, peaks = kernels.cross(lengths, cross_query, wire.step(text_proj))
+    resid_b = resid_a + core_total([(wire.step(attended), w_co, 1)])
     unit_f, _ = normalise(resid_b)
     normed_ffn = both((unit_f * (1.0 + scale_f) + shift_f).astype(BF16))
-    bias = side_by_side([up_b[0:1], up_b[1:2]], hidden)
-    pre = dot(normed_ffn, w_up, 1, 0) + bias
-    edges = jnp.concatenate(
-        [pre.reshape(micro, tokens, 2 * hidden)[:, :cols], pre.reshape(micro, tokens, 2 * hidden)[:, -cols:]], axis=1
-    )
-    top, bottom = halos(silu(edges).astype(BF16), cols)
-    filters = pad_to(conv_w.transpose(1, 0, 2), 2, 9, hidden)
-    filter_bias = pad_to(conv_b, 2, hidden)[:, None]
-    gated = kernels.conv(pre, top, bottom, filters, filter_bias)
-    ffn_out = core_total([(gated, w_down, 1)])
+
+    ffn_terms, backs, smalls, ffn_grads = [], [], [], []
+    for at in range(2):
+        w_up, w_down = wire.need(unit_rows[at])
+        bias = jnp.concatenate([units(up_b[0:1], at), units(up_b[1:2], at)], axis=1)
+        filters = jnp.stack([units(conv_w[:, j], at) for j in range(2)])
+        filter_bias = jnp.stack([units(conv_b[j : j + 1], at) for j in range(2)])
+        pre = dot(wire.step(normed_ffn), w_up, 1, 0) + bias
+        by_micro = pre.reshape(micro, tokens, 2 * half)
+        edges = jnp.concatenate([by_micro[:, :cols], by_micro[:, -cols:]], axis=1)
+        top, bottom = halos(silu(edges).astype(BF16), cols)
+        gated_grad = dot(ffn_out_grad, w_down, 1, 0)
+        pre, top, bottom = wire.step((pre, top, bottom))
+        gated = kernels.conv(pre, top, bottom, filters, filter_bias)
+        gated_grad = wire.step(gated_grad)
+        conv_grad0, conv_grad1, small = kernels.conv_back(pre, top, bottom, gated_grad, filters, filter_bias)
+        conv_grad = jnp.concatenate([conv_grad0, conv_grad1], axis=1)
+        top_grad, bottom_grad = halos(conv_grad.reshape(micro, tokens, 2 * half), cols)
+        down_parts = weight_grad(ffn_out_grad, gated)
+        top_grad, bottom_grad = wire.step((top_grad, bottom_grad))
+        up_low, bias_grad = kernels.act_back(pre, conv_grad, top_grad, bottom_grad, filters)
+        smalls.append(
+            jnp.concatenate([jnp.sum(small, axis=0)[:20], jnp.sum(bias_grad, axis=0)[:1].reshape(2, half)], axis=0)
+        )
+        up_low = wire.step(up_low)
+        ffn_grads.append(scatter(wire, [weight_grad(normed_ffn, up_low)], [down_parts]))
+        ffn_terms.append((gated, w_down, 1))
+        backs.append((up_low, w_up, 1))
+    small, head_peaks = [], []
+    wire.join(butterfly_phases(jnp.concatenate(smalls, axis=1), (SEQ, DP), jnp.add, small))
+    head_count = heads_width // HEAD_DIM
+    own_peaks = jnp.max(peaks[:, :, : LANES // HEAD_DIM, 0], axis=0).reshape(-1)[:head_count]
+    wire.join(butterfly_phases(own_peaks, (SEQ, DP), jnp.maximum, head_peaks))
+
+    normed_ffn_grad = core_total(backs)
+    ffn_out = core_total(ffn_terms)
     resid_c = resid_b + gate_f * ffn_out
     gate_f_grad = jnp.sum(grad_out * ffn_out, axis=0)
-
-    def weight_grad(activation, grad, long_first, flip):
-        parts = [
-            dot(activation[:, b * near : (b + 1) * near], grad, 0, 0).astype(BF16) for b in range(seq_size)
-        ]
-        return scatter_rows(parts, long_first, flip)
-
-    down_grad = weight_grad(ffn_grad, gated, False, True)
-    gated_grad = dot(ffn_grad, w_down, 1, 0)
-    conv_grad0, conv_grad1, small = kernels.conv_back(pre, top, bottom, gated_grad, filters, filter_bias)
-    conv_grad = jnp.concatenate([conv_grad0, conv_grad1], axis=1)
-    top_grad, bottom_grad = halos(conv_grad.reshape(micro, tokens, 2 * hidden), cols)
-    up_low, bias_grad = kernels.act_back(pre, conv_grad, top_grad, bottom_grad, filters)
-    small = butterfly(
-        jnp.concatenate([jnp.sum(small, axis=0)[:20], jnp.sum(bias_grad, axis=0)[:1].reshape(2, hidden)], axis=0),
-        (SEQ, DP), jnp.add,
-    )
-    up_grad = weight_grad(normed_ffn, up_low, True, False)
-    normed_ffn_grad = core_total([(up_low, w_up, 1)])
-    resid_b_part, shift_f_grad, scale_f_grad = normalise_back(resid_b, normed_ffn_grad, scale_f)
+    resid_b_part, shift_f_grad, scale_f_grad = normalise_back(resid_b, wire.step(normed_ffn_grad), scale_f)
     resid_b_grad = grad_out + resid_b_part
     cross_grad = both(resid_b_grad.astype(BF16))
-    attended_grad = dot(cross_grad, w_co, 1, 0).astype(BF16)
-    cross_out_grad = weight_grad(cross_grad, attended, False, True)
-    query_grad, key_grad, value_grad = kernels.cross_back(lengths, cross_query, text_proj, attended_grad)
-    cross_kv_grad = weight_grad(caption, jnp.concatenate([key_grad, value_grad], axis=1), True, False)
+    attended_grad = dot(wire.step(cross_grad), w_co, 1, 0).astype(BF16)
+    cross_out_parts = weight_grad(cross_grad, attended)
+    query_grad, key_grad, value_grad = kernels.cross_back(lengths, cross_query, text_proj, wire.step(attended_grad))
+    query_grad = wire.step(query_grad)
+    cross_kv_parts = weight_grad(caption, jnp.concatenate([key_grad, value_grad], axis=1))
+    text_grads = scatter(wire, [cross_kv_parts], [cross_out_parts])
     resid_a_grad = resid_b_grad + core_total([(query_grad, w_cq, 1)])
-    cross_q_grad = weight_grad(cross_input, query_grad, False, False)
+    cross_q_parts = weight_grad(cross_input, query_grad)
     gate_a_grad = jnp.sum(resid_a_grad * self_term, axis=0)
-    self_grad = both((gate_a * resid_a_grad).astype(BF16))
+    self_grad = both((gate_a * wire.step(resid_a_grad)).astype(BF16))
     mixed_grad = dot(self_grad, w_so, 1, 0)
-    self_out_grad = weight_grad(self_grad, mixed, False, True)
-    q_low, state_grad = kernels.mix_back(queries, states, mixed_grad)
+    q_low, state_grad = kernels.mix_back(queries, states, wire.step(mixed_grad))
     state_grad = butterfly(state_grad, (SEQ,), jnp.add)
-    kv_low = kernels.states_back(keys_values, state_grad)
-    q_grad = weight_grad(normed, q_low, False, False)
-    kv_grad = weight_grad(normed, kv_low, True, True)
+    token_grads = scatter(wire, [cross_q_parts], [weight_grad(self_grad, mixed)])
+    q_parts = weight_grad(normed, q_low)
+    kv_low = kernels.states_back(keys_values, wire.step(state_grad))
+    kv_low = wire.step(kv_low)
+    qkv_grads = scatter(wire, [weight_grad(normed, kv_low)], [q_parts])
     normed_grad = core_total([(q_low, w_q, 1), (kv_low, w_kv, 1)])
     resid_part, shift_a_grad, scale_a_grad = normalise_back(resid_in, normed_grad, scale_a)
     latent_grad = resid_a_grad + resid_part
@@ -663,11 +874,17 @@
     mod_grad = lax.dot_general(
         mod_grad, pick.astype(F32), (((1,), (1,)), ((), ())), precision=lax.Precision.HIGHEST
     )
-    table_grad = butterfly(mod_grad, (TP, SEQ, DP), jnp.add)
-
-    head_count = heads_width // HEAD_DIM
-    head_peaks = jnp.max(peaks[:, :, : LANES // HEAD_DIM, 0], axis=0).reshape(-1)[:head_count]
-    head_peaks = butterfly(head_peaks, (SEQ, DP), jnp.maximum)
+    table_grads = []
+    wire.join(butterfly_phases(butterfly(mod_grad, (TP,), jnp.add), (SEQ, DP), jnp.add, table_grads))
+    wire.finish()
+    (table_grad,), (head_peaks,), (small,) = table_grads, head_peaks, small
+    down_grad = jnp.concatenate([down for _, down in ffn_grads], axis=1)
+    up_grad = jnp.concatenate(
+        [up[:, j * half : (j + 1) * half] for j in range(2) for up, _ in ffn_grads], axis=1
+    )
+    (cross_kv_grad, cross_out_grad), (cross_q_grad, self_out_grad) = text_grads, token_grads
+    kv_grad, q_grad = qkv_grads
+
     factor = jnp.repeat(jnp.sqrt(CLIP_TAU / jnp.maximum(head_peaks, CLIP_TAU)), HEAD_DIM)
 
     def cut(grad, count, each, size):

time: 3070 us -> 2070 us (0.67)
  waiting for transfers between devices: 1690 us -> 648 us
  local copies, waits for them, and re-layouts: 201 us -> 246 us
  starting transfers between devices: 210 us -> 169 us
  matrix products: 470 us -> 501 us
    ppermute x15 -> x3, waiting for transfers between devices: 548 us -> 2.44 us  [butterfly(): lax.ppermute(values, axis, [(i, i ^ bit) for i in range(size)])]
    ppermute x163 -> x125, waiting for transfers between devices: 1120 us -> 604 us  [shift(): lax.ppermute(values, axis, [(cycle[i], cycle[(i + step) % size]) for i in...]
    unnamed x376 -> x772, local copies, waits for them, and re-layouts: 97.5 us -> 151 us
    ppermute x163 -> x125, starting transfers between devices: 188 us -> 136 us  [shift(): lax.ppermute(values, axis, [(cycle[i], cycle[(i + step) % size]) for i in...]
    another operation x8 -> x9, other arithmetic: 39.4 us -> 3.6 us
    dot_general x44 -> x54, matrix products: 455 us -> 487 us  [dot(): lax.dot_general(left, right, (((left_dim,), (right_dim,)), ((), ())), pre...]
    convert_element_type x46 -> x36, other arithmetic: 67.3 us -> 58.4 us  [the longest x15 23.1 us: scatter_phases(): sends.append((back.astype(BF16), DP, -1))]
    pallas_call x1 -> x2, Pallas kernels: 61.9 us -> 63.1 us  [act_back(): call(functools.partial(act_back_kernel, self.cols), (self.micro, 2 * unit...]
  transfers between devices with their start and end apart: 196 -> 162, of which waited for: 89 -> 75; matrix products, arithmetic and copies ran while one was open for 26% -> 39% of each run, Pallas kernels for 8% -> 10%
where the time goes in v1:
time: 2070 us; the launch traced here: 2050 us
  waiting for transfers between devices  648 us (31%)
  matrix products  501 us (24%)
  Pallas kernels  312 us (15%)
  local copies, waits for them, and re-layouts  246 us (12%)
  other arithmetic  170 us (8%)
  starting transfers between devices  169 us (8%)
    ppermute x125, waiting for transfers between devices, shift(): lax.ppermute(values, axis, [(cycle[i], cycle[(i + step) % size]) for i in...  604 us
    dot_general x54, matrix products, dot(): lax.dot_general(left, right, (((left_dim,), (right_dim,)), ((), ())), pre...  487 us
    unnamed x772, local copies, waits for them, and re-layouts  151 us
    ppermute x125, starting transfers between devices, shift(): lax.ppermute(values, axis, [(cycle[i], cycle[(i + step) % size]) for i in...  136 us
    pallas_call x2, Pallas kernels, act_back(): call(functools.partial(act_back_kernel, self.cols), (self.micro, 2 * unit...  63.1 us
    pallas_call x1, Pallas kernels, cross_back(): call(cross_back_kernel, (self.micro, self.groups), [smem, self.tile(), se...  53.2 us
    pallas_call x2, Pallas kernels, conv_back(): call(functools.partial(conv_back_kernel, self.cols), (self.micro, self.un...  53.1 us
  transfers between devices with their start and end apart: 162, of which 75 were waited for; matrix products, arithmetic and copies ran while one was open for 39% of the time, Pallas kernels for 10%

profile of v1, /device:TPU:0, one launch (start us, length us, event | category | flops | bytes accessed | tf_op | source)
XLA Modules:
  0.0 2051.7 jit_solution(4473862417426795977)
XLA Ops:
  49.3 27.8 %collective-permute-done.3 = bf16[144,4608]{1,0:T(8,128)(2,1)} collective-permute-done((bf16[144,4608]{1,0:T(8,128)(2,1)S(1)}, bf16[144,4608]{1,0:T(8,128)(2,1)}, u32[]{:S(2)}, u32[]{:S(2)}) %collective-permute-start.3) | collective-permute-done | bytes 1327136 | tf_op jit(solution)/shard_map/ppermute | solution.py:63
  87.1 25.0 %collective-permute-done.6 = bf16[144,4608]{1,0:T(8,128)(2,1)} collective-permute-done((bf16[144,4608]{1,0:T(8,128)(2,1)}, bf16[144,4608]{1,0:T(8,128)(2,1)}, u32[]{:S(2)}, u32[]{:S(2)}) %collective-permute-start.6) | collective-permute-done | bytes 1327136 | tf_op jit(solution)/shard_map/ppermute | solution.py:63
  357.3 27.5 %collective-permute-done.35 = bf16[144,4608]{1,0:T(8,128)(2,1)S(1)} collective-permute-done((bf16[144,4608]{1,0:T(8,128)(2,1)S(1)}, bf16[144,4608]{1,0:T(8,128)(2,1)S(1)}, u32[]{:S(2)}, u32[]{:S(2)}) %collective-permute-start.35) | collective-permute-done | bytes 1327136 | tf_op jit(solution)/shard_map/ppermute | solution.py:63
  400.6 16.5 collective-permute-done.38
  509.5 34.4 %shard_map.273 = (bf16[1024,1152]{1,0:T(8,128)(2,1)S(1)}, f32[2,9,8,128]{3,2,1,0:T(8,128)S(1)}) custom-call(s32[2]{0:T(128)S(1)} %broadcast_select_fusion.length_ref, bf16[1024,1152]{1,0:T(8,128)(2,1)S(1)} %fusion.26.query_ref, bf16[608,2304]{1,0:T(8,128)(2,1)} %convolution_convert_fusion.20.key_ref.value_ref, ...), custom_call_target="tpu_custom_call" | custom-call | flops 23592960000 | bytes 7077888 | tf_op jit(solution)/shard_map/pallas_call | solution.py:607
  557.3 23.0 %collective-permute-done.53 = bf16[144,5632]{1,0:T(8,128)(2,1)S(1)} collective-permute-done((bf16[144,5632]{1,0:T(8,128)(2,1)S(1)}, bf16[144,5632]{1,0:T(8,128)(2,1)S(1)}, u32[]{:S(2)}, u32[]{:S(2)}) %collective-permute-start.53) | collective-permute-done | bytes 1622048 | tf_op jit(solution)/shard_map/ppermute | solution.py:63
  663.9 19.2 convolution_add_fusion.1.z0.z1.z_ref
  709.3 18.8 shard_map.274
  751.9 26.5 %shard_map.275 = (bf16[1024,1408]{1,0:T(8,128)(2,1)S(1)}, bf16[1024,1408]{1,0:T(8,128)(2,1)}, f32[2,24,1408]{2,1,0:T(8,128)S(1)}) custom-call(f32[1024,2816]{1,0:T(8,128)} %convolution_add_fusion.1.z0.z1.z_ref, f32[1024,2816]{1,0:T(8,128)} %convolution_add_fusion.1.z0.z1.z_ref, bf16[2,32,2816]{2,1,0:T(8,128)(2,1)S(1)} %collective-permute-done.62.top0.top1, ...), custom_call_target="tpu_custom_call" | custom-call | flops 57671680000 | bytes 23068672 | tf_op jit(solution)/shard_map/pallas_call | solution.py:655
  806.3 31.6 %shard_map.276 = (bf16[1024,2816]{1,0:T(8,128)(2,1)}, f32[2,8,2816]{2,1,0:T(8,128)S(1)}) custom-call(f32[1024,2816]{1,0:T(8,128)} %convolution_add_fusion.1.z0.z1.z_ref, bf16[1024,2816]{1,0:T(8,128)(2,1)} %copy-done.152, bf16[2,32,2816]{2,1,0:T(8,128)(2,1)S(1)} %collective-permute-done.76.top, bf16[2,32,2816]{2,1,0:T(8,128)(2,1)S(1)} %collective-permute-done.77.bottom, ...), custom_call_target="tpu_custom_call" | custom-call | flops 28835840000 | bytes 23068672 | tf_op jit(solution)/shard_map/pallas_call | solution.py:666
  931.6 19.2 shard_map.277
  999.2 26.6 %shard_map.278 = (bf16[1024,1408]{1,0:T(8,128)(2,1)S(1)}, bf16[1024,1408]{1,0:T(8,128)(2,1)}, f32[2,24,1408]{2,1,0:T(8,128)S(1)}) custom-call(f32[1024,2816]{1,0:T(8,128)} %convolution_add_fusion.z0.z1.z_ref, f32[1024,2816]{1,0:T(8,128)} %convolution_add_fusion.z0.z1.z_ref, bf16[2,32,2816]{2,1,0:T(8,128)(2,1)S(1)} %collective-permute-done.73.top0.top1, ...), custom_call_target="tpu_custom_call" | custom-call | flops 57671680000 | bytes 23068672 | tf_op jit(solution)/shard_map/pallas_call | solution.py:655
  1044.2 18.1 collective-permute-done.84.top
  1075.4 31.5 %shard_map.279 = (bf16[1024,2816]{1,0:T(8,128)(2,1)}, f32[2,8,2816]{2,1,0:T(8,128)S(1)}) custom-call(f32[1024,2816]{1,0:T(8,128)} %convolution_add_fusion.z0.z1.z_ref, bf16[1024,2816]{1,0:T(8,128)(2,1)} %copy-done.151, bf16[2,32,2816]{2,1,0:T(8,128)(2,1)S(1)} %collective-permute-done.84.top, bf16[2,32,2816]{2,1,0:T(8,128)(2,1)S(1)} %collective-permute-done.85.bottom, ...), custom_call_target="tpu_custom_call" | custom-call | flops 28835840000 | bytes 23068672 | tf_op jit(solution)/shard_map/pallas_call | solution.py:666
  1163.9 16.5 collective-permute-done.93
  1222.2 16.3 fusion.179
  1304.9 53.2 %shard_map.280 = (bf16[1024,1152]{1,0:T(8,128)(2,1)S(1)}, bf16[608,1152]{1,0:T(8,128)(2,1)S(1)}, bf16[608,1152]{1,0:T(8,128)(2,1)S(1)}) custom-call(s32[2]{0:T(128)S(1)} %copy-done.11, bf16[1024,1152]{1,0:T(8,128)(2,1)} %copy-done.14, bf16[608,2304]{1,0:T(8,128)(2,1)} %convolution_convert_fusion.20.key_ref.value_ref, ...), custom_call_target="tpu_custom_call" | custom-call | flops 58982400000 | bytes 7077888 | tf_op jit(solution)/shard_map/pallas_call | solution.py:618
  1437.0 20.4 collective-permute-done.114
  1474.7 23.4 %collective-permute-done.117 = bf16[288,2304]{1,0:T(8,128)(2,1)S(1)} collective-permute-done((bf16[288,2304]{1,0:T(8,128)(2,1)S(1)}, bf16[288,2304]{1,0:T(8,128)(2,1)S(1)}, u32[]{:S(2)}, u32[]{:S(2)}) %collective-permute-start.117) | collective-permute-done | bytes 1327136 | tf_op jit(solution)/shard_map/ppermute | solution.py:63
  1522.4 19.1 collective-permute-done.122
  1570.5 18.0 shard_map.281
  1609.2 25.5 %shard_map.282 = bf16[1024,2304]{1,0:T(8,128)(2,1)S(1)} custom-call(f32[1024,2304]{1,0:T(8,128)} %fusion.178.key_ref.value_ref, f32[1024,2304]{1,0:T(8,128)} %fusion.178.key_ref.value_ref, f32[2,9,40,128]{3,2,1,0:T(8,128)S(1)} %add.752.state_ref), custom_call_target="tpu_custom_call" | custom-call | flops 1769472000 | bytes 23592960 | tf_op jit(solution)/shard_map/pallas_call | solution.py:593
  1740.6 19.9 collective-permute-done.133
  1938.6 16.4 collective-permute-done.156
  (1444 shorter events, 1471.8 us)
Async XLA Ops:
  25.8 126.1 %collective-permute-start = (bf16[512,2304]{1,0:T(8,128)(2,1)S(1)}, bf16[512,2304]{1,0:T(8,128)(2,1)}, u32[]{:S(2)}, u32[]{:S(2)}) collective-permute-start(bf16[512,2304]{1,0:T(8,128)(2,1)S(1)} %add_convert_fusion.2), channel_id=1, source_target_pairs={{0,1},{1,0},{2,3},{3,2},{4,5},{5,4},{6,7},{7,6},{8,9},{9,8},{10,11... | collective-permute-start | bytes 7077896 | tf_op jit(solution)/shard_map/ppermute | solution.py:317
  36.5 598.0 %collective-permute-start.75 = (bf16[512,2304]{1,0:T(8,128)(2,1)}, bf16[512,2304]{1,0:T(8,128)(2,1)}, u32[]{:S(2)}, u32[]{:S(2)}) collective-permute-start(bf16[512,2304]{1,0:T(8,128)(2,1)} %get-tuple-element.619), channel_id=1, source_target_pairs={{0,1},{1,0},{2,3},{3,2},{4,5},{5,4},{6,7},{7,6},{8,9},{9,8},{10,11... | collective-permute-start | bytes 7077896 | tf_op jit(solution)/shard_map/ppermute | solution.py:317
  291.1 60.2 %collective-permute-start.31 = (bf16[144,4608]{1,0:T(8,128)(2,1)}, bf16[144,4608]{1,0:T(8,128)(2,1)S(1)}, u32[]{:S(2)}, u32[]{:S(2)}) collective-permute-start(bf16[144,4608]{1,0:T(8,128)(2,1)} %pad_maximum_fusion.35), channel_id=1, source_target_pairs={{0,8},{8,16},{16,24},{24,28},{28,20},{20,12},{12,4},{4,0},{1,9},{9... | collective-permute-start | bytes 3981320 | tf_op jit(solution)/shard_map/ppermute | solution.py:63
  293.1 58.2 %collective-permute-start.32 = (bf16[144,4608]{1,0:T(8,128)(2,1)}, bf16[144,4608]{1,0:T(8,128)(2,1)S(1)}, u32[]{:S(2)}, u32[]{:S(2)}) collective-permute-start(bf16[144,4608]{1,0:T(8,128)(2,1)} %pad_maximum_fusion.35), channel_id=1, source_target_pairs={{0,4},{8,0},{16,8},{24,16},{28,24},{20,28},{12,20},{4,12},{1,5},{9... | collective-permute-start | bytes 3981320 | tf_op jit(solution)/shard_map/ppermute | solution.py:63
  293.1 56.4 %collective-permute-start.30 = (bf16[144,1152]{1,0:T(8,128)(2,1)S(1)}, bf16[144,1152]{1,0:T(8,128)(2,1)}, u32[]{:S(2)}, u32[]{:S(2)}) collective-permute-start(bf16[144,1152]{1,0:T(8,128)(2,1)S(1)} %get-tuple-element.223), channel_id=1, source_target_pairs={{0,2},{2,0},{1,3},{3,1},{4,6},{6,4},{5,7},{7,5},{8,10},{10,8},{9,1... | collective-permute-start | bytes 995336 | tf_op jit(solution)/shard_map/ppermute | solution.py:63
  293.6 57.8 %collective-permute-start.33 = (bf16[144,2304]{1,0:T(8,128)(2,1)S(1)}, bf16[144,2304]{1,0:T(8,128)(2,1)}, u32[]{:S(2)}, u32[]{:S(2)}) collective-permute-start(bf16[144,2304]{1,0:T(8,128)(2,1)S(1)} %copy-done.114), channel_id=1, source_target_pairs={{0,2},{2,0},{1,3},{3,1},{4,6},{6,4},{5,7},{7,5},{8,10},{10,8},{9,1... | collective-permute-start | bytes 1990664 | tf_op jit(solution)/shard_map/ppermute | solution.py:63
  396.4 44.0 %collective-permute-start.27 = (bf16[512,2304]{1,0:T(8,128)(2,1)}, bf16[512,2304]{1,0:T(8,128)(2,1)}, u32[]{:S(2)}, u32[]{:S(2)}) collective-permute-start(bf16[512,2304]{1,0:T(8,128)(2,1)} %get-tuple-element.615), channel_id=1, source_target_pairs={{0,1},{1,0},{2,3},{3,2},{4,5},{5,4},{6,7},{7,6},{8,9},{9,8},{10,11... | collective-permute-start | bytes 7077896 | tf_op jit(solution)/shard_map/ppermute | solution.py:317
  607.2 49.7 %collective-permute-start.51 = (bf16[512,2304]{1,0:T(8,128)(2,1)S(1)}, bf16[512,2304]{1,0:T(8,128)(2,1)S(1)}, u32[]{:S(2)}, u32[]{:S(2)}) collective-permute-start(bf16[512,2304]{1,0:T(8,128)(2,1)S(1)} %add_convert_fusion.1), channel_id=1, source_target_pairs={{0,1},{1,0},{2,3},{3,2},{4,5},{5,4},{6,7},{7,6},{8,9},{9,8},{10,11... | collective-permute-start | bytes 7077896 | tf_op jit(solution)/shard_map/ppermute | solution.py:317
  702.7 43.3 %collective-permute-start.67 = (bf16[144,5632]{1,0:T(8,128)(2,1)S(1)}, bf16[144,5632]{1,0:T(8,128)(2,1)}, u32[]{:S(2)}, u32[]{:S(2)}) collective-permute-start(bf16[144,5632]{1,0:T(8,128)(2,1)S(1)} %collective-permute-done.64), channel_id=1, source_target_pairs={{0,8},{8,16},{16,24},{24,28},{28,20},{20,12},{12,4},{4,0},{1,9},{9... | collective-permute-start | bytes 4866056 | tf_op jit(solution)/shard_map/ppermute | solution.py:63
  704.6 41.3 %collective-permute-start.68 = (bf16[144,5632]{1,0:T(8,128)(2,1)S(1)}, bf16[144,5632]{1,0:T(8,128)(2,1)S(1)}, u32[]{:S(2)}, u32[]{:S(2)}) collective-permute-start(bf16[144,5632]{1,0:T(8,128)(2,1)S(1)} %collective-permute-done.65), channel_id=1, source_target_pairs={{0,4},{8,0},{16,8},{24,16},{28,24},{20,28},{12,20},{4,12},{1,5},{9... | collective-permute-start | bytes 4866056 | tf_op jit(solution)/shard_map/ppermute | solution.py:63
  704.7 44.3 %collective-permute-start.69 = (bf16[288,2816]{1,0:T(8,128)(2,1)}, bf16[288,2816]{1,0:T(8,128)(2,1)}, u32[]{:S(2)}, u32[]{:S(2)}) collective-permute-start(bf16[288,2816]{1,0:T(8,128)(2,1)} %pad_maximum_fusion.23), channel_id=1, source_target_pairs={{0,2},{2,0},{1,3},{3,1},{4,6},{6,4},{5,7},{7,5},{8,10},{10,8},{9,1... | collective-permute-start | bytes 4866056 | tf_op jit(solution)/shard_map/ppermute | solution.py:63
  789.1 79.5 %collective-permute-start.72 = (bf16[144,2816]{1,0:T(8,128)(2,1)}, bf16[144,2816]{1,0:T(8,128)(2,1)}, u32[]{:S(2)}, u32[]{:S(2)}) collective-permute-start(bf16[144,2816]{1,0:T(8,128)(2,1)} %get-tuple-element.268), channel_id=1, source_target_pairs={{0,2},{2,0},{1,3},{3,1},{4,6},{6,4},{5,7},{7,5},{8,10},{10,8},{9,1... | collective-permute-start | bytes 2433032 | tf_op jit(solution)/shard_map/ppermute | solution.py:63
  1062.3 159.8 %collective-permute-start.79 = (bf16[512,2304]{1,0:T(8,128)(2,1)}, bf16[512,2304]{1,0:T(8,128)(2,1)}, u32[]{:S(2)}, u32[]{:S(2)}) collective-permute-start(bf16[512,2304]{1,0:T(8,128)(2,1)} %fusion.20), channel_id=1, source_target_pairs={{0,1},{1,0},{2,3},{3,2},{4,5},{5,4},{6,7},{7,6},{8,9},{9,8},{10,11... | collective-permute-start | bytes 7077896 | tf_op jit(solution)/shard_map/ppermute | solution.py:317
  1138.0 64.6 %collective-permute-start.92 = (bf16[512,2304]{1,0:T(8,128)(2,1)}, bf16[512,2304]{1,0:T(8,128)(2,1)S(1)}, u32[]{:S(2)}, u32[]{:S(2)}) collective-permute-start(bf16[512,2304]{1,0:T(8,128)(2,1)} %fusion.21), channel_id=1, source_target_pairs={{0,1},{1,0},{2,3},{3,2},{4,5},{5,4},{6,7},{7,6},{8,9},{9,8},{10,11... | collective-permute-start | bytes 7077896 | tf_op jit(solution)/shard_map/ppermute | solution.py:317
  1199.0 56.3 %collective-permute-start.95 = (bf16[144,1408]{1,0:T(8,128)(2,1)}, bf16[144,1408]{1,0:T(8,128)(2,1)}, u32[]{:S(2)}, u32[]{:S(2)}) collective-permute-start(bf16[144,1408]{1,0:T(8,128)(2,1)} %slice.2671), channel_id=1, source_target_pairs={{0,2},{2,0},{1,3},{3,1},{4,6},{6,4},{5,7},{7,5},{8,10},{10,8},{9,1... | collective-permute-start | bytes 1216520 | tf_op jit(solution)/shard_map/ppermute | solution.py:63
  1202.3 48.0 %collective-permute-start.98 = (bf16[288,2816]{1,0:T(8,128)(2,1)}, bf16[288,2816]{1,0:T(8,128)(2,1)}, u32[]{:S(2)}, u32[]{:S(2)}) collective-permute-start(bf16[288,2816]{1,0:T(8,128)(2,1)} %get-tuple-element.307), channel_id=1, source_target_pairs={{0,2},{2,0},{1,3},{3,1},{4,6},{6,4},{5,7},{7,5},{8,10},{10,8},{9,1... | collective-permute-start | bytes 4866056 | tf_op jit(solution)/shard_map/ppermute | solution.py:63
  1412.6 97.6 %collective-permute-start.109 = (bf16[512,2304]{1,0:T(8,128)(2,1)}, bf16[512,2304]{1,0:T(8,128)(2,1)}, u32[]{:S(2)}, u32[]{:S(2)}) collective-permute-start(bf16[512,2304]{1,0:T(8,128)(2,1)} %convolution_convert_fusion.21), channel_id=1, source_target_pairs={{0,1},{1,0},{2,3},{3,2},{4,5},{5,4},{6,7},{7,6},{8,9},{9,8},{10,11... | collective-permute-start | bytes 7077896 | tf_op jit(solution)/shard_map/ppermute | solution.py:317
  1420.1 42.0 %collective-permute-start.112 = (bf16[144,5632]{1,0:T(8,128)(2,1)}, bf16[144,5632]{1,0:T(8,128)(2,1)}, u32[]{:S(2)}, u32[]{:S(2)}) collective-permute-start(bf16[144,5632]{1,0:T(8,128)(2,1)} %fusion.38), channel_id=1, source_target_pairs={{0,4},{8,0},{16,8},{24,16},{28,24},{20,28},{12,20},{4,12},{1,5},{9... | collective-permute-start | bytes 4866056 | tf_op jit(solution)/shard_map/ppermute | solution.py:63
  1553.9 80.8 %collective-permute-start.123 = (bf16[144,4608]{1,0:T(8,128)(2,1)}, bf16[144,4608]{1,0:T(8,128)(2,1)S(1)}, u32[]{:S(2)}, u32[]{:S(2)}) collective-permute-start(bf16[144,4608]{1,0:T(8,128)(2,1)} %fusion.52), channel_id=1, source_target_pairs={{0,4},{8,0},{16,8},{24,16},{28,24},{20,28},{12,20},{4,12},{1,5},{9... | collective-permute-start | bytes 3981320 | tf_op jit(solution)/shard_map/ppermute | solution.py:63
  1555.0 79.8 %collective-permute-start.124 = (bf16[144,4608]{1,0:T(8,128)(2,1)}, bf16[144,4608]{1,0:T(8,128)(2,1)S(1)}, u32[]{:S(2)}, u32[]{:S(2)}) collective-permute-start(bf16[144,4608]{1,0:T(8,128)(2,1)} %fusion.53), channel_id=1, source_target_pairs={{0,8},{8,16},{16,24},{24,28},{28,20},{20,12},{12,4},{4,0},{1,9},{9... | collective-permute-start | bytes 3981320 | tf_op jit(solution)/shard_map/ppermute | solution.py:63
  1555.9 78.8 %collective-permute-start.125 = (bf16[288,2304]{1,0:T(8,128)(2,1)}, bf16[288,2304]{1,0:T(8,128)(2,1)}, u32[]{:S(2)}, u32[]{:S(2)}) collective-permute-start(bf16[288,2304]{1,0:T(8,128)(2,1)} %get-tuple-element.342), channel_id=1, source_target_pairs={{0,2},{2,0},{1,3},{3,1},{4,6},{6,4},{5,7},{7,5},{8,10},{10,8},{9,1... | collective-permute-start | bytes 3981320 | tf_op jit(solution)/shard_map/ppermute | solution.py:63
  1660.9 58.7 %collective-permute-start.129 = (bf16[144,4608]{1,0:T(8,128)(2,1)}, bf16[144,4608]{1,0:T(8,128)(2,1)}, u32[]{:S(2)}, u32[]{:S(2)}) collective-permute-start(bf16[144,4608]{1,0:T(8,128)(2,1)} %fusion.54), channel_id=1, source_target_pairs={{0,4},{8,0},{16,8},{24,16},{28,24},{20,28},{12,20},{4,12},{1,5},{9... | collective-permute-start | bytes 3981320 | tf_op jit(solution)/shard_map/ppermute | solution.py:63
  1661.9 59.5 %collective-permute-start.131 = (bf16[144,4608]{1,0:T(8,128)(2,1)}, bf16[144,4608]{1,0:T(8,128)(2,1)}, u32[]{:S(2)}, u32[]{:S(2)}) collective-permute-start(bf16[144,4608]{1,0:T(8,128)(2,1)} %fusion.55), channel_id=1, source_target_pairs={{0,8},{8,16},{16,24},{24,28},{28,20},{20,12},{12,4},{4,0},{1,9},{9... | collective-permute-start | bytes 3981320 | tf_op jit(solution)/shard_map/ppermute | solution.py:63
  1923.4 88.7 %collective-permute-start.127 = (f32[512,2240]{0,1:T(8,128)}, f32[512,2240]{0,1:T(8,128)}, u32[]{:S(2)}, u32[]{:S(2)}) collective-permute-start(f32[512,2240]{0,1:T(8,128)} %fusion.16), channel_id=1, source_target_pairs={{0,1},{1,0},{2,3},{3,2},{4,5},{5,4},{6,7},{7,6},{8,9},{9,8},{10,11... | collective-permute-start | bytes 13762568 | tf_op jit(solution)/shard_map/ppermute | solution.py:317
  (453 other events, 8898.5 us)

commit v2 on v1

--- a/solution.py
+++ b/solution.py
@@ -63,34 +63,6 @@
     return lax.ppermute(values, axis, [(cycle[i], cycle[(i + step) % size]) for i in range(size)])
 
 
-def ring_gather(own, axis, flip):
-    size = lax.axis_size(axis)
-    pieces = [own] + [None] * (size - 1)
-    ahead = size // 2 if not flip else size - 1 - size // 2
-    for a in range(1, ahead + 1):
-        pieces[a] = shift(pieces[a - 1], axis, 1)
-    for a in range(size - 1, ahead, -1):
-        pieces[a] = shift(pieces[(a + 1) % size], axis, -1)
-    return pieces
-
-
-def ring_scatter(blocks, axis, flip):
-    size = lax.axis_size(axis)
-    ahead = size // 2 if not flip else size - 1 - size // 2
-    total = blocks[0]().astype(F32)
-    if ahead > 0:
-        running = blocks[ahead]().astype(BF16)
-        for a in range(ahead - 1, 0, -1):
-            running = (shift(running, axis, -1).astype(F32) + blocks[a]()).astype(BF16)
-        total = total + shift(running, axis, -1).astype(F32)
-    if ahead < size - 1:
-        running = blocks[ahead + 1]().astype(BF16)
-        for a in range(ahead + 2, size):
-            running = (shift(running, axis, 1).astype(F32) + blocks[a]()).astype(BF16)
-        total = total + shift(running, axis, 1).astype(F32)
-    return total
-
-
 def slot_order(size):
     ahead = size // 2
     order = []
@@ -101,25 +73,30 @@
     return order + [0]
 
 
-def in_slots(pieces):
-    return [pieces[a] for a in slot_order(len(pieces))]
+def chip_back(back_dp, back_seq):
+    dp_size, seq_size = lax.axis_size(DP), lax.axis_size(SEQ)
+    from_dp = ring_member(DP, (ring_place(DP) - back_dp) % dp_size)
+    return from_dp * seq_size + (lax.axis_index(SEQ) - back_seq) % seq_size
 
 
 class Wire:
     def __init__(self):
-        self.running, self.queue, self.last = [], [], ()
+        self.running, self.queue, self.last, self.before, self.patient = [], [], (), (), False
         self.stride, self.since = lax.axis_size(DP) // 2, lax.axis_size(DP)
 
     def join(self, phases):
         self.running.append((phases, next(phases)))
 
-    def push(self, phases):
-        self.queue.append(phases)
-
-    def round(self):
+    def push(self, phases, patient):
+        self.queue.append((phases, patient))
+
+    def round(self, hurry=False):
         if self.queue and self.since >= self.stride:
-            self.join(self.queue.pop(0))
+            phases, self.patient = self.queue.pop(0)
+            self.join(phases)
             self.since = 0
+        elif self.patient and self.since >= self.stride and not hurry:
+            return
         if not self.running:
             return
         self.since += 1
@@ -128,7 +105,7 @@
         if self.last:
             values, _ = lax.optimization_barrier((values, self.last))
         arrived = tuple(shift(value, axis, step) for value, (_, axis, step) in zip(values, sends))
-        self.last = arrived
+        self.before, self.last = self.last, arrived
         running, at = [], 0
         for phases, pending in self.running:
             mine = arrived[at : at + len(pending)]
@@ -139,19 +116,22 @@
                 pass
         self.running = running
 
-    def step(self, value):
-        before = self.last
+    def after(self, value):
+        return lax.optimization_barrier((value, self.last))[0] if self.last else value
+
+    def step(self, value, slack=False):
+        value = lax.optimization_barrier((value, self.before))[0] if slack else self.after(value)
         self.round()
-        return lax.optimization_barrier((value, before))[0] if before else value
+        return value
 
     def need(self, done):
         while not done:
-            self.round()
+            self.round(True)
         return done
 
     def finish(self):
         while self.running or self.queue:
-            self.round()
+            self.round(True)
 
 
 def butterfly_phases(values, axes, combine, done):
@@ -196,74 +176,141 @@
         sends.append((jnp.concatenate(across, axis=0) if len(across) > 1 else across[0], SEQ, 1))
         arrived = yield sends
         for i, a in enumerate(fresh):
-            far[a] = arrived[-1][i * rows : (i + 1) * rows]
+            far[a] = (arrived[-1], i * rows)
         for a, piece in zip(places, arrived):
             pieces[a] = piece
         fresh = places
-    full = []
+    arrays, moves = [], []
+
+    def source(array):
+        for place, known in enumerate(arrays):
+            if known is array:
+                return place
+        arrays.append(array)
+        return len(arrays) - 1
+
+    for a in range(size):
+        near, (across, start) = source(pieces[a]), far[a]
+        across = source(across)
+        at = 0
+        for weight, width in enumerate(widths_a):
+            moves.append((weight, a, near, 0, at, width))
+            moves.append((weight, size + a, across, start, at, width))
+            at += width
+        for weight, width in enumerate(widths_b):
+            moves.append((len(widths_a) + weight, a, near, 0, at, width))
+            moves.append((len(widths_a) + weight, size + a, near, 0, at + n_b, width))
+            at += width
+    place = jnp.stack([chip_back(a, b).astype(jnp.int32) for b in range(2) for a in range(size)])
+    done.extend(assemble(place, arrays, moves, rows, widths_a + widths_b))
+
+
+def assemble_kernel(moves, rows, count, place_ref, *refs):
+    sources, outs = refs[:count], refs[count:]
+    for slot in range(place_ref.shape[0]):
+
+        @pl.when(pl.program_id(0) == slot)
+        def _(slot=slot):
+            for weight, to, array, start, at, width in moves:
+                if to == slot:
+                    outs[weight][...] = sources[array][start : start + rows, at : at + width]
+
+
+def assemble(place, arrays, moves, rows, widths):
+    slots = place.shape[0]
+    return pl.pallas_call(
+        functools.partial(assemble_kernel, moves, rows, len(arrays)),
+        grid_spec=pltpu.PrefetchScalarGridSpec(
+            num_scalar_prefetch=1,
+            grid=(slots,),
+            in_specs=[
+                pl.BlockSpec(array.shape, lambda i, place_ref: (0, 0), pipeline_mode=pl.Buffered(1)) for array in arrays
+            ],
+            out_specs=[pl.BlockSpec((rows, width), lambda i, place_ref: (place_ref[i], 0)) for width in widths],
+        ),
+        out_shape=[struct((slots * rows, width), BF16) for width in widths],
+        compiler_params=pltpu.CompilerParams(vmem_limit_bytes=VMEM_LIMIT),
+        cost_estimate=pl.CostEstimate(flops=0, bytes_accessed=slots * rows * sum(widths) * 4, transcendentals=0),
+    )(place, *arrays)
+
+
+def gather(wire, first, second, gate=None):
+    done = []
+    if wire is not None and lax.axis_size(SEQ) == 2:
+        wire.push(gather_phases(first, second, done), False)
+    else:
+        shard = jnp.concatenate(first + second, axis=1)
+        if gate is not None:
+            shard, _ = lax.optimization_barrier((shard, gate))
+        full = lax.all_gather(shard, (DP, SEQ), axis=0, tiled=False).reshape(-1, shard.shape[1])
+        done.extend(columns(full, [w.shape[1] for w in first + second]))
+    return done
+
+
+def combine_kernel(near_count, flat_count, index_ref, *refs):
+    near, flat, far = refs[:near_count], refs[near_count : near_count + flat_count], refs[near_count + flat_count]
+    running, out = refs[near_count + flat_count + 1 : -1], refs[-1]
     at = 0
-    for width in widths_a:
-        blocks = [p[:, at : at + width] for p in in_slots(pieces)] + [p[:, at : at + width] for p in in_slots(far)]
-        full.append(jnp.concatenate(blocks, axis=0))
+    for place, ref in enumerate(near + flat):
+        width = ref.shape[1]
+        part = ref[...].astype(F32)
+        if place < near_count:
+            part = part + far[:, at : at + width].astype(F32)
+        for other in running:
+            part = part + other[:, at : at + width].astype(F32)
+        out[:, at : at + width] = part.astype(out.dtype)
         at += width
-    for width in widths_b:
-        blocks = [p[:, at : at + width] for p in in_slots(pieces)]
-        blocks += [p[:, at + n_b : at + n_b + width] for p in in_slots(pieces)]
-        full.append(jnp.concatenate(blocks, axis=0))
-        at += width
-    done.extend(full)
-
-
-def gather_slow(shard):
-    near = jnp.concatenate(in_slots(ring_gather(shard, DP, False)), axis=0)
-    return jnp.concatenate(ring_gather(near, SEQ, False), axis=0)
-
-
-def gather(wire, first, second):
-    done = []
-    if lax.axis_size(SEQ) == 2:
-        wire.push(gather_phases(first, second, done))
-    else:
-        done.extend(gather_slow(shard) for shard in first + second)
-    return done
-
-
-def scatter_slow(parts):
-    dp_size = lax.axis_size(DP)
-    order = slot_order(dp_size)
-    parts = [part.reshape(dp_size, part.shape[0] // dp_size, part.shape[1]) for part in parts]
-    near = ring_scatter([lambda b=b: parts[b].astype(F32) for b in range(len(parts))], SEQ, False)
-    return ring_scatter([lambda a=a: near[order.index(a)] for a in range(dp_size)], DP, False)
+
+
+def combine(blocks, near_count, far, running, rows, dtype):
+    steps = 3 if rows % 48 == 0 else 1
+    size = rows // steps
+    width = sum(array.shape[1] for array, _ in blocks)
+    sources = blocks + [far] + [(array, 0) for array in running]
+    index = jnp.stack([jnp.asarray(at, jnp.int32) for _, at in sources])
+
+    def spec(place, array):
+        return pl.BlockSpec((size, array.shape[1]), lambda i, index_ref: (index_ref[place] * steps + i, 0))
+
+    return pl.pallas_call(
+        functools.partial(combine_kernel, near_count, len(blocks) - near_count),
+        grid_spec=pltpu.PrefetchScalarGridSpec(
+            num_scalar_prefetch=1,
+            grid=(steps,),
+            in_specs=[spec(place, array) for place, (array, _) in enumerate(sources)],
+            out_specs=pl.BlockSpec((size, width), lambda i, index_ref: (i, 0)),
+        ),
+        out_shape=struct((rows, width), dtype),
+        compiler_params=pltpu.CompilerParams(vmem_limit_bytes=VMEM_LIMIT),
+        cost_estimate=pl.CostEstimate(flops=rows * width * 4, bytes_accessed=rows * width * 10, transcendentals=0),
+    )(index, *[array for array, _ in sources])
 
 
 def scatter_phases(first, second, done):
     size = lax.axis_size(DP)
     ahead = size // 2
     order = slot_order(size)
-    rows = first[0][0].shape[0] // size
-    widths = [parts[0].shape[1] for parts in first + second]
-    n_a = sum(parts[0].shape[1] for parts in first)
-    n_b = sum(parts[0].shape[1] for parts in second)
-
-    def block(array, start, count=1):
-        return array[start * rows : (start + count) * rows]
+    rows = first[0].shape[0] // (2 * size)
+    widths = [part.shape[1] for part in first + second]
+    n_a = sum(part.shape[1] for part in first)
+    n_b = sum(part.shape[1] for part in second)
 
     def across(start, count):
-        blocks = [block(parts[1], start, count) for parts in first]
-        return (jnp.concatenate(blocks, axis=1) if len(blocks) > 1 else blocks[0], SEQ, 1)
-
-    def value(a, far):
-        slot = order.index(a)
-        near = [block(parts[0], slot) for parts in first]
-        near = jnp.concatenate(near, axis=1) if len(near) > 1 else near[0]
-        terms = [near.astype(F32) + far[a].astype(F32)]
-        for b in range(2):
-            terms += [block(parts[b], slot).astype(F32) for parts in second]
-        return jnp.concatenate(terms, axis=1)
+        blocks = [
+            [lax.dynamic_slice_in_dim(part, chip_back(order[start + i], 1) * rows, rows, 0) for part in first]
+            for i in range(count)
+        ]
+        blocks = [jnp.concatenate(each, axis=1) if len(each) > 1 else each[0] for each in blocks]
+        return (jnp.concatenate(blocks, axis=0) if count > 1 else blocks[0], SEQ, 1)
+
+    def value(a, far, running, dtype):
+        blocks = [(part, chip_back(a, 0)) for part in first]
+        blocks += [(part, chip_back(a, b)) for b in range(2) for part in second]
+        return combine(blocks, len(first), far[a], running, rows, dtype)
 
     def take(far, arrived, start):
         for i in range(arrived.shape[0] // rows):
-            far[order[start + i]] = arrived[i * rows : (i + 1) * rows]
+            far[order[start + i]] = (arrived, i)
 
     far = {}
     (arrived,) = yield [across(0, 2)]
@@ -271,14 +318,12 @@
     back = forth = None
     for step in range(ahead):
         sends = []
-        here = value(ahead - step, far)
-        back = here if back is None else back.astype(F32) + here
-        sends.append((back.astype(BF16), DP, -1))
+        back = value(ahead - step, far, [] if back is None else [back], BF16)
+        sends.append((back, DP, -1))
         place = ahead + 1 + step
         if place < size:
-            here = value(place, far)
-            forth = here if forth is None else forth.astype(F32) + here
-            sends.append((forth.astype(BF16), DP, 1))
+            forth = value(place, far, [] if forth is None else [forth], BF16)
+            sends.append((forth, DP, 1))
         start = 2 * step + 2
         if start < size:
             sends.append(across(start, min(2, size - start)))
@@ -288,7 +333,7 @@
             forth = arrived[1]
         if start < size:
             take(far, arrived[-1], start)
-    total = value(0, far) + back.astype(F32) + forth.astype(F32)
+    total = value(0, far, [back, forth], F32)
     (other,) = yield [(total[:, n_a + n_b :].astype(BF16), SEQ, 1)]
     mine = total[:, n_a : n_a + n_b] + other.astype(F32)
     done.extend(columns(total[:, :n_a], widths[: len(first)]) + columns(mine, widths[len(first) :]))
@@ -296,10 +341,14 @@
 
 def scatter(wire, first, second):
     done = []
-    if lax.axis_size(SEQ) == 2:
-        wire.push(scatter_phases(first, second, done))
+    if wire is not None and lax.axis_size(SEQ) == 2:
+        wire.push(scatter_phases(first, second, done), True)
     else:
-        done.extend(scatter_slow(parts) for parts in first + second)
+        parts = jnp.concatenate(first + second, axis=1)
+        devices = lax.axis_size(DP) * lax.axis_size(SEQ)
+        parts = parts.reshape(devices, parts.shape[0] // devices, parts.shape[1])
+        total = lax.psum_scatter(parts, (DP, SEQ), scatter_dimension=0, tiled=False)
+        done.extend(columns(total.astype(F32), [w.shape[1] for w in first + second]))
     return done
 
 
@@ -520,15 +569,18 @@
     small_ref[0, 20:24] = jnp.zeros((4, LANES), F32)
 
 
-def act_back_kernel(cols, z_ref, grad_ref, top, bottom, w_ref, out_ref, bias_ref, scratch):
-    tokens = z_ref.shape[0]
-    stage_columns(scratch, top[0], grad_ref[...].astype(F32), bottom[0], cols)
-    total = jnp.zeros((8, LANES), F32)
-    for at, size in strips_of(tokens, cols):
-        part = taps(scratch, w_ref[0], at, size, cols, True) * silu_slope(z_ref[at : at + size])
-        out_ref[at : at + size] = part.astype(BF16)
-        total = total + jnp.sum(part.reshape(size // 8, 8, LANES), axis=0)
-    bias_ref[0] = jnp.broadcast_to(jnp.sum(total, axis=0, keepdims=True), (8, LANES))
+def act_back_kernel(cols, z0, z1, grad0, grad1, top0, top1, bottom0, bottom1, w_ref, out0, out1, bias_ref, s0, s1):
+    tokens = z0.shape[0]
+    for grad, top, bottom, scratch in ((grad0, top0, bottom0, s0), (grad1, top1, bottom1, s1)):
+        stage_columns(scratch, top[0], grad[...].astype(F32), bottom[0], cols)
+    for j, (z, scratch, out) in enumerate(((z0, s0, out0), (z1, s1, out1))):
+        total = jnp.zeros((8, LANES), F32)
+        for at, size in strips_of(tokens, cols):
+            part = taps(scratch, w_ref[j], at, size, cols, True) * silu_slope(z[at : at + size])
+            out[at : at + size] = part.astype(BF16)
+            total = total + jnp.sum(part.reshape(size // 8, 8, LANES), axis=0)
+        bias_ref[0, j : j + 1] = jnp.sum(total, axis=0, keepdims=True)
+    bias_ref[0, 2:8] = jnp.zeros((6, LANES), F32)
 
 
 def call(kernel, grid, in_specs, out_specs, out_shape, flops, moved, scratch=(), **extra):
@@ -660,19 +712,17 @@
             [self.scratch(), self.scratch()],
         )(pre, pre, top, top, bottom, bottom, grad, conv_w, conv_b)
 
-    def act_back(self, pre, grad, top, bottom, conv_w):
+    def act_back(self, pre, grads, tops, bottoms, conv_w):
         size = self.micro * self.tokens * self.hidden
-        units = self.units
+        data, weights = self.conv_specs()
+        one = struct((pre.shape[0], self.hidden), BF16)
         return call(
-            functools.partial(act_back_kernel, self.cols), (self.micro, 2 * units),
-            [
-                self.tile(), self.tile(), self.edge(), self.edge(),
-                pl.BlockSpec((1, 9, LANES), lambda m, g: (g // units, 0, g % units)),
-            ],
-            [self.tile(), pl.BlockSpec((1, 8, LANES), lambda m, g: (m, 0, g))],
-            [struct(pre.shape, BF16), struct((self.micro, 8, pre.shape[1]), F32)], size * 20000, size * 16,
-            [self.scratch()],
-        )(pre, grad, top, bottom, conv_w)
+            functools.partial(act_back_kernel, self.cols), (self.micro, self.units),
+            data[:2] + [self.tile(), self.tile()] + [self.edge()] * 4 + weights[:1],
+            [self.tile(), self.tile(), pl.BlockSpec((1, 8, LANES), lambda m, g: (m, 0, g))],
+            [one, one, struct((self.micro, 8, self.hidden), F32)], size * 40000, size * 20,
+            [self.scratch(), self.scratch()],
+        )(pre, pre, *grads, *tops, *bottoms, conv_w)
 
 
 def pad_to(values, *sizes):
@@ -703,8 +753,7 @@
     width, hidden, slots = up_to(heads_width, LANES), up_to(hidden_width, 2 * LANES), up_to(text_len, 16)
     rows = up_to(own_rows, 16)
     dp_size, seq_size = lax.axis_size(DP), lax.axis_size(SEQ)
-    near = dp_size * rows
-    wide = seq_size * near
+    wide = dp_size * seq_size * rows
     core = lax.axis_index(TP)
     kernels = Kernels(micro, tokens, cols, width, hidden // 2, slots)
 
@@ -724,16 +773,12 @@
     qkv_rows = gather(wire, [heads_rows(self_qkv[1], self_qkv[2])], [heads_rows(self_qkv[0])])
     token_rows = gather(wire, [heads_rows(cross_q)], [heads_rows(self_out.T)])
     text_rows = gather(wire, [heads_rows(cross_kv[0], cross_kv[1])], [heads_rows(cross_out.T)])
+
     unit_rows = [gather(wire, *ffn_rows(at)) for at in range(2)]
 
     slot = jnp.arange(wide)
-    block, row = slot // rows, slot % rows
-    back_seq = block // dp_size
-    back_dp = sum(jnp.where(block % dp_size == k, a, 0) for k, a in enumerate(slot_order(dp_size)))
-    from_seq = (lax.axis_index(SEQ) - back_seq) % seq_size
-    from_dp = ring_member(DP, (ring_place(DP) - back_dp) % dp_size)
-    valid = row < own_rows
-    channel = jnp.where(valid, (from_dp * seq_size + from_seq) * own_rows + row, -1)
+    valid = slot % rows < own_rows
+    channel = jnp.where(valid, slot // rows * own_rows + slot % rows, -1)
     pick = (jnp.arange(features)[:, None] == channel[None, :]).astype(BF16)
 
     def relative(values):
@@ -779,7 +824,7 @@
     ffn_out_grad = both((gate_f * grad_out).astype(BF16))
 
     def weight_grad(activation, grad):
-        return [dot(activation[:, b * near : (b + 1) * near], grad, 0, 0).astype(BF16) for b in range(seq_size)]
+        return dot(activation, grad, 0, 0).astype(BF16)
 
     unit_a, _ = normalise(resid_in)
     normed = both((unit_a * (1.0 + scale_a) + shift_a).astype(BF16))
@@ -796,6 +841,10 @@
     w_ckv, w_co = wire.need(text_rows)
     text_proj = dot(caption, w_ckv, 1, 0).astype(BF16)
     attended, peaks = kernels.cross(lengths, cross_query, wire.step(text_proj))
+    head_count = heads_width // HEAD_DIM
+    head_peaks = []
+    own_peaks = jnp.max(peaks[:, :, : LANES // HEAD_DIM, 0], axis=0).reshape(-1)[:head_count]
+    wire.join(butterfly_phases(own_peaks, (SEQ, DP), jnp.maximum, head_peaks))
     resid_b = resid_a + core_total([(wire.step(attended), w_co, 1)])
     unit_f, _ = normalise(resid_b)
     normed_ffn = both((unit_f * (1.0 + scale_f) + shift_f).astype(BF16))
@@ -806,61 +855,77 @@
         bias = jnp.concatenate([units(up_b[0:1], at), units(up_b[1:2], at)], axis=1)
         filters = jnp.stack([units(conv_w[:, j], at) for j in range(2)])
         filter_bias = jnp.stack([units(conv_b[j : j + 1], at) for j in range(2)])
-        pre = dot(wire.step(normed_ffn), w_up, 1, 0) + bias
+        pre = dot(wire.step(normed_ffn) if at == 0 else normed_ffn, w_up, 1, 0) + bias
         by_micro = pre.reshape(micro, tokens, 2 * half)
         edges = jnp.concatenate([by_micro[:, :cols], by_micro[:, -cols:]], axis=1)
         top, bottom = halos(silu(edges).astype(BF16), cols)
         gated_grad = dot(ffn_out_grad, w_down, 1, 0)
-        pre, top, bottom = wire.step((pre, top, bottom))
+        if at == 0:
+            pre, top, bottom = wire.step((pre, top, bottom))
         gated = kernels.conv(pre, top, bottom, filters, filter_bias)
-        gated_grad = wire.step(gated_grad)
+        if at == 0:
+            gated_grad = wire.step(gated_grad)
         conv_grad0, conv_grad1, small = kernels.conv_back(pre, top, bottom, gated_grad, filters, filter_bias)
-        conv_grad = jnp.concatenate([conv_grad0, conv_grad1], axis=1)
-        top_grad, bottom_grad = halos(conv_grad.reshape(micro, tokens, 2 * half), cols)
+        edges = [grad.reshape(micro, tokens, half) for grad in (conv_grad0, conv_grad1)]
+        edges = jnp.concatenate(
+            [jnp.concatenate([grad[:, :cols], grad[:, -cols:]], axis=1) for grad in edges], axis=2
+        )
+        top_grad, bottom_grad = halos(edges, cols)
         down_parts = weight_grad(ffn_out_grad, gated)
-        top_grad, bottom_grad = wire.step((top_grad, bottom_grad))
-        up_low, bias_grad = kernels.act_back(pre, conv_grad, top_grad, bottom_grad, filters)
-        smalls.append(
-            jnp.concatenate([jnp.sum(small, axis=0)[:20], jnp.sum(bias_grad, axis=0)[:1].reshape(2, half)], axis=0)
+        down_sum = scatter(None, [down_parts], []) if at == 0 else []
+        if at == 0:
+            top_grad, bottom_grad = wire.step((top_grad, bottom_grad))
+        up_low0, up_low1, bias_grad = kernels.act_back(
+            pre, (conv_grad0, conv_grad1), [top_grad[:, :, :half], top_grad[:, :, half:]],
+            [bottom_grad[:, :, :half], bottom_grad[:, :, half:]], filters,
         )
-        up_low = wire.step(up_low)
-        ffn_grads.append(scatter(wire, [weight_grad(normed_ffn, up_low)], [down_parts]))
+        smalls.append(jnp.concatenate([jnp.sum(small, axis=0)[:20], jnp.sum(bias_grad, axis=0)[:2]], axis=0))
+        if at == 0:
+            up_low0, up_low1 = wire.step((up_low0, up_low1))
+        up_low = jnp.concatenate([up_low0, up_low1], axis=1)
+        up_parts = weight_grad(normed_ffn, up_low)
+        if at == 0:
+            ffn_grads.append(scatter(None, [up_parts], []) + down_sum)
+        else:
+            ffn_grads.append(scatter(wire, [up_parts], [down_parts]))
         ffn_terms.append((gated, w_down, 1))
         backs.append((up_low, w_up, 1))
-    small, head_peaks = [], []
+    small = []
     wire.join(butterfly_phases(jnp.concatenate(smalls, axis=1), (SEQ, DP), jnp.add, small))
-    head_count = heads_width // HEAD_DIM
-    own_peaks = jnp.max(peaks[:, :, : LANES // HEAD_DIM, 0], axis=0).reshape(-1)[:head_count]
-    wire.join(butterfly_phases(own_peaks, (SEQ, DP), jnp.maximum, head_peaks))
-
+
+    backs[1] = (wire.step(up_low, True), *backs[1][1:])
     normed_ffn_grad = core_total(backs)
-    ffn_out = core_total(ffn_terms)
+    resid_b_part, shift_f_grad, scale_f_grad = normalise_back(resid_b, normed_ffn_grad, scale_f)
+    resid_b_grad = grad_out + resid_b_part
+    cross_grad = both(wire.step(resid_b_grad, True).astype(BF16))
+    attended_grad = dot(cross_grad, w_co, 1, 0).astype(BF16)
+    query_grad, key_grad, value_grad = kernels.cross_back(lengths, cross_query, text_proj, wire.step(attended_grad, True))
+    (query_grad, key_grad, value_grad), _ = lax.optimization_barrier(((query_grad, key_grad, value_grad), ffn_grads[0]))
+    query_grad, key_grad, value_grad = wire.step((query_grad, key_grad, value_grad), True)
+    cross_out_parts = weight_grad(cross_grad, attended)
+    cross_kv_parts = weight_grad(caption, jnp.concatenate([key_grad, value_grad], axis=1))
+    text_grads = scatter(None, [cross_kv_parts], [])
+    text_grads += scatter(None, [cross_out_parts], [])
+    resid_a_grad = resid_b_grad + core_total([(wire.step(query_grad, True), w_cq, 1)])
+    cross_q_parts = weight_grad(cross_input, query_grad)
+    gate_a_grad = jnp.sum(resid_a_grad * self_term, axis=0)
+    self_grad = both((gate_a * resid_a_grad).astype(BF16))
+    mixed_grad = dot(wire.step(self_grad, True), w_so, 1, 0)
+    q_low, state_grad = kernels.mix_back(queries, states, wire.step(mixed_grad, True))
+    self_out_parts = weight_grad(self_grad, mixed)
+    state_grad = butterfly(state_grad, (SEQ,), jnp.add)
+    token_grads = scatter(wire, [cross_q_parts, weight_grad(normed, q_low)], [self_out_parts])
+    kv_low = kernels.states_back(keys_values, wire.step(state_grad, True))
+    key_parts, value_parts = [weight_grad(normed, kv_low[:, j * width : (j + 1) * width]) for j in range(2)]
+    kv_grads = scatter(wire, [key_parts], [value_parts])
+    kv_low, _ = lax.optimization_barrier((wire.step(kv_low, True), text_grads))
+    normed_grad = core_total([(q_low, w_q, 1), (kv_low, w_kv, 1)])
+    resid_part, shift_a_grad, scale_a_grad = normalise_back(resid_in, wire.step(normed_grad, True), scale_a)
+    latent_grad = resid_a_grad + resid_part
+    ffn_terms = wire.after([left for left, _, _ in ffn_terms])
+    ffn_out = core_total([(left, rows_of[1], 1) for left, rows_of in zip(ffn_terms, unit_rows)])
     resid_c = resid_b + gate_f * ffn_out
     gate_f_grad = jnp.sum(grad_out * ffn_out, axis=0)
-    resid_b_part, shift_f_grad, scale_f_grad = normalise_back(resid_b, wire.step(normed_ffn_grad), scale_f)
-    resid_b_grad = grad_out + resid_b_part
-    cross_grad = both(resid_b_grad.astype(BF16))
-    attended_grad = dot(wire.step(cross_grad), w_co, 1, 0).astype(BF16)
-    cross_out_parts = weight_grad(cross_grad, attended)
-    query_grad, key_grad, value_grad = kernels.cross_back(lengths, cross_query, text_proj, wire.step(attended_grad))
-    query_grad = wire.step(query_grad)
-    cross_kv_parts = weight_grad(caption, jnp.concatenate([key_grad, value_grad], axis=1))
-    text_grads = scatter(wire, [cross_kv_parts], [cross_out_parts])
-    resid_a_grad = resid_b_grad + core_total([(query_grad, w_cq, 1)])
-    cross_q_parts = weight_grad(cross_input, query_grad)
-    gate_a_grad = jnp.sum(resid_a_grad * self_term, axis=0)
-    self_grad = both((gate_a * wire.step(resid_a_grad)).astype(BF16))
-    mixed_grad = dot(self_grad, w_so, 1, 0)
-    q_low, state_grad = kernels.mix_back(queries, states, wire.step(mixed_grad))
-    state_grad = butterfly(state_grad, (SEQ,), jnp.add)
-    token_grads = scatter(wire, [cross_q_parts], [weight_grad(self_grad, mixed)])
-    q_parts = weight_grad(normed, q_low)
-    kv_low = kernels.states_back(keys_values, wire.step(state_grad))
-    kv_low = wire.step(kv_low)
-    qkv_grads = scatter(wire, [weight_grad(normed, kv_low)], [q_parts])
-    normed_grad = core_total([(q_low, w_q, 1), (kv_low, w_kv, 1)])
-    resid_part, shift_a_grad, scale_a_grad = normalise_back(resid_in, normed_grad, scale_a)
-    latent_grad = resid_a_grad + resid_part
 
     def whole(own):
         other = other_core(own)
@@ -882,8 +947,7 @@
     up_grad = jnp.concatenate(
         [up[:, j * half : (j + 1) * half] for j in range(2) for up, _ in ffn_grads], axis=1
     )
-    (cross_kv_grad, cross_out_grad), (cross_q_grad, self_out_grad) = text_grads, token_grads
-    kv_grad, q_grad = qkv_grads
+    (cross_kv_grad, cross_out_grad), (cross_q_grad, q_grad, self_out_grad) = text_grads, token_grads
 
     factor = jnp.repeat(jnp.sqrt(CLIP_TAU / jnp.maximum(head_peaks, CLIP_TAU)), HEAD_DIM)
 
@@ -899,7 +963,7 @@
         output,
         latents_grad,
         table_grad,
-        jnp.concatenate([heads(q_grad)[None], cut(kv_grad, 2, width, heads_width)], axis=0),
+        jnp.stack([heads(grad) for grad in [q_grad] + kv_grads]),
         heads(self_out_grad).T,
         heads(cross_q_grad),
         cut(cross_kv_grad, 2, width, heads_width),

time: 2070 us -> 1910 us (0.923)
  Pallas kernels: 312 us -> 447 us
  waiting for transfers between devices: 648 us -> 516 us
  local copies, waits for them, and re-layouts: 246 us -> 149 us
  other arithmetic: 170 us -> 103 us
    ppermute x125 -> x101, waiting for transfers between devices: 604 us -> 349 us  [shift(): lax.ppermute(values, axis, [(cycle[i], cycle[(i + step) % size]) for i in...]
    ppermute x12, waiting for transfers between devices: 15.5 us -> 154 us  [shift(): return lax.ppermute(values, axis, step)]
    pallas_call x2 -> x31, Pallas kernels: 63.1 us -> 200 us  [the longest x24 85.6 us: combine(): pl.pallas_call(functools.partial(combine_kernel, near_count, len(blocks)...]
    unnamed x772 -> x428, local copies, waits for them, and re-layouts: 151 us -> 40.8 us
    convert_element_type x36 -> x4, other arithmetic: 58.4 us -> 7.23 us  [the longest x3 5.43 us: scatter(): total.astype(F32)]
    ppermute x125 -> x101, starting transfers between devices: 136 us -> 104 us  [shift(): lax.ppermute(values, axis, [(cycle[i], cycle[(i + step) % size]) for i in...]
    add x20 -> x1, other arithmetic: 29.1 us -> 6.14 us  [shards(): resid_b_grad = grad_out + resid_b_part]
    dot_general x54 -> x45, matrix products: 487 us -> 496 us  [dot(): lax.dot_general(left, right, (((left_dim,), (right_dim,)), ((), ())), pre...]
  transfers between devices with their start and end apart: 162 -> 142, of which waited for: 75 -> 51; matrix products, arithmetic and copies ran while one was open for 39% -> 38% of each run, Pallas kernels for 10% -> 24%
where the time goes in v2:
time: 1910 us; the launch traced here: 1890 us
  waiting for transfers between devices  516 us (27%)
  matrix products  511 us (27%)
  Pallas kernels  447 us (23%)
  starting transfers between devices  151 us (8%)
  local copies, waits for them, and re-layouts  149 us (8%)
  other arithmetic  103 us (5%)
    dot_general x45, matrix products, dot(): lax.dot_general(left, right, (((left_dim,), (right_dim,)), ((), ())), pre...  496 us
    ppermute x101, waiting for transfers between devices, shift(): lax.ppermute(values, axis, [(cycle[i], cycle[(i + step) % size]) for i in...  349 us
    ppermute x12, waiting for transfers between devices, shift(): return lax.ppermute(values, axis, step)  154 us
    ppermute x101, starting transfers between devices, shift(): lax.ppermute(values, axis, [(cycle[i], cycle[(i + step) % size]) for i in...  104 us
    pallas_call x24, Pallas kernels, combine(): pl.pallas_call(functools.partial(combine_kernel, near_count, len(blocks)...  85.6 us
    pallas_call x5, Pallas kernels, assemble(): pl.pallas_call(functools.partial(assemble_kernel, moves, rows, len(arrays...  70.7 us
    pallas_call x2, Pallas kernels, conv_back(): call(functools.partial(conv_back_kernel, self.cols), (self.micro, self.un...  53.2 us
    pallas_call x1, Pallas kernels, cross_back(): call(cross_back_kernel, (self.micro, self.groups), [smem, self.tile(), se...  52.6 us
  transfers between devices with their start and end apart: 142, of which 51 were waited for; matrix products, arithmetic and copies ran while one was open for 38% of the time, Pallas kernels for 24%

profile of v2, /device:TPU:0, one launch (start us, length us, event | category | flops | bytes accessed | tf_op | source)
XLA Modules:
  0.0 1893.4 jit_solution(9640221599552202403)
XLA Ops:
  97.7 22.9 %collective-permute-done.8.refs_6_ = bf16[144,4608]{1,0:T(8,128)(2,1)S(1)} collective-permute-done((bf16[144,4608]{1,0:T(8,128)(2,1)S(1)}, bf16[144,4608]{1,0:T(8,128)(2,1)S(1)}, u32[]{:S(2)}, u32[]{:S(2)}) %collective-permute-start.8) | collective-permute-done | bytes 1327136 | tf_op jit(solution)/shard_map/ppermute | solution.py:63
  126.9 30.5 %collective-permute-done.12 = bf16[144,1152]{1,0:T(8,128)(2,1)S(1)} collective-permute-done((bf16[144,1152]{1,0:T(8,128)(2,1)S(1)}, bf16[144,1152]{1,0:T(8,128)(2,1)S(1)}, u32[]{:S(2)}, u32[]{:S(2)}) %collective-permute-start.12) | collective-permute-done | bytes 331808 | tf_op jit(solution)/shard_map/ppermute | solution.py:63
  374.8 17.8 collective-permute-done.38.refs_6_
  397.9 34.0 %collective-permute-done.42 = bf16[144,1408]{1,0:T(8,128)(2,1)S(1)} collective-permute-done((bf16[144,1408]{1,0:T(8,128)(2,1)S(1)}, bf16[144,1408]{1,0:T(8,128)(2,1)S(1)}, u32[]{:S(2)}, u32[]{:S(2)}) %collective-permute-start.42) | collective-permute-done | bytes 405536 | tf_op jit(solution)/shard_map/ppermute | solution.py:63
  485.8 34.4 %shard_map.276 = (bf16[1024,1152]{1,0:T(8,128)(2,1)S(1)}, f32[2,9,8,128]{3,2,1,0:T(8,128)S(1)}) custom-call(s32[2]{0:T(128)S(1)} %broadcast_select_fusion.length_ref, bf16[1024,1152]{1,0:T(8,128)(2,1)S(1)} %convolution_convert_fusion.16.query_ref, bf16[608,2304]{1,0:T(8,128)(2,1)} %convolution_convert_fusion.11.key_ref.value_ref, ...), custom_call_target="tpu_custom_call" | custom-call | flops 23592960000 | bytes 7077888 | tf_op jit(solution)/shard_map/pallas_call | solution.py:659
  537.5 21.0 %collective-permute-done.54 = f32[35]{0:T(128)S(1)} collective-permute-done((f32[35]{0:T(128)S(1)}, f32[35]{0:T(128)S(1)}, u32[]{:S(2)}, u32[]{:S(2)}) %collective-permute-start.54) | collective-permute-done | bytes 172 | tf_op jit(solution)/shard_map/ppermute | solution.py:60
  668.3 19.3 %convolution_add_fusion.1.z0.z1 = f32[1024,2816]{1,0:T(8,128)} fusion(bf16[1024,2304]{1,0:T(8,128)(2,1)S(1)} %pad_maximum_fusion.2, bf16[2304,2816]{1,0:T(8,128)(2,1)} %get-tuple-element.258, f32[2816]{0:T(1024)S(1)} %copy-done.181), kind=kOutput, calls=%fused_computation.30 | convolution fusion | flops 13290438656 | bytes 29240320 | tf_op jit(solution)/shard_map/dot_general | solution.py:27
  713.6 18.8 shard_map.278
  745.2 26.7 %shard_map.281 = (bf16[1024,1408]{1,0:T(8,128)(2,1)S(1)}, bf16[1024,1408]{1,0:T(8,128)(2,1)}, f32[2,24,1408]{2,1,0:T(8,128)S(1)}) custom-call(f32[1024,2816]{1,0:T(8,128)} %convolution_add_fusion.1.z0.z1, f32[1024,2816]{1,0:T(8,128)} %convolution_add_fusion.1.z0.z1, bf16[2,32,2816]{2,1,0:T(8,128)(2,1)S(1)} %collective-permute-done.65.top0.top1, ...), custom_call_target="tpu_custom_call" | custom-call | flops 57671680000 | bytes 23068672 | tf_op jit(solution)/shard_map/pallas_call | solution.py:707
  799.2 21.7 %shard_map.282 = (bf16[1024,1408]{1,0:T(8,128)(2,1)S(1)}, bf16[1024,1408]{1,0:T(8,128)(2,1)}, f32[2,8,1408]{2,1,0:T(8,128)S(1)}) custom-call(f32[1024,2816]{1,0:T(8,128)} %convolution_add_fusion.1.z0.z1, f32[1024,2816]{1,0:T(8,128)} %convolution_add_fusion.1.z0.z1, bf16[1024,1408]{1,0:T(8,128)(2,1)} %copy-done.34, ...), custom_call_target="tpu_custom_call" | custom-call | flops 57671680000 | bytes 28835840 | tf_op jit(solution)/shard_map/pallas_call | solution.py:719
  842.0 18.6 convolution_add_fusion.z0.z1
  871.7 19.8 %convolution_convert_fusion.1 = bf16[2304,2816]{1,0:T(8,128)(2,1)} fusion(bf16[1024,2816]{1,0:T(8,128)(2,1)} %constant_dynamic-update-slice_fusion, bf16[512,2304]{1,0:T(8,128)(2,1)} %collective-permute-done.51, bf16[512,2304]{1,0:T(8,128)(2,1)S(1)} %copy-done.69), kind=kOutput, calls=%fused_computation.10 | convolution fusion | flops 13303480320 | bytes 23461888 | tf_op jit(solution)/shard_map/dot_general | solution.py:27
  907.8 26.5 %shard_map.283 = (bf16[1024,1408]{1,0:T(8,128)(2,1)S(1)}, bf16[1024,1408]{1,0:T(8,128)(2,1)}, f32[2,24,1408]{2,1,0:T(8,128)S(1)}) custom-call(f32[1024,2816]{1,0:T(8,128)} %copy-done.159, f32[1024,2816]{1,0:T(8,128)} %copy-done.159, bf16[2,32,2816]{2,1,0:T(8,128)(2,1)S(1)} %copy-done.43, bf16[2,32,2816]{2,1,0:T(8,128)(2,1)S(1)} %copy-done.43, ...), custom_call_target="tpu_custom_call" | custom-call | flops 57671680000 | bytes 23068672 | tf_op jit(solution)/shard_map/pallas_call | solution.py:707
  938.2 18.9 shard_map.280
  983.8 21.5 %shard_map.284 = (bf16[1024,1408]{1,0:T(8,128)(2,1)S(1)}, bf16[1024,1408]{1,0:T(8,128)(2,1)}, f32[2,8,1408]{2,1,0:T(8,128)S(1)}) custom-call(f32[1024,2816]{1,0:T(8,128)} %copy-done.159, f32[1024,2816]{1,0:T(8,128)} %copy-done.159, bf16[1024,1408]{1,0:T(8,128)(2,1)} %copy-done.35, bf16[1024,1408]{1,0:T(8,128)(2,1)} %get-tuple-element.285.grad1, ...), custom_call_target="tpu_custom_call" | custom-call | flops 57671680000 | bytes 28835840 | tf_op jit(solution)/shard_map/pallas_call | solution.py:719
  1079.5 18.1 multiply_reduce_fusion.1
  1135.3 41.3 %collective-permute-done.88 = f32[22,2816]{1,0:T(8,128)S(1)} collective-permute-done((f32[22,2816]{1,0:T(8,128)}, f32[22,2816]{1,0:T(8,128)S(1)}, u32[]{:S(2)}, u32[]{:S(2)}) %collective-permute-start.88) | collective-permute-done | bytes 247840 | tf_op jit(solution)/shard_map/ppermute | solution.py:60
  1211.1 43.8 %collective-permute-done.92 = f32[22,2816]{1,0:T(8,128)S(1)} collective-permute-done((f32[22,2816]{1,0:T(8,128)}, f32[22,2816]{1,0:T(8,128)S(1)}, u32[]{:S(2)}, u32[]{:S(2)}) %collective-permute-start.92) | collective-permute-done | bytes 247840 | tf_op jit(solution)/shard_map/ppermute | solution.py:60
  1279.1 52.6 %shard_map.285 = (bf16[1024,1152]{1,0:T(8,128)(2,1)S(1)}, bf16[608,1152]{1,0:T(8,128)(2,1)S(1)}, bf16[608,1152]{1,0:T(8,128)(2,1)S(1)}) custom-call(s32[2]{0:T(128)S(1)} %copy-done.39, bf16[1024,1152]{1,0:T(8,128)(2,1)} %copy-done.57, bf16[608,2304]{1,0:T(8,128)(2,1)} %convolution_convert_fusion.11.key_ref.value_ref, ...), custom_call_target="tpu_custom_call" | custom-call | flops 58982400000 | bytes 7077888 | tf_op jit(solution)/shard_map/pallas_call | solution.py:670
  1452.9 25.6 %shard_map.299 = bf16[1024,2304]{1,0:T(8,128)(2,1)S(1)} custom-call(f32[1024,2304]{1,0:T(8,128)} %fusion.108.key_ref.value_ref, f32[1024,2304]{1,0:T(8,128)} %fusion.108.key_ref.value_ref, f32[2,9,40,128]{3,2,1,0:T(8,128)S(1)} %add.1512.state_ref), custom_call_target="tpu_custom_call" | custom-call | flops 1769472000 | bytes 23592960 | tf_op jit(solution)/shard_map/pallas_call | solution.py:645
  1549.5 26.2 %collective-permute-done.104.refs_4_ = bf16[288,2304]{1,0:T(8,128)(2,1)S(1)} collective-permute-done((bf16[288,2304]{1,0:T(8,128)(2,1)}, bf16[288,2304]{1,0:T(8,128)(2,1)S(1)}, u32[]{:S(2)}, u32[]{:S(2)}) %collective-permute-start.104) | collective-permute-done | bytes 1327136 | tf_op jit(solution)/shard_map/ppermute | solution.py:63
  1693.4 19.5 %collective-permute-done.117 = f32[6,2240]{1,0:T(8,128)S(1)} collective-permute-done((f32[6,2240]{1,0:T(8,128)S(1)}, f32[6,2240]{1,0:T(8,128)S(1)}, u32[]{:S(2)}, u32[]{:S(2)}) %collective-permute-start.117) | collective-permute-done | bytes 53792 | tf_op jit(solution)/shard_map/ppermute | solution.py:60
  1722.6 24.4 %collective-permute-done.121 = f32[6,2240]{1,0:T(8,128)S(1)} collective-permute-done((f32[6,2240]{1,0:T(8,128)S(1)}, f32[6,2240]{1,0:T(8,128)S(1)}, u32[]{:S(2)}, u32[]{:S(2)}) %collective-permute-start.121) | collective-permute-done | bytes 53792 | tf_op jit(solution)/shard_map/ppermute | solution.py:60
  1853.9 17.6 collective-permute-done.136.refs_4_
  (1030 shorter events, 1254.5 us)
Async XLA Ops:
  7.2 1340.4 %reduce-scatter.7.cloned.1.call-start = ((), (), s32[]{:S(2)}) async-start(), calls=%async_computation.5 | async-start | bytes 6893568 | tf_op jit(solution)/shard_map/reduce_scatter | solution.py:350
  38.7 184.1 %collective-permute-start = (bf16[512,2304]{1,0:T(8,128)(2,1)}, bf16[512,2304]{1,0:T(8,128)(2,1)}, u32[]{:S(2)}, u32[]{:S(2)}) collective-permute-start(bf16[512,2304]{1,0:T(8,128)(2,1)} %add_convert_fusion.2), channel_id=1, source_target_pairs={{0,1},{1,0},{2,3},{3,2},{4,5},{5,4},{6,7},{7,6},{8,9},{9,8},{10,11... | collective-permute-start | bytes 7077896 | tf_op jit(solution)/shard_map/ppermute | solution.py:366
  374.1 59.5 %collective-permute-start.30 = (bf16[512,2304]{1,0:T(8,128)(2,1)}, bf16[512,2304]{1,0:T(8,128)(2,1)S(1)}, u32[]{:S(2)}, u32[]{:S(2)}) collective-permute-start(bf16[512,2304]{1,0:T(8,128)(2,1)} %get-tuple-element.482), channel_id=1, source_target_pairs={{0,1},{1,0},{2,3},{3,2},{4,5},{5,4},{6,7},{7,6},{8,9},{9,8},{10,11... | collective-permute-start | bytes 7077896 | tf_op jit(solution)/shard_map/ppermute | solution.py:366
  558.5 86.6 %collective-permute-start.79 = (bf16[512,2304]{1,0:T(8,128)(2,1)}, bf16[512,2304]{1,0:T(8,128)(2,1)}, u32[]{:S(2)}, u32[]{:S(2)}) collective-permute-start(bf16[512,2304]{1,0:T(8,128)(2,1)} %get-tuple-element.486), channel_id=1, source_target_pairs={{0,1},{1,0},{2,3},{3,2},{4,5},{5,4},{6,7},{7,6},{8,9},{9,8},{10,11... | collective-permute-start | bytes 7077896 | tf_op jit(solution)/shard_map/ppermute | solution.py:366
  792.8 556.7 %reduce-scatter.5.cloned.1.call-start = ((), (), s32[]{:S(2)}) async-start(), calls=%async_computation.4 | async-start | bytes 13787136 | tf_op jit(solution)/shard_map/reduce_scatter | solution.py:350
  891.6 467.9 %reduce-scatter.9.cloned.1.call-start = ((), (), s32[]{:S(2)}) async-start(), calls=%async_computation.6 | async-start | bytes 5640192 | tf_op jit(solution)/shard_map/reduce_scatter | solution.py:350
  1066.8 53.5 %collective-permute-start.87 = (bf16[288,2816]{1,0:T(8,128)(2,1)}, bf16[288,2816]{1,0:T(8,128)(2,1)S(1)}, u32[]{:S(2)}, u32[]{:S(2)}) collective-permute-start(bf16[288,2816]{1,0:T(8,128)(2,1)} %pad_maximum_fusion.23), channel_id=1, source_target_pairs={{0,2},{2,0},{1,3},{3,1},{4,6},{6,4},{5,7},{7,5},{8,10},{10,8},{9,1... | collective-permute-start | bytes 4866056 | tf_op jit(solution)/shard_map/ppermute | solution.py:63
  1106.6 86.3 %collective-permute-start.85 = (bf16[512,2304]{1,0:T(8,128)(2,1)}, bf16[512,2304]{1,0:T(8,128)(2,1)}, u32[]{:S(2)}, u32[]{:S(2)}) collective-permute-start(bf16[512,2304]{1,0:T(8,128)(2,1)} %convert_element_type.229), channel_id=1, source_target_pairs={{0,1},{1,0},{2,3},{3,2},{4,5},{5,4},{6,7},{7,6},{8,9},{9,8},{10,11... | collective-permute-start | bytes 7077896 | tf_op jit(solution)/shard_map/ppermute | solution.py:366
  1127.2 53.5 %collective-permute-start.90 = (bf16[144,5632]{1,0:T(8,128)(2,1)}, bf16[144,5632]{1,0:T(8,128)(2,1)}, u32[]{:S(2)}, u32[]{:S(2)}) collective-permute-start(bf16[144,5632]{1,0:T(8,128)(2,1)} %shard_map.287), channel_id=1, source_target_pairs={{0,8},{8,16},{16,24},{24,28},{28,20},{20,12},{12,4},{4,0},{1,9},{9... | collective-permute-start | bytes 4866056 | tf_op jit(solution)/shard_map/ppermute | solution.py:63
  1128.2 52.5 %collective-permute-start.91 = (bf16[288,2816]{1,0:T(8,128)(2,1)}, bf16[288,2816]{1,0:T(8,128)(2,1)S(1)}, u32[]{:S(2)}, u32[]{:S(2)}) collective-permute-start(bf16[288,2816]{1,0:T(8,128)(2,1)} %pad_maximum_fusion.24), channel_id=1, source_target_pairs={{0,2},{2,0},{1,3},{3,1},{4,6},{6,4},{5,7},{7,5},{8,10},{10,8},{9,1... | collective-permute-start | bytes 4866056 | tf_op jit(solution)/shard_map/ppermute | solution.py:63
  1129.9 55.5 %collective-permute-start.89 = (bf16[144,5632]{1,0:T(8,128)(2,1)S(1)}, bf16[144,5632]{1,0:T(8,128)(2,1)}, u32[]{:S(2)}, u32[]{:S(2)}) collective-permute-start(bf16[144,5632]{1,0:T(8,128)(2,1)S(1)} %shard_map.286), channel_id=1, source_target_pairs={{0,4},{8,0},{16,8},{24,16},{28,24},{20,28},{12,20},{4,12},{1,5},{9... | collective-permute-start | bytes 4866056 | tf_op jit(solution)/shard_map/ppermute | solution.py:63
  1189.0 82.2 %collective-permute-start.93 = (bf16[144,5632]{1,0:T(8,128)(2,1)S(1)}, bf16[144,5632]{1,0:T(8,128)(2,1)}, u32[]{:S(2)}, u32[]{:S(2)}) collective-permute-start(bf16[144,5632]{1,0:T(8,128)(2,1)S(1)} %shard_map.288), channel_id=1, source_target_pairs={{0,4},{8,0},{16,8},{24,16},{28,24},{20,28},{12,20},{4,12},{1,5},{9... | collective-permute-start | bytes 4866056 | tf_op jit(solution)/shard_map/ppermute | solution.py:63
  1190.8 75.8 %collective-permute-start.94 = (bf16[144,5632]{1,0:T(8,128)(2,1)}, bf16[144,5632]{1,0:T(8,128)(2,1)}, u32[]{:S(2)}, u32[]{:S(2)}) collective-permute-start(bf16[144,5632]{1,0:T(8,128)(2,1)} %shard_map.289), channel_id=1, source_target_pairs={{0,8},{8,16},{16,24},{24,28},{28,20},{20,12},{12,4},{4,0},{1,9},{9... | collective-permute-start | bytes 4866056 | tf_op jit(solution)/shard_map/ppermute | solution.py:63
  1191.6 75.0 %collective-permute-start.95 = (bf16[288,2816]{1,0:T(8,128)(2,1)}, bf16[288,2816]{1,0:T(8,128)(2,1)S(1)}, u32[]{:S(2)}, u32[]{:S(2)}) collective-permute-start(bf16[288,2816]{1,0:T(8,128)(2,1)} %pad_maximum_fusion.25), channel_id=1, source_target_pairs={{0,2},{2,0},{1,3},{3,1},{4,6},{6,4},{5,7},{7,5},{8,10},{10,8},{9,1... | collective-permute-start | bytes 4866056 | tf_op jit(solution)/shard_map/ppermute | solution.py:63
  1202.9 680.3 %reduce-scatter.11.cloned.1.call-start = ((), (), s32[]{:S(2)}) async-start(), calls=%async_computation.7 | async-start | bytes 11280384 | tf_op jit(solution)/shard_map/reduce_scatter | solution.py:350
  1275.8 61.0 %collective-permute-start.100 = (f32[22,2816]{1,0:T(8,128)S(1)}, f32[22,2816]{1,0:T(8,128)S(1)}, u32[]{:S(2)}, u32[]{:S(2)}) collective-permute-start(f32[22,2816]{1,0:T(8,128)S(1)} %add.1505), channel_id=1, source_target_pairs={{0,16},{4,20},{8,24},{12,28},{16,0},{20,4},{24,8},{28,12},{1,17},{... | collective-permute-start | bytes 743432 | tf_op jit(solution)/shard_map/ppermute | solution.py:60
  1277.9 64.8 %collective-permute-start.98 = (bf16[288,2816]{1,0:T(8,128)(2,1)}, bf16[288,2816]{1,0:T(8,128)(2,1)S(1)}, u32[]{:S(2)}, u32[]{:S(2)}) collective-permute-start(bf16[288,2816]{1,0:T(8,128)(2,1)} %pad_maximum_fusion.26), channel_id=1, source_target_pairs={{0,2},{2,0},{1,3},{3,1},{4,6},{6,4},{5,7},{7,5},{8,10},{10,8},{9,1... | collective-permute-start | bytes 4866056 | tf_op jit(solution)/shard_map/ppermute | solution.py:63
  1279.1 63.6 %collective-permute-start.99 = (bf16[144,5632]{1,0:T(8,128)(2,1)}, bf16[144,5632]{1,0:T(8,128)(2,1)}, u32[]{:S(2)}, u32[]{:S(2)}) collective-permute-start(bf16[144,5632]{1,0:T(8,128)(2,1)} %shard_map.291), channel_id=1, source_target_pairs={{0,4},{8,0},{16,8},{24,16},{28,24},{20,28},{12,20},{4,12},{1,5},{9... | collective-permute-start | bytes 4866056 | tf_op jit(solution)/shard_map/ppermute | solution.py:63
  1334.2 105.6 %collective-permute-start.101 = (bf16[144,5632]{1,0:T(8,128)(2,1)}, bf16[144,5632]{1,0:T(8,128)(2,1)S(1)}, u32[]{:S(2)}, u32[]{:S(2)}) collective-permute-start(bf16[144,5632]{1,0:T(8,128)(2,1)} %shard_map.292), channel_id=1, source_target_pairs={{0,8},{8,16},{16,24},{24,28},{28,20},{20,12},{12,4},{4,0},{1,9},{9... | collective-permute-start | bytes 4866056 | tf_op jit(solution)/shard_map/ppermute | solution.py:63
  1439.8 78.2 %collective-permute-start.103 = (bf16[288,2304]{1,0:T(8,128)(2,1)}, bf16[288,2304]{1,0:T(8,128)(2,1)S(1)}, u32[]{:S(2)}, u32[]{:S(2)}) collective-permute-start(bf16[288,2304]{1,0:T(8,128)(2,1)} %maximum_maximum_fusion), channel_id=1, source_target_pairs={{0,2},{2,0},{1,3},{3,1},{4,6},{6,4},{5,7},{7,5},{8,10},{10,8},{9,1... | collective-permute-start | bytes 3981320 | tf_op jit(solution)/shard_map/ppermute | solution.py:63
  1440.9 84.0 %collective-permute-start.102 = (bf16[144,5632]{1,0:T(8,128)(2,1)S(1)}, bf16[144,5632]{1,0:T(8,128)(2,1)S(1)}, u32[]{:S(2)}, u32[]{:S(2)}) collective-permute-start(bf16[144,5632]{1,0:T(8,128)(2,1)S(1)} %copy-done.13), channel_id=1, source_target_pairs={{0,4},{8,0},{16,8},{24,16},{28,24},{20,28},{12,20},{4,12},{1,5},{9... | collective-permute-start | bytes 4866056 | tf_op jit(solution)/shard_map/ppermute | solution.py:63
  1497.9 87.6 %collective-permute-start.114 = (bf16[512,2304]{1,0:T(8,128)(2,1)}, bf16[512,2304]{1,0:T(8,128)(2,1)}, u32[]{:S(2)}, u32[]{:S(2)}) collective-permute-start(bf16[512,2304]{1,0:T(8,128)(2,1)} %fusion.20), channel_id=1, source_target_pairs={{0,1},{1,0},{2,3},{3,2},{4,5},{5,4},{6,7},{7,6},{8,9},{9,8},{10,11... | collective-permute-start | bytes 7077896 | tf_op jit(solution)/shard_map/ppermute | solution.py:366
  1692.8 102.9 %collective-permute-start.115 = (f32[512,2240]{0,1:T(8,128)}, f32[512,2240]{0,1:T(8,128)}, u32[]{:S(2)}, u32[]{:S(2)}) collective-permute-start(f32[512,2240]{0,1:T(8,128)} %fusion.16), channel_id=1, source_target_pairs={{0,1},{1,0},{2,3},{3,2},{4,5},{5,4},{6,7},{7,6},{8,9},{9,8},{10,11... | collective-permute-start | bytes 13762568 | tf_op jit(solution)/shard_map/ppermute | solution.py:366
  1773.3 59.4 %collective-permute-start.112 = (bf16[512,2240]{0,1:T(8,128)(2,1)}, bf16[512,2240]{0,1:T(8,128)(2,1)}, u32[]{:S(2)}, u32[]{:S(2)}) collective-permute-start(bf16[512,2240]{0,1:T(8,128)(2,1)} %fusion.21), channel_id=1, source_target_pairs={{0,1},{1,0},{2,3},{3,2},{4,5},{5,4},{6,7},{7,6},{8,9},{9,8},{10,11... | collective-permute-start | bytes 6881288 | tf_op jit(solution)/shard_map/ppermute | solution.py:366
  (331 other events, 7018.2 us)
Sparse Core Ops, SparseCore 0:
  793.0 149.1 reduce-scatter.6
  947.9 227.7 reduce-scatter.4
  1203.0 153.7 reduce-scatter.8
  1374.8 206.4 reduce-scatter.10

commit v3 on v2

--- a/solution.py
+++ b/solution.py
@@ -286,6 +286,29 @@
     )(index, *[array for array, _ in sources])
 
 
+def pack_kernel(index_ref, *refs):
+    out, at = refs[-1], 0
+    for ref in refs[:-1]:
+        out[:, at : at + ref.shape[1]] = ref[...]
+        at += ref.shape[1]
+
+
+def pack(index, parts, rows):
+    count, width = index.shape[0], sum(part.shape[1] for part in parts)
+    return pl.pallas_call(
+        pack_kernel,
+        grid_spec=pltpu.PrefetchScalarGridSpec(
+            num_scalar_prefetch=1,
+            grid=(count,),
+            in_specs=[pl.BlockSpec((rows, part.shape[1]), lambda i, index_ref: (index_ref[i], 0)) for part in parts],
+            out_specs=pl.BlockSpec((rows, width), lambda i, index_ref: (i, 0)),
+        ),
+        out_shape=struct((count * rows, width), BF16),
+        compiler_params=pltpu.CompilerParams(vmem_limit_bytes=VMEM_LIMIT),
+        cost_estimate=pl.CostEstimate(flops=0, bytes_accessed=count * rows * width * 4, transcendentals=0),
+    )(index, *parts)
+
+
 def scatter_phases(first, second, done):
     size = lax.axis_size(DP)
     ahead = size // 2
@@ -296,12 +319,8 @@
     n_b = sum(part.shape[1] for part in second)
 
     def across(start, count):
-        blocks = [
-            [lax.dynamic_slice_in_dim(part, chip_back(order[start + i], 1) * rows, rows, 0) for part in first]
-            for i in range(count)
-        ]
-        blocks = [jnp.concatenate(each, axis=1) if len(each) > 1 else each[0] for each in blocks]
-        return (jnp.concatenate(blocks, axis=0) if count > 1 else blocks[0], SEQ, 1)
+        index = jnp.stack([chip_back(order[start + i], 1).astype(jnp.int32) for i in range(count)])
+        return (pack(index, first, rows), SEQ, 1)
 
     def value(a, far, running, dtype):
         blocks = [(part, chip_back(a, 0)) for part in first]
@@ -532,17 +551,7 @@
     return result
 
 
-def conv_kernel(cols, z0, z1, top0, top1, bottom0, bottom1, w_ref, b_ref, out_ref, s0, s1):
-    tokens = z0.shape[0]
-    for z, top, bottom, scratch in ((z0, top0, bottom0, s0), (z1, top1, bottom1, s1)):
-        stage_columns(scratch, top[0], silu(z[...]).astype(BF16).astype(F32), bottom[0], cols)
-    for at, size in strips_of(tokens, cols):
-        first = taps(s0, w_ref[0], at, size, cols, False) + b_ref[0, 0:1]
-        second = taps(s1, w_ref[1], at, size, cols, False) + b_ref[1, 0:1]
-        out_ref[at : at + size] = (first * silu(second)).astype(BF16)
-
-
-def conv_back_kernel(cols, z0, z1, top0, top1, bottom0, bottom1, grad_ref, w_ref, b_ref, out0, out1, small_ref, s0, s1):
+def conv_kernel(cols, z0, z1, top0, top1, bottom0, bottom1, grad_ref, w_ref, b_ref, gated_ref, out0, out1, small_ref, s0, s1):
     tokens = z0.shape[0]
     for z, top, bottom, scratch in ((z0, top0, bottom0, s0), (z1, top1, bottom1, s1)):
         stage_columns(scratch, top[0], silu(z[...]).astype(BF16).astype(F32), bottom[0], cols)
@@ -552,9 +561,11 @@
         second = taps(s1, w_ref[1], at, size, cols, False) + b_ref[1, 0:1]
         grad = grad_ref[at : at + size]
         sigma = jax.nn.sigmoid(second)
-        slope = sigma * (1.0 + second * (1.0 - sigma))
+        gate = second * sigma
+        gated_ref[at : at + size] = (first * gate).astype(BF16)
+        slope = sigma + gate * (1.0 - sigma)
         for j, (part, scratch, out) in enumerate(
-            ((grad * second * sigma, s0, out0), (grad * first * slope, s1, out1))
+            ((grad * gate, s0, out0), (grad * first * slope, s1, out1))
         ):
             out[at : at + size] = part.astype(BF16)
             for row_tap in range(3):
@@ -691,24 +702,15 @@
             ],
         )
 
-    def conv(self, pre, top, bottom, conv_w, conv_b):
-        size = self.micro * self.tokens * self.hidden
-        data, weights = self.conv_specs()
-        return call(
-            functools.partial(conv_kernel, self.cols), (self.micro, self.units), data + weights,
-            self.tile(), struct((pre.shape[0], self.hidden), BF16), size * 20000, size * 10,
-            [self.scratch(), self.scratch()],
-        )(pre, pre, top, top, bottom, bottom, conv_w, conv_b)
-
-    def conv_back(self, pre, top, bottom, grad, conv_w, conv_b):
+    def conv(self, pre, top, bottom, grad, conv_w, conv_b):
         size = self.micro * self.tokens * self.hidden
         data, weights = self.conv_specs()
         one = struct((pre.shape[0], self.hidden), BF16)
         return call(
-            functools.partial(conv_back_kernel, self.cols), (self.micro, self.units),
+            functools.partial(conv_kernel, self.cols), (self.micro, self.units),
             data + [self.tile()] + weights,
-            [self.tile(), self.tile(), pl.BlockSpec((1, 24, LANES), lambda m, g: (m, 0, g))],
-            [one, one, struct((self.micro, 24, self.hidden), F32)], size * 40000, size * 16,
+            [self.tile()] * 3 + [pl.BlockSpec((1, 24, LANES), lambda m, g: (m, 0, g))],
+            [one, one, one, struct((self.micro, 24, self.hidden), F32)], size * 40000, size * 16,
             [self.scratch(), self.scratch()],
         )(pre, pre, top, top, bottom, bottom, grad, conv_w, conv_b)
 
@@ -852,6 +854,9 @@
     ffn_terms, backs, smalls, ffn_grads = [], [], [], []
     for at in range(2):
         w_up, w_down = wire.need(unit_rows[at])
+        if at == 1:
+            early, _ = lax.optimization_barrier((early, w_down))
+            ffn_grads.append([part for parts in early for part in scatter(None, [parts], [])])
         bias = jnp.concatenate([units(up_b[0:1], at), units(up_b[1:2], at)], axis=1)
         filters = jnp.stack([units(conv_w[:, j], at) for j in range(2)])
         filter_bias = jnp.stack([units(conv_b[j : j + 1], at) for j in range(2)])
@@ -862,17 +867,13 @@
         gated_grad = dot(ffn_out_grad, w_down, 1, 0)
         if at == 0:
             pre, top, bottom = wire.step((pre, top, bottom))
-        gated = kernels.conv(pre, top, bottom, filters, filter_bias)
-        if at == 0:
-            gated_grad = wire.step(gated_grad)
-        conv_grad0, conv_grad1, small = kernels.conv_back(pre, top, bottom, gated_grad, filters, filter_bias)
+        gated, conv_grad0, conv_grad1, small = kernels.conv(pre, top, bottom, gated_grad, filters, filter_bias)
         edges = [grad.reshape(micro, tokens, half) for grad in (conv_grad0, conv_grad1)]
         edges = jnp.concatenate(
             [jnp.concatenate([grad[:, :cols], grad[:, -cols:]], axis=1) for grad in edges], axis=2
         )
         top_grad, bottom_grad = halos(edges, cols)
         down_parts = weight_grad(ffn_out_grad, gated)
-        down_sum = scatter(None, [down_parts], []) if at == 0 else []
         if at == 0:
             top_grad, bottom_grad = wire.step((top_grad, bottom_grad))
         up_low0, up_low1, bias_grad = kernels.act_back(
@@ -885,13 +886,13 @@
         up_low = jnp.concatenate([up_low0, up_low1], axis=1)
         up_parts = weight_grad(normed_ffn, up_low)
         if at == 0:
-            ffn_grads.append(scatter(None, [up_parts], []) + down_sum)
+            early = (up_parts, down_parts)
+            normed_ffn, _ = lax.optimization_barrier((normed_ffn, early))
         else:
             ffn_grads.append(scatter(wire, [up_parts], [down_parts]))
+            up_low, _ = lax.optimization_barrier((up_low, (up_parts, down_parts)))
         ffn_terms.append((gated, w_down, 1))
         backs.append((up_low, w_up, 1))
-    small = []
-    wire.join(butterfly_phases(jnp.concatenate(smalls, axis=1), (SEQ, DP), jnp.add, small))
 
     backs[1] = (wire.step(up_low, True), *backs[1][1:])
     normed_ffn_grad = core_total(backs)
@@ -900,25 +901,27 @@
     cross_grad = both(wire.step(resid_b_grad, True).astype(BF16))
     attended_grad = dot(cross_grad, w_co, 1, 0).astype(BF16)
     query_grad, key_grad, value_grad = kernels.cross_back(lengths, cross_query, text_proj, wire.step(attended_grad, True))
-    (query_grad, key_grad, value_grad), _ = lax.optimization_barrier(((query_grad, key_grad, value_grad), ffn_grads[0]))
+    (query_grad, key_grad, value_grad), _ = lax.optimization_barrier(((query_grad, key_grad, value_grad), ffn_grads[0][1]))
     query_grad, key_grad, value_grad = wire.step((query_grad, key_grad, value_grad), True)
     cross_out_parts = weight_grad(cross_grad, attended)
     cross_kv_parts = weight_grad(caption, jnp.concatenate([key_grad, value_grad], axis=1))
     text_grads = scatter(None, [cross_kv_parts], [])
-    text_grads += scatter(None, [cross_out_parts], [])
     resid_a_grad = resid_b_grad + core_total([(wire.step(query_grad, True), w_cq, 1)])
     cross_q_parts = weight_grad(cross_input, query_grad)
     gate_a_grad = jnp.sum(resid_a_grad * self_term, axis=0)
     self_grad = both((gate_a * resid_a_grad).astype(BF16))
     mixed_grad = dot(wire.step(self_grad, True), w_so, 1, 0)
+    mixed_grad, _ = lax.optimization_barrier((mixed_grad, ffn_grads[0][0]))
     q_low, state_grad = kernels.mix_back(queries, states, wire.step(mixed_grad, True))
     self_out_parts = weight_grad(self_grad, mixed)
     state_grad = butterfly(state_grad, (SEQ,), jnp.add)
-    token_grads = scatter(wire, [cross_q_parts, weight_grad(normed, q_low)], [self_out_parts])
+    small = []
+    wire.join(butterfly_phases(jnp.concatenate(smalls, axis=1), (SEQ, DP), jnp.add, small))
+    token_grads = scatter(wire, [cross_q_parts, weight_grad(normed, q_low), cross_out_parts], [self_out_parts])
     kv_low = kernels.states_back(keys_values, wire.step(state_grad, True))
-    key_parts, value_parts = [weight_grad(normed, kv_low[:, j * width : (j + 1) * width]) for j in range(2)]
-    kv_grads = scatter(wire, [key_parts], [value_parts])
-    kv_low, _ = lax.optimization_barrier((wire.step(kv_low, True), text_grads))
+    kv_parts = weight_grad(normed, kv_low)
+    kv_low, _ = lax.optimization_barrier((wire.step(kv_low, True), (text_grads, kv_parts)))
+    kv_grads = scatter(None, [kv_parts], [])
     normed_grad = core_total([(q_low, w_q, 1), (kv_low, w_kv, 1)])
     resid_part, shift_a_grad, scale_a_grad = normalise_back(resid_in, wire.step(normed_grad, True), scale_a)
     latent_grad = resid_a_grad + resid_part
@@ -939,15 +942,14 @@
     mod_grad = lax.dot_general(
         mod_grad, pick.astype(F32), (((1,), (1,)), ((), ())), precision=lax.Precision.HIGHEST
     )
-    table_grads = []
-    wire.join(butterfly_phases(butterfly(mod_grad, (TP,), jnp.add), (SEQ, DP), jnp.add, table_grads))
+    table_grad = butterfly(mod_grad, (TP, SEQ, DP), jnp.add)
     wire.finish()
-    (table_grad,), (head_peaks,), (small,) = table_grads, head_peaks, small
+    (head_peaks,), (small,) = head_peaks, small
     down_grad = jnp.concatenate([down for _, down in ffn_grads], axis=1)
     up_grad = jnp.concatenate(
         [up[:, j * half : (j + 1) * half] for j in range(2) for up, _ in ffn_grads], axis=1
     )
-    (cross_kv_grad, cross_out_grad), (cross_q_grad, q_grad, self_out_grad) = text_grads, token_grads
+    (cross_kv_grad,), (cross_q_grad, q_grad, cross_out_grad, self_out_grad) = text_grads, token_grads
 
     factor = jnp.repeat(jnp.sqrt(CLIP_TAU / jnp.maximum(head_peaks, CLIP_TAU)), HEAD_DIM)
 
@@ -963,7 +965,7 @@
         output,
         latents_grad,
         table_grad,
-        jnp.stack([heads(grad) for grad in [q_grad] + kv_grads]),
+        jnp.concatenate([heads(q_grad)[None], cut(kv_grads[0], 2, width, heads_width)], axis=0),
         heads(self_out_grad).T,
         heads(cross_q_grad),
         cut(cross_kv_grad, 2, width, heads_width),

time: 1910 us -> 2020 us (1.058)
  waiting for transfers between devices: 516 us -> 736 us
  Pallas kernels: 447 us -> 412 us
  local copies, waits for them, and re-layouts: 149 us -> 119 us
    ppermute x101 -> x89, waiting for transfers between devices: 349 us -> 515 us  [shift(): lax.ppermute(values, axis, [(cycle[i], cycle[(i + step) % size]) for i in...]
    ppermute x3 -> x7, waiting for transfers between devices: 0.01 us -> 72.5 us  [butterfly(): lax.ppermute(values, axis, [(i, i ^ bit) for i in range(size)])]
    pallas_call x2 -> x8, Pallas kernels: 53.2 us -> 20.6 us  [pack(): pl.pallas_call(pack_kernel, grid_spec=pltpu.PrefetchScalarGridSpec(num_sc...]
    pallas_call x24 -> x16, Pallas kernels: 85.6 us -> 67.8 us  [combine(): pl.pallas_call(functools.partial(combine_kernel, near_count, len(blocks)...]
    ppermute x101 -> x89, starting transfers between devices: 104 us -> 94.5 us  [shift(): lax.ppermute(values, axis, [(cycle[i], cycle[(i + step) % size]) for i in...]
    unnamed x428 -> x385, local copies, waits for them, and re-layouts: 40.8 us -> 31.6 us
    ppermute x12 -> x8, waiting for transfers between devices: 154 us -> 149 us  [shift(): return lax.ppermute(values, axis, step)]
    dot_general x45 -> x44, matrix products: 496 us -> 496 us  [dot(): lax.dot_general(left, right, (((left_dim,), (right_dim,)), ((), ())), pre...]
  transfers between devices with their start and end apart: 142 -> 130, of which waited for: 51 -> 49; matrix products, arithmetic and copies ran while one was open for 38% -> 33% of each run, Pallas kernels for 24% -> 18%
where the time goes in v3:
time: 2020 us; the launch traced here: 2010 us
  waiting for transfers between devices  736 us (36%)
  matrix products  510 us (25%)
  Pallas kernels  412 us (20%)
  starting transfers between devices  134 us (7%)
  local copies, waits for them, and re-layouts  119 us (6%)
  other arithmetic  83.4 us (4%)
    ppermute x89, waiting for transfers between devices, shift(): lax.ppermute(values, axis, [(cycle[i], cycle[(i + step) % size]) for i in...  515 us
    dot_general x44, matrix products, dot(): lax.dot_general(left, right, (((left_dim,), (right_dim,)), ((), ())), pre...  496 us
    ppermute x8, waiting for transfers between devices, shift(): return lax.ppermute(values, axis, step)  149 us
    ppermute x89, starting transfers between devices, shift(): lax.ppermute(values, axis, [(cycle[i], cycle[(i + step) % size]) for i in...  94.5 us
    ppermute x7, waiting for transfers between devices, butterfly(): lax.ppermute(values, axis, [(i, i ^ bit) for i in range(size)])  72.5 us
    pallas_call x5, Pallas kernels, assemble(): pl.pallas_call(functools.partial(assemble_kernel, moves, rows, len(arrays...  70.7 us
    pallas_call x16, Pallas kernels, combine(): pl.pallas_call(functools.partial(combine_kernel, near_count, len(blocks)...  67.8 us
    pallas_call x2, Pallas kernels, conv(): call(functools.partial(conv_kernel, self.cols), (self.micro, self.units),...  53.5 us
  transfers between devices with their start and end apart: 130, of which 49 were waited for; matrix products, arithmetic and copies ran while one was open for 33% of the time, Pallas kernels for 18%

profile of v3, /device:TPU:0, one launch (start us, length us, event | category | flops | bytes accessed | tf_op | source)
XLA Modules:
  0.0 2012.6 jit_solution(3915847302841464004)
XLA Ops:
  23.3 26.5 %collective-permute-done.2.refs_2_ = bf16[144,4608]{1,0:T(8,128)(2,1)S(1)} collective-permute-done((bf16[144,4608]{1,0:T(8,128)(2,1)S(1)}, bf16[144,4608]{1,0:T(8,128)(2,1)S(1)}, u32[]{:S(2)}, u32[]{:S(2)}) %collective-permute-start.2) | collective-permute-done | bytes 1327136 | tf_op jit(solution)/shard_map/ppermute | solution.py:63
  127.0 29.3 %collective-permute-done.12 = bf16[144,1152]{1,0:T(8,128)(2,1)S(1)} collective-permute-done((bf16[144,1152]{1,0:T(8,128)(2,1)S(1)}, bf16[144,1152]{1,0:T(8,128)(2,1)S(1)}, u32[]{:S(2)}, u32[]{:S(2)}) %collective-permute-start.12) | collective-permute-done | bytes 331808 | tf_op jit(solution)/shard_map/ppermute | solution.py:63
  338.6 24.7 %collective-permute-done.35.refs_4_ = bf16[144,4608]{1,0:T(8,128)(2,1)S(1)} collective-permute-done((bf16[144,4608]{1,0:T(8,128)(2,1)S(1)}, bf16[144,4608]{1,0:T(8,128)(2,1)S(1)}, u32[]{:S(2)}, u32[]{:S(2)}) %collective-permute-start.35) | collective-permute-done | bytes 1327136 | tf_op jit(solution)/shard_map/ppermute | solution.py:63
  401.1 31.3 %collective-permute-done.42 = bf16[144,1408]{1,0:T(8,128)(2,1)S(1)} collective-permute-done((bf16[144,1408]{1,0:T(8,128)(2,1)S(1)}, bf16[144,1408]{1,0:T(8,128)(2,1)S(1)}, u32[]{:S(2)}, u32[]{:S(2)}) %collective-permute-start.42) | collective-permute-done | bytes 405536 | tf_op jit(solution)/shard_map/ppermute | solution.py:63
  484.2 34.4 %shard_map.276 = (bf16[1024,1152]{1,0:T(8,128)(2,1)S(1)}, f32[2,9,8,128]{3,2,1,0:T(8,128)S(1)}) custom-call(s32[2]{0:T(128)S(1)} %broadcast_select_fusion.length_ref, bf16[1024,1152]{1,0:T(8,128)(2,1)S(1)} %convolution_convert_fusion.15.query_ref, bf16[608,2304]{1,0:T(8,128)(2,1)} %convolution_convert_fusion.10.key_ref.value_ref, ...), custom_call_target="tpu_custom_call" | custom-call | flops 23592960000 | bytes 7077888 | tf_op jit(solution)/shard_map/pallas_call | solution.py:670
  546.8 23.1 %collective-permute-done.54 = f32[35]{0:T(128)S(1)} collective-permute-done((f32[35]{0:T(128)S(1)}, f32[35]{0:T(128)S(1)}, u32[]{:S(2)}, u32[]{:S(2)}) %collective-permute-start.54) | collective-permute-done | bytes 172 | tf_op jit(solution)/shard_map/ppermute | solution.py:60
  587.3 21.6 %collective-permute-done.56.refs_8_ = bf16[144,5632]{1,0:T(8,128)(2,1)S(1)} collective-permute-done((bf16[144,5632]{1,0:T(8,128)(2,1)S(1)}, bf16[144,5632]{1,0:T(8,128)(2,1)S(1)}, u32[]{:S(2)}, u32[]{:S(2)}) %collective-permute-start.56) | collective-permute-done | bytes 1622048 | tf_op jit(solution)/shard_map/ppermute | solution.py:63
  621.1 32.2 %collective-permute-done.61 = f32[35]{0:T(128)S(1)} collective-permute-done((f32[35]{0:T(128)S(1)}, f32[35]{0:T(128)S(1)}, u32[]{:S(2)}, u32[]{:S(2)}) %collective-permute-start.61) | collective-permute-done | bytes 172 | tf_op jit(solution)/shard_map/ppermute | solution.py:60
  672.6 22.0 %convolution_add_fusion.1.z0.z1 = f32[1024,2816]{1,0:T(8,128)} fusion(bf16[1024,2304]{1,0:T(8,128)(2,1)S(1)} %pad_maximum_fusion.2, bf16[2304,2816]{1,0:T(8,128)(2,1)} %get-tuple-element.248, f32[2816]{0:T(1024)S(1)} %maximum_reduce_fusion), kind=kOutput, calls=%fused_computation.29 | convolution fusion | flops 13290438656 | bytes 29240320 | tf_op jit(solution)/shard_map/dot_general | solution.py:27
  705.1 31.6 %collective-permute-done.67 = f32[35]{0:T(128)S(1)} collective-permute-done((f32[35]{0:T(128)S(1)}, f32[35]{0:T(128)S(1)}, u32[]{:S(2)}, u32[]{:S(2)}) %collective-permute-start.67) | collective-permute-done | bytes 172 | tf_op jit(solution)/shard_map/ppermute | solution.py:60
  750.3 23.8 %collective-permute-done.70.refs_3_ = bf16[288,2816]{1,0:T(8,128)(2,1)} collective-permute-done((bf16[288,2816]{1,0:T(8,128)(2,1)S(1)}, bf16[288,2816]{1,0:T(8,128)(2,1)}, u32[]{:S(2)}, u32[]{:S(2)}) %collective-permute-start.70) | collective-permute-done | bytes 1622048 | tf_op jit(solution)/shard_map/ppermute | solution.py:63
  774.1 26.7 %shard_map.278 = (bf16[1024,1408]{1,0:T(8,128)(2,1)S(1)}, bf16[1024,1408]{1,0:T(8,128)(2,1)}, bf16[1024,1408]{1,0:T(8,128)(2,1)}, f32[2,24,1408]{2,1,0:T(8,128)S(1)}) custom-call(f32[1024,2816]{1,0:T(8,128)} %convolution_add_fusion.1.z0.z1, f32[1024,2816]{1,0:T(8,128)} %convolution_add_fusion.1.z0.z1, ...), custom_call_target="tpu_custom_call" | custom-call | flops 57671680000 | bytes 23068672 | tf_op jit(solution)/shard_map/pallas_call | solution.py:709
  853.5 21.4 %shard_map.279 = (bf16[1024,1408]{1,0:T(8,128)(2,1)S(1)}, bf16[1024,1408]{1,0:T(8,128)(2,1)}, f32[2,8,1408]{2,1,0:T(8,128)S(1)}) custom-call(f32[1024,2816]{1,0:T(8,128)} %convolution_add_fusion.1.z0.z1, f32[1024,2816]{1,0:T(8,128)} %convolution_add_fusion.1.z0.z1, bf16[1024,1408]{1,0:T(8,128)(2,1)} %get-tuple-element.258.grad0, ...), custom_call_target="tpu_custom_call" | custom-call | flops 57671680000 | bytes 28835840 | tf_op jit(solution)/shard_map/pallas_call | solution.py:721
  967.0 26.9 %shard_map.281 = (bf16[1024,1408]{1,0:T(8,128)(2,1)S(1)}, bf16[1024,1408]{1,0:T(8,128)(2,1)}, bf16[1024,1408]{1,0:T(8,128)(2,1)}, f32[2,24,1408]{2,1,0:T(8,128)S(1)}) custom-call(f32[1024,2816]{1,0:T(8,128)} %copy-done.140, f32[1024,2816]{1,0:T(8,128)} %copy-done.140, bf16[2,32,2816]{2,1,0:T(8,128)(2,1)S(1)} %collective-permute-done.80.top0.top1, ...), custom_call_target="tpu_custom_call" | custom-call | flops 57671680000 | bytes 23068672 | tf_op jit(solution)/shard_map/pallas_call | solution.py:709
  1014.7 21.6 %shard_map.282 = (bf16[1024,1408]{1,0:T(8,128)(2,1)S(1)}, bf16[1024,1408]{1,0:T(8,128)(2,1)}, f32[2,8,1408]{2,1,0:T(8,128)S(1)}) custom-call(f32[1024,2816]{1,0:T(8,128)} %copy-done.140, f32[1024,2816]{1,0:T(8,128)} %copy-done.140, bf16[1024,1408]{1,0:T(8,128)(2,1)} %get-tuple-element.279.grad0, bf16[1024,1408]{1,0:T(8,128)(2,1)} %get-tuple-element.280.grad1, ...), custom_call_target="tpu_custom_call" | custom-call | flops 57671680000 | bytes 28835840 | tf_op jit(solution)/shard_map/pallas_call | solution.py:721
  1133.5 46.0 %collective-permute-done.84.refs_3_ = bf16[288,2816]{1,0:T(8,128)(2,1)S(1)} collective-permute-done((bf16[288,2816]{1,0:T(8,128)(2,1)S(1)}, bf16[288,2816]{1,0:T(8,128)(2,1)S(1)}, u32[]{:S(2)}, u32[]{:S(2)}) %collective-permute-start.84) | collective-permute-done | bytes 1622048 | tf_op jit(solution)/shard_map/ppermute | solution.py:63
  1198.2 52.6 %shard_map.294 = (bf16[1024,1152]{1,0:T(8,128)(2,1)S(1)}, bf16[608,1152]{1,0:T(8,128)(2,1)S(1)}, bf16[608,1152]{1,0:T(8,128)(2,1)S(1)}) custom-call(s32[2]{0:T(128)S(1)} %copy-done.53, bf16[1024,1152]{1,0:T(8,128)(2,1)} %copy-done.68, bf16[608,2304]{1,0:T(8,128)(2,1)} %convolution_convert_fusion.10.key_ref.value_ref, ...), custom_call_target="tpu_custom_call" | custom-call | flops 58982400000 | bytes 7077888 | tf_op jit(solution)/shard_map/pallas_call | solution.py:681
  1283.2 38.2 %collective-permute-done.88.refs_3_ = bf16[288,2816]{1,0:T(8,128)(2,1)S(1)} collective-permute-done((bf16[288,2816]{1,0:T(8,128)(2,1)S(1)}, bf16[288,2816]{1,0:T(8,128)(2,1)S(1)}, u32[]{:S(2)}, u32[]{:S(2)}) %collective-permute-start.88) | collective-permute-done | bytes 1622048 | tf_op jit(solution)/shard_map/ppermute | solution.py:63
  1381.8 23.3 %collective-permute-done.91.refs_3_ = bf16[288,2816]{1,0:T(8,128)(2,1)S(1)} collective-permute-done((bf16[288,2816]{1,0:T(8,128)(2,1)S(1)}, bf16[288,2816]{1,0:T(8,128)(2,1)S(1)}, u32[]{:S(2)}, u32[]{:S(2)}) %collective-permute-start.91) | collective-permute-done | bytes 1622048 | tf_op jit(solution)/shard_map/ppermute | solution.py:63
  1405.1 30.9 %collective-permute-done.92.refs_4_ = bf16[144,5632]{1,0:T(8,128)(2,1)S(1)} collective-permute-done((bf16[144,5632]{1,0:T(8,128)(2,1)S(1)}, bf16[144,5632]{1,0:T(8,128)(2,1)S(1)}, u32[]{:S(2)}, u32[]{:S(2)}) %collective-permute-start.92) | collective-permute-done | bytes 1622048 | tf_op jit(solution)/shard_map/ppermute | solution.py:63
  1519.9 55.9 %collective-permute-done.112 = f32[2,9,40,128]{3,2,1,0:T(8,128)S(1)} collective-permute-done((f32[2,9,40,128]{3,2,1,0:T(8,128)S(1)}, f32[2,9,40,128]{3,2,1,0:T(8,128)S(1)}, u32[]{:S(2)}, u32[]{:S(2)}) %collective-permute-start.112) | collective-permute-done | bytes 368672 | tf_op jit(solution)/shard_map/ppermute | solution.py:379
  1575.8 25.9 %shard_map.304 = bf16[1024,2304]{1,0:T(8,128)(2,1)S(1)} custom-call(f32[1024,2304]{1,0:T(8,128)} %fusion.105.key_ref.value_ref, f32[1024,2304]{1,0:T(8,128)} %fusion.105.key_ref.value_ref, f32[2,9,40,128]{3,2,1,0:T(8,128)S(1)} %add.1292.state_ref), custom_call_target="tpu_custom_call" | custom-call | flops 1769472000 | bytes 23592960 | tf_op jit(solution)/shard_map/pallas_call | solution.py:656
  1693.2 27.3 %collective-permute-done.104.refs_6_ = bf16[144,5760]{1,0:T(8,128)(2,1)} collective-permute-done((bf16[144,5760]{1,0:T(8,128)(2,1)}, bf16[144,5760]{1,0:T(8,128)(2,1)}, u32[]{:S(2)}, u32[]{:S(2)}) %collective-permute-start.104) | collective-permute-done | bytes 1658912 | tf_op jit(solution)/shard_map/ppermute | solution.py:63
  1755.9 54.0 %collective-permute-done.106 = f32[22,2816]{1,0:T(8,128)S(1)} collective-permute-done((f32[22,2816]{1,0:T(8,128)S(1)}, f32[22,2816]{1,0:T(8,128)S(1)}, u32[]{:S(2)}, u32[]{:S(2)}) %collective-permute-start.106) | collective-permute-done | bytes 247840 | tf_op jit(solution)/shard_map/ppermute | solution.py:60
  (948 shorter events, 1244.3 us)
Async XLA Ops:
  7.2 1247.3 %reduce-scatter.5.cloned.1.call-start = ((), (), s32[]{:S(2)}) async-start(), calls=%async_computation.4 | async-start | bytes 6893568 | tf_op jit(solution)/shard_map/reduce_scatter | solution.py:369
  162.9 64.4 %collective-permute-start = (bf16[512,2304]{1,0:T(8,128)(2,1)}, bf16[512,2304]{1,0:T(8,128)(2,1)}, u32[]{:S(2)}, u32[]{:S(2)}) collective-permute-start(bf16[512,2304]{1,0:T(8,128)(2,1)} %add_convert_fusion.2), channel_id=1, source_target_pairs={{0,1},{1,0},{2,3},{3,2},{4,5},{5,4},{6,7},{7,6},{8,9},{9,8},{10,11... | collective-permute-start | bytes 7077896 | tf_op jit(solution)/shard_map/ppermute | solution.py:385
  585.1 85.5 %collective-permute-start.51 = (bf16[512,2304]{1,0:T(8,128)(2,1)S(1)}, bf16[512,2304]{1,0:T(8,128)(2,1)}, u32[]{:S(2)}, u32[]{:S(2)}) collective-permute-start(bf16[512,2304]{1,0:T(8,128)(2,1)S(1)} %add_convert_fusion.1), channel_id=1, source_target_pairs={{0,1},{1,0},{2,3},{3,2},{4,5},{5,4},{6,7},{7,6},{8,9},{9,8},{10,11... | collective-permute-start | bytes 7077896 | tf_op jit(solution)/shard_map/ppermute | solution.py:385
  928.9 543.4 %reduce-scatter.7.cloned.1.call-start = ((), (), s32[]{:S(2)}) async-start(), calls=%async_computation.5 | async-start | bytes 13787136 | tf_op jit(solution)/shard_map/reduce_scatter | solution.py:369
  954.3 1008.1 %reduce-scatter.11.cloned.1.call-start = ((), (), s32[]{:S(2)}) async-start(), calls=%async_computation.7 | async-start | bytes 11280384 | tf_op jit(solution)/shard_map/reduce_scatter | solution.py:369
  1127.6 61.6 %collective-permute-start.94 = (bf16[512,2304]{1,0:T(8,128)(2,1)S(1)}, bf16[512,2304]{1,0:T(8,128)(2,1)}, u32[]{:S(2)}, u32[]{:S(2)}) collective-permute-start(bf16[512,2304]{1,0:T(8,128)(2,1)S(1)} %convert_element_type.222), channel_id=1, source_target_pairs={{0,1},{1,0},{2,3},{3,2},{4,5},{5,4},{6,7},{7,6},{8,9},{9,8},{10,11... | collective-permute-start | bytes 7077896 | tf_op jit(solution)/shard_map/ppermute | solution.py:385
  1186.9 69.6 %collective-permute-start.85 = (bf16[288,2816]{1,0:T(8,128)(2,1)}, bf16[288,2816]{1,0:T(8,128)(2,1)S(1)}, u32[]{:S(2)}, u32[]{:S(2)}) collective-permute-start(bf16[288,2816]{1,0:T(8,128)(2,1)} %shard_map.286), channel_id=1, source_target_pairs={{0,2},{2,0},{1,3},{3,1},{4,6},{6,4},{5,7},{7,5},{8,10},{10,8},{9,1... | collective-permute-start | bytes 4866056 | tf_op jit(solution)/shard_map/ppermute | solution.py:63
  1187.2 69.2 %collective-permute-start.86 = (bf16[144,5632]{1,0:T(8,128)(2,1)}, bf16[144,5632]{1,0:T(8,128)(2,1)}, u32[]{:S(2)}, u32[]{:S(2)}) collective-permute-start(bf16[144,5632]{1,0:T(8,128)(2,1)} %shard_map.284), channel_id=1, source_target_pairs={{0,4},{8,0},{16,8},{24,16},{28,24},{20,28},{12,20},{4,12},{1,5},{9... | collective-permute-start | bytes 4866056 | tf_op jit(solution)/shard_map/ppermute | solution.py:63
  1188.9 67.6 %collective-permute-start.87 = (bf16[144,5632]{1,0:T(8,128)(2,1)S(1)}, bf16[144,5632]{1,0:T(8,128)(2,1)}, u32[]{:S(2)}, u32[]{:S(2)}) collective-permute-start(bf16[144,5632]{1,0:T(8,128)(2,1)S(1)} %shard_map.285), channel_id=1, source_target_pairs={{0,8},{8,16},{16,24},{24,28},{28,20},{20,12},{12,4},{4,0},{1,9},{9... | collective-permute-start | bytes 4866056 | tf_op jit(solution)/shard_map/ppermute | solution.py:63
  1269.9 730.9 %reduce-scatter.9.cloned.1.call-start = ((), (), s32[]{:S(2)}) async-start(), calls=%async_computation.6 | async-start | bytes 11280384 | tf_op jit(solution)/shard_map/reduce_scatter | solution.py:369
  1361.0 75.1 %collective-permute-start.92 = (bf16[144,5632]{1,0:T(8,128)(2,1)S(1)}, bf16[144,5632]{1,0:T(8,128)(2,1)S(1)}, u32[]{:S(2)}, u32[]{:S(2)}) collective-permute-start(bf16[144,5632]{1,0:T(8,128)(2,1)S(1)} %shard_map.290), channel_id=1, source_target_pairs={{0,4},{8,0},{16,8},{24,16},{28,24},{20,28},{12,20},{4,12},{1,5},{9... | collective-permute-start | bytes 4866056 | tf_op jit(solution)/shard_map/ppermute | solution.py:63
  1372.3 78.0 %collective-permute-start.96 = (bf16[512,2304]{1,0:T(8,128)(2,1)S(1)}, bf16[512,2304]{1,0:T(8,128)(2,1)}, u32[]{:S(2)}, u32[]{:S(2)}) collective-permute-start(bf16[512,2304]{1,0:T(8,128)(2,1)S(1)} %get-tuple-element.438), channel_id=1, source_target_pairs={{0,1},{1,0},{2,3},{3,2},{4,5},{5,4},{6,7},{7,6},{8,9},{9,8},{10,11... | collective-permute-start | bytes 7077896 | tf_op jit(solution)/shard_map/ppermute | solution.py:385
  1381.8 123.7 %collective-permute-start.97 = (bf16[144,5632]{1,0:T(8,128)(2,1)}, bf16[144,5632]{1,0:T(8,128)(2,1)S(1)}, u32[]{:S(2)}, u32[]{:S(2)}) collective-permute-start(bf16[144,5632]{1,0:T(8,128)(2,1)} %shard_map.291), channel_id=1, source_target_pairs={{0,8},{8,16},{16,24},{24,28},{28,20},{20,12},{12,4},{4,0},{1,9},{9... | collective-permute-start | bytes 4866056 | tf_op jit(solution)/shard_map/ppermute | solution.py:63
  1517.8 131.8 %collective-permute-start.100 = (bf16[288,3456]{1,0:T(8,128)(2,1)}, bf16[288,3456]{1,0:T(8,128)(2,1)S(1)}, u32[]{:S(2)}, u32[]{:S(2)}) collective-permute-start(bf16[288,3456]{1,0:T(8,128)(2,1)} %shard_map.296), channel_id=1, source_target_pairs={{0,2},{2,0},{1,3},{3,1},{4,6},{6,4},{5,7},{7,5},{8,10},{10,8},{9,1... | collective-permute-start | bytes 5971976 | tf_op jit(solution)/shard_map/ppermute | solution.py:63
  1518.3 124.8 %collective-permute-start.99 = (bf16[144,5632]{1,0:T(8,128)(2,1)}, bf16[144,5632]{1,0:T(8,128)(2,1)}, u32[]{:S(2)}, u32[]{:S(2)}) collective-permute-start(bf16[144,5632]{1,0:T(8,128)(2,1)} %shard_map.293), channel_id=1, source_target_pairs={{0,4},{8,0},{16,8},{24,16},{28,24},{20,28},{12,20},{4,12},{1,5},{9... | collective-permute-start | bytes 4866056 | tf_op jit(solution)/shard_map/ppermute | solution.py:63
  1667.3 61.7 %collective-permute-start.102 = (bf16[288,3456]{1,0:T(8,128)(2,1)}, bf16[288,3456]{1,0:T(8,128)(2,1)S(1)}, u32[]{:S(2)}, u32[]{:S(2)}) collective-permute-start(bf16[288,3456]{1,0:T(8,128)(2,1)} %shard_map.300), channel_id=1, source_target_pairs={{0,2},{2,0},{1,3},{3,1},{4,6},{6,4},{5,7},{7,5},{8,10},{10,8},{9,1... | collective-permute-start | bytes 5971976 | tf_op jit(solution)/shard_map/ppermute | solution.py:63
  1668.9 64.1 %collective-permute-start.103 = (bf16[144,5760]{1,0:T(8,128)(2,1)}, bf16[144,5760]{1,0:T(8,128)(2,1)}, u32[]{:S(2)}, u32[]{:S(2)}) collective-permute-start(bf16[144,5760]{1,0:T(8,128)(2,1)} %shard_map.298), channel_id=1, source_target_pairs={{0,4},{8,0},{16,8},{24,16},{28,24},{20,28},{12,20},{4,12},{1,5},{9... | collective-permute-start | bytes 4976648 | tf_op jit(solution)/shard_map/ppermute | solution.py:63
  1736.8 73.1 %collective-permute-start.109 = (bf16[288,3456]{1,0:T(8,128)(2,1)S(1)}, bf16[288,3456]{1,0:T(8,128)(2,1)S(1)}, u32[]{:S(2)}, u32[]{:S(2)}) collective-permute-start(bf16[288,3456]{1,0:T(8,128)(2,1)S(1)} %copy-done.17), channel_id=1, source_target_pairs={{0,2},{2,0},{1,3},{3,1},{4,6},{6,4},{5,7},{7,5},{8,10},{10,8},{9,1... | collective-permute-start | bytes 5971976 | tf_op jit(solution)/shard_map/ppermute | solution.py:63
  1737.6 72.3 %collective-permute-start.108 = (bf16[144,5760]{1,0:T(8,128)(2,1)S(1)}, bf16[144,5760]{1,0:T(8,128)(2,1)S(1)}, u32[]{:S(2)}, u32[]{:S(2)}) collective-permute-start(bf16[144,5760]{1,0:T(8,128)(2,1)S(1)} %shard_map.302), channel_id=1, source_target_pairs={{0,8},{8,16},{16,24},{24,28},{28,20},{20,12},{12,4},{4,0},{1,9},{9... | collective-permute-start | bytes 4976648 | tf_op jit(solution)/shard_map/ppermute | solution.py:63
  1737.6 72.4 %collective-permute-start.107 = (bf16[144,5760]{1,0:T(8,128)(2,1)S(1)}, bf16[144,5760]{1,0:T(8,128)(2,1)S(1)}, u32[]{:S(2)}, u32[]{:S(2)}) collective-permute-start(bf16[144,5760]{1,0:T(8,128)(2,1)S(1)} %shard_map.301), channel_id=1, source_target_pairs={{0,4},{8,0},{16,8},{24,16},{28,24},{20,28},{12,20},{4,12},{1,5},{9... | collective-permute-start | bytes 4976648 | tf_op jit(solution)/shard_map/ppermute | solution.py:63
  1744.5 65.4 %collective-permute-start.106 = (f32[22,2816]{1,0:T(8,128)S(1)}, f32[22,2816]{1,0:T(8,128)S(1)}, u32[]{:S(2)}, u32[]{:S(2)}) collective-permute-start(f32[22,2816]{1,0:T(8,128)S(1)} %add.1287), channel_id=1, source_target_pairs={{0,8},{4,12},{8,0},{12,4},{16,24},{20,28},{24,16},{28,20},{1,9},{5... | collective-permute-start | bytes 743432 | tf_op jit(solution)/shard_map/ppermute | solution.py:60
  1839.0 89.3 %collective-permute-start.114 = (f32[512,2240]{0,1:T(8,128)}, f32[512,2240]{0,1:T(8,128)}, u32[]{:S(2)}, u32[]{:S(2)}) collective-permute-start(f32[512,2240]{0,1:T(8,128)} %fusion.16), channel_id=1, source_target_pairs={{0,1},{1,0},{2,3},{3,2},{4,5},{5,4},{6,7},{7,6},{8,9},{9,8},{10,11... | collective-permute-start | bytes 13762568 | tf_op jit(solution)/shard_map/ppermute | solution.py:385
  1913.0 62.1 %collective-permute-start.124 = (bf16[144,5760]{1,0:T(8,128)(2,1)}, bf16[144,5760]{1,0:T(8,128)(2,1)}, u32[]{:S(2)}, u32[]{:S(2)}) collective-permute-start(bf16[144,5760]{1,0:T(8,128)(2,1)} %shard_map.308), channel_id=1, source_target_pairs={{0,4},{8,0},{16,8},{24,16},{28,24},{20,28},{12,20},{4,12},{1,5},{9... | collective-permute-start | bytes 4976648 | tf_op jit(solution)/shard_map/ppermute | solution.py:63
  1924.5 66.0 %collective-permute-start.111 = (bf16[512,2240]{0,1:T(8,128)(2,1)}, bf16[512,2240]{0,1:T(8,128)(2,1)}, u32[]{:S(2)}, u32[]{:S(2)}) collective-permute-start(bf16[512,2240]{0,1:T(8,128)(2,1)} %fusion.21), channel_id=1, source_target_pairs={{0,1},{1,0},{2,3},{3,2},{4,5},{5,4},{6,7},{7,6},{8,9},{9,8},{10,11... | collective-permute-start | bytes 6881288 | tf_op jit(solution)/shard_map/ppermute | solution.py:385
  (297 other events, 7325.4 us)
Sparse Core Ops, SparseCore 0:
  929.1 147.6 reduce-scatter.4
  1082.4 242.7 reduce-scatter.6
  1332.0 229.3 reduce-scatter.10
  1619.6 224.9 reduce-scatter.8

commit v4 on v3

--- a/solution.py
+++ b/solution.py
@@ -286,29 +286,6 @@
     )(index, *[array for array, _ in sources])
 
 
-def pack_kernel(index_ref, *refs):
-    out, at = refs[-1], 0
-    for ref in refs[:-1]:
-        out[:, at : at + ref.shape[1]] = ref[...]
-        at += ref.shape[1]
-
-
-def pack(index, parts, rows):
-    count, width = index.shape[0], sum(part.shape[1] for part in parts)
-    return pl.pallas_call(
-        pack_kernel,
-        grid_spec=pltpu.PrefetchScalarGridSpec(
-            num_scalar_prefetch=1,
-            grid=(count,),
-            in_specs=[pl.BlockSpec((rows, part.shape[1]), lambda i, index_ref: (index_ref[i], 0)) for part in parts],
-            out_specs=pl.BlockSpec((rows, width), lambda i, index_ref: (i, 0)),
-        ),
-        out_shape=struct((count * rows, width), BF16),
-        compiler_params=pltpu.CompilerParams(vmem_limit_bytes=VMEM_LIMIT),
-        cost_estimate=pl.CostEstimate(flops=0, bytes_accessed=count * rows * width * 4, transcendentals=0),
-    )(index, *parts)
-
-
 def scatter_phases(first, second, done):
     size = lax.axis_size(DP)
     ahead = size // 2
@@ -319,8 +296,12 @@
     n_b = sum(part.shape[1] for part in second)
 
     def across(start, count):
-        index = jnp.stack([chip_back(order[start + i], 1).astype(jnp.int32) for i in range(count)])
-        return (pack(index, first, rows), SEQ, 1)
+        blocks = [
+            [lax.dynamic_slice_in_dim(part, chip_back(order[start + i], 1) * rows, rows, 0) for part in first]
+            for i in range(count)
+        ]
+        blocks = [jnp.concatenate(each, axis=1) if len(each) > 1 else each[0] for each in blocks]
+        return (jnp.concatenate(blocks, axis=0) if count > 1 else blocks[0], SEQ, 1)
 
     def value(a, far, running, dtype):
         blocks = [(part, chip_back(a, 0)) for part in first]
@@ -917,7 +898,7 @@
     state_grad = butterfly(state_grad, (SEQ,), jnp.add)
     small = []
     wire.join(butterfly_phases(jnp.concatenate(smalls, axis=1), (SEQ, DP), jnp.add, small))
-    token_grads = scatter(wire, [cross_q_parts, weight_grad(normed, q_low), cross_out_parts], [self_out_parts])
+    token_grads = scatter(wire, [cross_q_parts, weight_grad(normed, q_low)], [self_out_parts, cross_out_parts])
     kv_low = kernels.states_back(keys_values, wire.step(state_grad, True))
     kv_parts = weight_grad(normed, kv_low)
     kv_low, _ = lax.optimization_barrier((wire.step(kv_low, True), (text_grads, kv_parts)))
@@ -942,14 +923,15 @@
     mod_grad = lax.dot_general(
         mod_grad, pick.astype(F32), (((1,), (1,)), ((), ())), precision=lax.Precision.HIGHEST
     )
-    table_grad = butterfly(mod_grad, (TP, SEQ, DP), jnp.add)
+    table_grads = []
+    wire.join(butterfly_phases(butterfly(mod_grad, (TP,), jnp.add), (SEQ, DP), jnp.add, table_grads))
     wire.finish()
-    (head_peaks,), (small,) = head_peaks, small
+    (table_grad,), (head_peaks,), (small,) = table_grads, head_peaks, small
     down_grad = jnp.concatenate([down for _, down in ffn_grads], axis=1)
     up_grad = jnp.concatenate(
         [up[:, j * half : (j + 1) * half] for j in range(2) for up, _ in ffn_grads], axis=1
     )
-    (cross_kv_grad,), (cross_q_grad, q_grad, cross_out_grad, self_out_grad) = text_grads, token_grads
+    (cross_kv_grad,), (cross_q_grad, q_grad, self_out_grad, cross_out_grad) = text_grads, token_grads
 
     factor = jnp.repeat(jnp.sqrt(CLIP_TAU / jnp.maximum(head_peaks, CLIP_TAU)), HEAD_DIM)
 

time: 2020 us -> 1860 us (0.921)
  waiting for transfers between devices: 736 us -> 545 us
  other arithmetic: 83.4 us -> 110 us
    ppermute x89, waiting for transfers between devices: 515 us -> 439 us  [shift(): lax.ppermute(values, axis, [(cycle[i], cycle[(i + step) % size]) for i in...]
    ppermute x7 -> x3, waiting for transfers between devices: 72.5 us -> 0.01 us  [butterfly(): lax.ppermute(values, axis, [(i, i ^ bit) for i in range(size)])]
    ppermute x8 -> x12, waiting for transfers between devices: 149 us -> 101 us  [shift(): return lax.ppermute(values, axis, step)]
    pallas_call x8 -> x0, Pallas kernels: 20.6 us -> none  [pack(): pl.pallas_call(pack_kernel, grid_spec=pltpu.PrefetchScalarGridSpec(num_sc...]
  transfers between devices with their start and end apart: 130 -> 130, of which waited for: 49 -> 47; matrix products, arithmetic and copies ran while one was open for 33% -> 39% of each run, Pallas kernels for 18% -> 20%
where the time goes in v4:
time: 1860 us; the launch traced here: 1850 us
  waiting for transfers between devices  545 us (29%)
  matrix products  506 us (27%)
  Pallas kernels  392 us (21%)
  starting transfers between devices  140 us (8%)
  local copies, waits for them, and re-layouts  137 us (7%)
  other arithmetic  110 us (6%)
    dot_general x44, matrix products, dot(): lax.dot_general(left, right, (((left_dim,), (right_dim,)), ((), ())), pre...  491 us
    ppermute x89, waiting for transfers between devices, shift(): lax.ppermute(values, axis, [(cycle[i], cycle[(i + step) % size]) for i in...  439 us
    ppermute x12, waiting for transfers between devices, shift(): return lax.ppermute(values, axis, step)  101 us
    ppermute x89, starting transfers between devices, shift(): lax.ppermute(values, axis, [(cycle[i], cycle[(i + step) % size]) for i in...  99 us
    pallas_call x5, Pallas kernels, assemble(): pl.pallas_call(functools.partial(assemble_kernel, moves, rows, len(arrays...  70.3 us
    pallas_call x16, Pallas kernels, combine(): pl.pallas_call(functools.partial(combine_kernel, near_count, len(blocks)...  68.7 us
    pallas_call x2, Pallas kernels, conv(): call(functools.partial(conv_kernel, self.cols), (self.micro, self.units),...  53.6 us
    pallas_call x1, Pallas kernels, cross_back(): call(cross_back_kernel, (self.micro, self.groups), [smem, self.tile(), se...  52.5 us
  transfers between devices with their start and end apart: 130, of which 47 were waited for; matrix products, arithmetic and copies ran while one was open for 39% of the time, Pallas kernels for 20%

profile of v4, /device:TPU:0, one launch (start us, length us, event | category | flops | bytes accessed | tf_op | source)
XLA Modules:
  0.0 1847.6 jit_solution(14483857096684914614)
XLA Ops:
  98.8 18.4 collective-permute-done.8.refs_6_
  379.7 34.8 %collective-permute-done.42 = bf16[144,1408]{1,0:T(8,128)(2,1)S(1)} collective-permute-done((bf16[144,1408]{1,0:T(8,128)(2,1)S(1)}, bf16[144,1408]{1,0:T(8,128)(2,1)S(1)}, u32[]{:S(2)}, u32[]{:S(2)}) %collective-permute-start.42) | collective-permute-done | bytes 405536 | tf_op jit(solution)/shard_map/ppermute | solution.py:63
  469.8 34.4 %shard_map.276 = (bf16[1024,1152]{1,0:T(8,128)(2,1)S(1)}, f32[2,9,8,128]{3,2,1,0:T(8,128)S(1)}) custom-call(s32[2]{0:T(128)S(1)} %broadcast_select_fusion.length_ref, bf16[1024,1152]{1,0:T(8,128)(2,1)S(1)} %convolution_convert_fusion.15.query_ref, bf16[608,2304]{1,0:T(8,128)(2,1)} %convolution_convert_fusion.10.key_ref.value_ref, ...), custom_call_target="tpu_custom_call" | custom-call | flops 23592960000 | bytes 7077888 | tf_op jit(solution)/shard_map/pallas_call | solution.py:651
  519.6 22.5 %collective-permute-done.54 = f32[35]{0:T(128)S(1)} collective-permute-done((f32[35]{0:T(128)S(1)}, f32[35]{0:T(128)S(1)}, u32[]{:S(2)}, u32[]{:S(2)}) %collective-permute-start.54) | collective-permute-done | bytes 172 | tf_op jit(solution)/shard_map/ppermute | solution.py:60
  650.5 19.2 %convolution_add_fusion.1.z0.z1 = f32[1024,2816]{1,0:T(8,128)} fusion(bf16[1024,2304]{1,0:T(8,128)(2,1)S(1)} %pad_maximum_fusion.2, bf16[2304,2816]{1,0:T(8,128)(2,1)} %get-tuple-element.252, f32[2816]{0:T(1024)S(1)} %maximum_reduce_fusion), kind=kOutput, calls=%fused_computation.29 | convolution fusion | flops 13290438656 | bytes 29240320 | tf_op jit(solution)/shard_map/dot_general | solution.py:27
  695.8 26.7 %shard_map.278 = (bf16[1024,1408]{1,0:T(8,128)(2,1)S(1)}, bf16[1024,1408]{1,0:T(8,128)(2,1)}, bf16[1024,1408]{1,0:T(8,128)(2,1)}, f32[2,24,1408]{2,1,0:T(8,128)S(1)}) custom-call(f32[1024,2816]{1,0:T(8,128)} %convolution_add_fusion.1.z0.z1, f32[1024,2816]{1,0:T(8,128)} %convolution_add_fusion.1.z0.z1, ...), custom_call_target="tpu_custom_call" | custom-call | flops 57671680000 | bytes 23068672 | tf_op jit(solution)/shard_map/pallas_call | solution.py:690
  745.5 21.4 %shard_map.279 = (bf16[1024,1408]{1,0:T(8,128)(2,1)S(1)}, bf16[1024,1408]{1,0:T(8,128)(2,1)}, f32[2,8,1408]{2,1,0:T(8,128)S(1)}) custom-call(f32[1024,2816]{1,0:T(8,128)} %convolution_add_fusion.1.z0.z1, f32[1024,2816]{1,0:T(8,128)} %convolution_add_fusion.1.z0.z1, bf16[1024,1408]{1,0:T(8,128)(2,1)} %get-tuple-element.262.grad0, ...), custom_call_target="tpu_custom_call" | custom-call | flops 57671680000 | bytes 28835840 | tf_op jit(solution)/shard_map/pallas_call | solution.py:702
  785.8 19.9 %convolution_convert_fusion.3 = bf16[2304,2816]{1,0:T(8,128)(2,1)} fusion(bf16[1024,2816]{1,0:T(8,128)(2,1)} %constant_dynamic-update-slice_fusion, bf16[512,2304]{1,0:T(8,128)(2,1)S(1)} %copy-done.107, bf16[512,2304]{1,0:T(8,128)(2,1)} %add_convert_fusion.1), kind=kOutput, calls=%fused_computation.12 | convolution fusion | flops 13303480320 | bytes 23461888 | tf_op jit(solution)/shard_map/dot_general | solution.py:27
  822.4 19.2 %convolution_add_fusion.z0.z1 = f32[1024,2816]{1,0:T(8,128)S(1)} fusion(bf16[1024,2304]{1,0:T(8,128)(2,1)} %copy-done.72, bf16[2304,2816]{1,0:T(8,128)(2,1)} %get-tuple-element.277, f32[2816]{0:T(1024)S(1)} %fusion.94), kind=kOutput, calls=%fused_computation.28 | convolution fusion | flops 13290438656 | bytes 29240320 | tf_op jit(solution)/shard_map/dot_general | solution.py:27
  860.9 26.9 %shard_map.281 = (bf16[1024,1408]{1,0:T(8,128)(2,1)S(1)}, bf16[1024,1408]{1,0:T(8,128)(2,1)}, bf16[1024,1408]{1,0:T(8,128)(2,1)}, f32[2,24,1408]{2,1,0:T(8,128)S(1)}) custom-call(f32[1024,2816]{1,0:T(8,128)} %copy-done.151, f32[1024,2816]{1,0:T(8,128)} %copy-done.151, bf16[2,32,2816]{2,1,0:T(8,128)(2,1)S(1)} %collective-permute-done.80.top0.top1, ...), custom_call_target="tpu_custom_call" | custom-call | flops 57671680000 | bytes 23068672 | tf_op jit(solution)/shard_map/pallas_call | solution.py:690
  908.5 21.7 %shard_map.282 = (bf16[1024,1408]{1,0:T(8,128)(2,1)S(1)}, bf16[1024,1408]{1,0:T(8,128)(2,1)}, f32[2,8,1408]{2,1,0:T(8,128)S(1)}) custom-call(f32[1024,2816]{1,0:T(8,128)} %copy-done.151, f32[1024,2816]{1,0:T(8,128)} %copy-done.151, bf16[1024,1408]{1,0:T(8,128)(2,1)} %get-tuple-element.283.grad0, bf16[1024,1408]{1,0:T(8,128)(2,1)} %get-tuple-element.284.grad1, ...), custom_call_target="tpu_custom_call" | custom-call | flops 57671680000 | bytes 28835840 | tf_op jit(solution)/shard_map/pallas_call | solution.py:702
  935.0 18.8 %convolution_convert_fusion.2.refs_0_ = bf16[2304,2816]{1,0:T(8,128)(2,1)} fusion(bf16[1024,2304]{1,0:T(8,128)(2,1)S(1)} %bitcast.177, bf16[1024,2816]{1,0:T(8,128)(2,1)} %constant_dynamic-update-slice_fusion.2), kind=kOutput, calls=%fused_computation.11 | convolution fusion | flops 13294043136 | bytes 23461888 | tf_op jit(solution)/shard_map/dot_general | solution.py:27
  1001.1 17.7 multiply_reduce_fusion.1
  1049.9 45.3 %collective-permute-done.85.refs_3_ = bf16[288,2816]{1,0:T(8,128)(2,1)S(1)} collective-permute-done((bf16[288,2816]{1,0:T(8,128)(2,1)}, bf16[288,2816]{1,0:T(8,128)(2,1)S(1)}, u32[]{:S(2)}, u32[]{:S(2)}) %collective-permute-start.85) | collective-permute-done | bytes 1622048 | tf_op jit(solution)/shard_map/ppermute | solution.py:63
  1118.0 52.5 %shard_map.290 = (bf16[1024,1152]{1,0:T(8,128)(2,1)S(1)}, bf16[608,1152]{1,0:T(8,128)(2,1)S(1)}, bf16[608,1152]{1,0:T(8,128)(2,1)S(1)}) custom-call(s32[2]{0:T(128)S(1)} %copy-done.43, bf16[1024,1152]{1,0:T(8,128)(2,1)} %copy-done.55, bf16[608,2304]{1,0:T(8,128)(2,1)} %convolution_convert_fusion.10.key_ref.value_ref, ...), custom_call_target="tpu_custom_call" | custom-call | flops 58982400000 | bytes 7077888 | tf_op jit(solution)/shard_map/pallas_call | solution.py:662
  1242.2 25.4 %collective-permute-done.91.refs_3_ = bf16[288,2816]{1,0:T(8,128)(2,1)S(1)} collective-permute-done((bf16[288,2816]{1,0:T(8,128)(2,1)S(1)}, bf16[288,2816]{1,0:T(8,128)(2,1)S(1)}, u32[]{:S(2)}, u32[]{:S(2)}) %collective-permute-start.91) | collective-permute-done | bytes 1622048 | tf_op jit(solution)/shard_map/ppermute | solution.py:63
  1267.6 19.8 %collective-permute-done.92.refs_4_ = bf16[144,5632]{1,0:T(8,128)(2,1)S(1)} collective-permute-done((bf16[144,5632]{1,0:T(8,128)(2,1)S(1)}, bf16[144,5632]{1,0:T(8,128)(2,1)S(1)}, u32[]{:S(2)}, u32[]{:S(2)}) %collective-permute-start.92) | collective-permute-done | bytes 1622048 | tf_op jit(solution)/shard_map/ppermute | solution.py:63
  1362.9 25.8 %shard_map.297 = bf16[1024,2304]{1,0:T(8,128)(2,1)S(1)} custom-call(f32[1024,2304]{1,0:T(8,128)} %fusion.104.key_ref.value_ref, f32[1024,2304]{1,0:T(8,128)} %fusion.104.key_ref.value_ref, f32[2,9,40,128]{3,2,1,0:T(8,128)S(1)} %add.1420.state_ref), custom_call_target="tpu_custom_call" | custom-call | flops 1769472000 | bytes 23592960 | tf_op jit(solution)/shard_map/pallas_call | solution.py:637
  1388.6 18.5 convolution_convert_fusion.1
  1479.2 28.2 %collective-permute-done.102.refs_6_ = bf16[288,2304]{1,0:T(8,128)(2,1)S(1)} collective-permute-done((bf16[288,2304]{1,0:T(8,128)(2,1)}, bf16[288,2304]{1,0:T(8,128)(2,1)S(1)}, u32[]{:S(2)}, u32[]{:S(2)}) %collective-permute-start.102) | collective-permute-done | bytes 1327136 | tf_op jit(solution)/shard_map/ppermute | solution.py:63
  1507.4 34.6 %collective-permute-done.103.refs_7_ = bf16[144,6912]{1,0:T(8,128)(2,1)S(1)} collective-permute-done((bf16[144,6912]{1,0:T(8,128)(2,1)S(1)}, bf16[144,6912]{1,0:T(8,128)(2,1)S(1)}, u32[]{:S(2)}, u32[]{:S(2)}) %collective-permute-start.103) | collective-permute-done | bytes 1990688 | tf_op jit(solution)/shard_map/ppermute | solution.py:63
  1573.0 42.2 %collective-permute-done.106 = f32[22,2816]{1,0:T(8,128)S(1)} collective-permute-done((f32[22,2816]{1,0:T(8,128)S(1)}, f32[22,2816]{1,0:T(8,128)S(1)}, u32[]{:S(2)}, u32[]{:S(2)}) %collective-permute-start.106) | collective-permute-done | bytes 247840 | tf_op jit(solution)/shard_map/ppermute | solution.py:60
  1723.4 18.5 %collective-permute-done.117.refs_6_ = bf16[288,2304]{1,0:T(8,128)(2,1)S(1)} collective-permute-done((bf16[288,2304]{1,0:T(8,128)(2,1)}, bf16[288,2304]{1,0:T(8,128)(2,1)S(1)}, u32[]{:S(2)}, u32[]{:S(2)}) %collective-permute-start.117) | collective-permute-done | bytes 1327136 | tf_op jit(solution)/shard_map/ppermute | solution.py:63
  1782.4 19.2 %collective-permute-done.121 = f32[6,2240]{1,0:T(8,128)S(1)} collective-permute-done((f32[6,2240]{1,0:T(8,128)S(1)}, f32[6,2240]{1,0:T(8,128)S(1)}, u32[]{:S(2)}, u32[]{:S(2)}) %collective-permute-start.121) | collective-permute-done | bytes 53792 | tf_op jit(solution)/shard_map/ppermute | solution.py:60
  (962 shorter events, 1199.1 us)
Async XLA Ops:
  7.2 1167.1 %reduce-scatter.5.cloned.1.call-start = ((), (), s32[]{:S(2)}) async-start(), calls=%async_computation.4 | async-start | bytes 6893568 | tf_op jit(solution)/shard_map/reduce_scatter | solution.py:350
  96.0 110.0 %collective-permute-start = (bf16[512,2304]{1,0:T(8,128)(2,1)}, bf16[512,2304]{1,0:T(8,128)(2,1)}, u32[]{:S(2)}, u32[]{:S(2)}) collective-permute-start(bf16[512,2304]{1,0:T(8,128)(2,1)} %add_convert_fusion.2), channel_id=1, source_target_pairs={{0,1},{1,0},{2,3},{3,2},{4,5},{5,4},{6,7},{7,6},{8,9},{9,8},{10,11... | collective-permute-start | bytes 7077896 | tf_op jit(solution)/shard_map/ppermute | solution.py:366
  542.1 85.8 %collective-permute-start.71 = (bf16[512,2304]{1,0:T(8,128)(2,1)}, bf16[512,2304]{1,0:T(8,128)(2,1)}, u32[]{:S(2)}, u32[]{:S(2)}) collective-permute-start(bf16[512,2304]{1,0:T(8,128)(2,1)} %get-tuple-element.468), channel_id=1, source_target_pairs={{0,1},{1,0},{2,3},{3,2},{4,5},{5,4},{6,7},{7,6},{8,9},{9,8},{10,11... | collective-permute-start | bytes 7077896 | tf_op jit(solution)/shard_map/ppermute | solution.py:366
  821.3 502.8 %reduce-scatter.7.cloned.1.call-start = ((), (), s32[]{:S(2)}) async-start(), calls=%async_computation.5 | async-start | bytes 13787136 | tf_op jit(solution)/shard_map/reduce_scatter | solution.py:350
  848.1 922.1 %reduce-scatter.11.cloned.1.call-start = ((), (), s32[]{:S(2)}) async-start(), calls=%async_computation.7 | async-start | bytes 11280384 | tf_op jit(solution)/shard_map/reduce_scatter | solution.py:350
  1028.2 79.5 %collective-permute-start.94 = (bf16[512,2304]{1,0:T(8,128)(2,1)}, bf16[512,2304]{1,0:T(8,128)(2,1)}, u32[]{:S(2)}, u32[]{:S(2)}) collective-permute-start(bf16[512,2304]{1,0:T(8,128)(2,1)} %convert_element_type.222), channel_id=1, source_target_pairs={{0,1},{1,0},{2,3},{3,2},{4,5},{5,4},{6,7},{7,6},{8,9},{9,8},{10,11... | collective-permute-start | bytes 7077896 | tf_op jit(solution)/shard_map/ppermute | solution.py:366
  1104.8 71.4 %collective-permute-start.88 = (bf16[288,2816]{1,0:T(8,128)(2,1)}, bf16[288,2816]{1,0:T(8,128)(2,1)S(1)}, u32[]{:S(2)}, u32[]{:S(2)}) collective-permute-start(bf16[288,2816]{1,0:T(8,128)(2,1)} %pad_maximum_fusion.25), channel_id=1, source_target_pairs={{0,2},{2,0},{1,3},{3,1},{4,6},{6,4},{5,7},{7,5},{8,10},{10,8},{9,1... | collective-permute-start | bytes 4866056 | tf_op jit(solution)/shard_map/ppermute | solution.py:63
  1105.5 70.7 %collective-permute-start.89 = (bf16[144,5632]{1,0:T(8,128)(2,1)}, bf16[144,5632]{1,0:T(8,128)(2,1)S(1)}, u32[]{:S(2)}, u32[]{:S(2)}) collective-permute-start(bf16[144,5632]{1,0:T(8,128)(2,1)} %shard_map.285), channel_id=1, source_target_pairs={{0,4},{8,0},{16,8},{24,16},{28,24},{20,28},{12,20},{4,12},{1,5},{9... | collective-permute-start | bytes 4866056 | tf_op jit(solution)/shard_map/ppermute | solution.py:63
  1107.3 69.0 %collective-permute-start.90 = (bf16[144,5632]{1,0:T(8,128)(2,1)}, bf16[144,5632]{1,0:T(8,128)(2,1)}, u32[]{:S(2)}, u32[]{:S(2)}) collective-permute-start(bf16[144,5632]{1,0:T(8,128)(2,1)} %shard_map.286), channel_id=1, source_target_pairs={{0,8},{8,16},{16,24},{24,28},{28,20},{20,12},{12,4},{4,0},{1,9},{9... | collective-permute-start | bytes 4866056 | tf_op jit(solution)/shard_map/ppermute | solution.py:63
  1195.0 640.8 %reduce-scatter.9.cloned.1.call-start = ((), (), s32[]{:S(2)}) async-start(), calls=%async_computation.6 | async-start | bytes 11280384 | tf_op jit(solution)/shard_map/reduce_scatter | solution.py:350
  1221.4 66.0 %collective-permute-start.92 = (bf16[144,5632]{1,0:T(8,128)(2,1)S(1)}, bf16[144,5632]{1,0:T(8,128)(2,1)S(1)}, u32[]{:S(2)}, u32[]{:S(2)}) collective-permute-start(bf16[144,5632]{1,0:T(8,128)(2,1)S(1)} %shard_map.287), channel_id=1, source_target_pairs={{0,4},{8,0},{16,8},{24,16},{28,24},{20,28},{12,20},{4,12},{1,5},{9... | collective-permute-start | bytes 4866056 | tf_op jit(solution)/shard_map/ppermute | solution.py:63
  1232.0 71.9 %collective-permute-start.96 = (bf16[512,2304]{1,0:T(8,128)(2,1)S(1)}, bf16[512,2304]{1,0:T(8,128)(2,1)}, u32[]{:S(2)}, u32[]{:S(2)}) collective-permute-start(bf16[512,2304]{1,0:T(8,128)(2,1)S(1)} %get-tuple-element.471), channel_id=1, source_target_pairs={{0,1},{1,0},{2,3},{3,2},{4,5},{5,4},{6,7},{7,6},{8,9},{9,8},{10,11... | collective-permute-start | bytes 7077896 | tf_op jit(solution)/shard_map/ppermute | solution.py:366
  1242.2 113.7 %collective-permute-start.97 = (bf16[144,5632]{1,0:T(8,128)(2,1)}, bf16[144,5632]{1,0:T(8,128)(2,1)S(1)}, u32[]{:S(2)}, u32[]{:S(2)}) collective-permute-start(bf16[144,5632]{1,0:T(8,128)(2,1)} %shard_map.288), channel_id=1, source_target_pairs={{0,8},{8,16},{16,24},{24,28},{28,20},{20,12},{12,4},{4,0},{1,9},{9... | collective-permute-start | bytes 4866056 | tf_op jit(solution)/shard_map/ppermute | solution.py:63
  1357.1 71.0 %collective-permute-start.98 = (f32[22,2816]{1,0:T(8,128)}, f32[22,2816]{1,0:T(8,128)}, u32[]{:S(2)}, u32[]{:S(2)}) collective-permute-start(f32[22,2816]{1,0:T(8,128)} %maximum_maximum_fusion.6), channel_id=1, source_target_pairs={{0,2},{2,0},{1,3},{3,1},{4,6},{6,4},{5,7},{7,5},{8,10},{10,8},{9,1... | collective-permute-start | bytes 743432 | tf_op jit(solution)/shard_map/ppermute | solution.py:60
  1358.4 71.6 %collective-permute-start.100 = (bf16[288,2304]{1,0:T(8,128)(2,1)}, bf16[288,2304]{1,0:T(8,128)(2,1)S(1)}, u32[]{:S(2)}, u32[]{:S(2)}) collective-permute-start(bf16[288,2304]{1,0:T(8,128)(2,1)} %maximum_maximum_fusion), channel_id=1, source_target_pairs={{0,2},{2,0},{1,3},{3,1},{4,6},{6,4},{5,7},{7,5},{8,10},{10,8},{9,1... | collective-permute-start | bytes 3981320 | tf_op jit(solution)/shard_map/ppermute | solution.py:63
  1359.2 78.8 %collective-permute-start.99 = (bf16[144,5632]{1,0:T(8,128)(2,1)}, bf16[144,5632]{1,0:T(8,128)(2,1)}, u32[]{:S(2)}, u32[]{:S(2)}) collective-permute-start(bf16[144,5632]{1,0:T(8,128)(2,1)} %shard_map.289), channel_id=1, source_target_pairs={{0,4},{8,0},{16,8},{24,16},{28,24},{20,28},{12,20},{4,12},{1,5},{9... | collective-permute-start | bytes 4866056 | tf_op jit(solution)/shard_map/ppermute | solution.py:63
  1460.3 88.7 %collective-permute-start.105 = (bf16[144,1408]{1,0:T(8,128)(2,1)S(1)}, bf16[144,1408]{1,0:T(8,128)(2,1)S(1)}, u32[]{:S(2)}, u32[]{:S(2)}) collective-permute-start(bf16[144,1408]{1,0:T(8,128)(2,1)S(1)} %slice.794), channel_id=1, source_target_pairs={{0,2},{2,0},{1,3},{3,1},{4,6},{6,4},{5,7},{7,5},{8,10},{10,8},{9,1... | collective-permute-start | bytes 1216520 | tf_op jit(solution)/shard_map/ppermute | solution.py:63
  1462.3 79.6 %collective-permute-start.103 = (bf16[144,6912]{1,0:T(8,128)(2,1)S(1)}, bf16[144,6912]{1,0:T(8,128)(2,1)S(1)}, u32[]{:S(2)}, u32[]{:S(2)}) collective-permute-start(bf16[144,6912]{1,0:T(8,128)(2,1)S(1)} %copy-done.16), channel_id=1, source_target_pairs={{0,4},{8,0},{16,8},{24,16},{28,24},{20,28},{12,20},{4,12},{1,5},{9... | collective-permute-start | bytes 5971976 | tf_op jit(solution)/shard_map/ppermute | solution.py:63
  1462.5 82.9 %collective-permute-start.104 = (bf16[144,6912]{1,0:T(8,128)(2,1)S(1)}, bf16[144,6912]{1,0:T(8,128)(2,1)S(1)}, u32[]{:S(2)}, u32[]{:S(2)}) collective-permute-start(bf16[144,6912]{1,0:T(8,128)(2,1)S(1)} %shard_map.294), channel_id=1, source_target_pairs={{0,8},{8,16},{16,24},{24,28},{28,20},{20,12},{12,4},{4,0},{1,9},{9... | collective-permute-start | bytes 5971976 | tf_op jit(solution)/shard_map/ppermute | solution.py:63
  1549.0 66.2 %collective-permute-start.109 = (bf16[288,2304]{1,0:T(8,128)(2,1)}, bf16[288,2304]{1,0:T(8,128)(2,1)S(1)}, u32[]{:S(2)}, u32[]{:S(2)}) collective-permute-start(bf16[288,2304]{1,0:T(8,128)(2,1)} %maximum_maximum_fusion.2), channel_id=1, source_target_pairs={{0,2},{2,0},{1,3},{3,1},{4,6},{6,4},{5,7},{7,5},{8,10},{10,8},{9,1... | collective-permute-start | bytes 3981320 | tf_op jit(solution)/shard_map/ppermute | solution.py:63
  1549.5 65.7 %collective-permute-start.107 = (bf16[144,6912]{1,0:T(8,128)(2,1)S(1)}, bf16[144,6912]{1,0:T(8,128)(2,1)S(1)}, u32[]{:S(2)}, u32[]{:S(2)}) collective-permute-start(bf16[144,6912]{1,0:T(8,128)(2,1)S(1)} %shard_map.295), channel_id=1, source_target_pairs={{0,4},{8,0},{16,8},{24,16},{28,24},{20,28},{12,20},{4,12},{1,5},{9... | collective-permute-start | bytes 5971976 | tf_op jit(solution)/shard_map/ppermute | solution.py:63
  1551.7 63.5 %collective-permute-start.108 = (bf16[144,6912]{1,0:T(8,128)(2,1)S(1)}, bf16[144,6912]{1,0:T(8,128)(2,1)S(1)}, u32[]{:S(2)}, u32[]{:S(2)}) collective-permute-start(bf16[144,6912]{1,0:T(8,128)(2,1)S(1)} %shard_map.296), channel_id=1, source_target_pairs={{0,8},{8,16},{16,24},{24,28},{28,20},{20,12},{12,4},{4,0},{1,9},{9... | collective-permute-start | bytes 5971976 | tf_op jit(solution)/shard_map/ppermute | solution.py:63
  1691.3 63.4 %collective-permute-start.120 = (bf16[144,6912]{1,0:T(8,128)(2,1)}, bf16[144,6912]{1,0:T(8,128)(2,1)S(1)}, u32[]{:S(2)}, u32[]{:S(2)}) collective-permute-start(bf16[144,6912]{1,0:T(8,128)(2,1)} %shard_map.299), channel_id=1, source_target_pairs={{0,8},{8,16},{16,24},{24,28},{28,20},{20,12},{12,4},{4,0},{1,9},{9... | collective-permute-start | bytes 5971976 | tf_op jit(solution)/shard_map/ppermute | solution.py:63
  1723.4 78.2 %collective-permute-start.111 = (bf16[512,2240]{0,1:T(8,128)(2,1)}, bf16[512,2240]{0,1:T(8,128)(2,1)}, u32[]{:S(2)}, u32[]{:S(2)}) collective-permute-start(bf16[512,2240]{0,1:T(8,128)(2,1)} %fusion.21), channel_id=1, source_target_pairs={{0,1},{1,0},{2,3},{3,2},{4,5},{5,4},{6,7},{7,6},{8,9},{9,8},{10,11... | collective-permute-start | bytes 6881288 | tf_op jit(solution)/shard_map/ppermute | solution.py:366
  (304 other events, 7766.8 us)
Sparse Core Ops, SparseCore 0:
  821.4 148.7 reduce-scatter.4
  975.9 242.6 reduce-scatter.6
  1225.5 239.7 reduce-scatter.10
  1470.9 233.4 reduce-scatter.8
